TPU v7x, 256 devices: a whole 4x4x8 slice. The times are simulated.
256 devices in a mesh: row: 8 (over z_hi, y), col: 32 (over z_lo, x, core).
Axes of the slice: x: 4, y: 4, z: 8 (z_hi: 2, z_lo: 4; z = z_hi * 4 + z_lo), core: 2. Of those that a mesh axis runs over, the one named last changes fastest.
Arguments:
- start_block: float32 [32, 16384], P(None, 'col'), may hold values from -6 to 6
- energies: float32 [16384], P('col'), may hold values from 1 to 10
- hamiltonian: float32 [32, 32, 512, 512], P('row', 'col'), may hold values from -0.09375 to 0.09375
Outputs:
- recurrence: float32 [2, 2, 32, 32], replicated
- next_block: float32 [32, 16384], P(None, 'col')
All inputs are finite; a program needn't handle non-finite values.
Results may differ from a plain program's by a relative error of at most 0.0003.
Values sent between devices are 32-bit elements; how exact they have to be, the bound alone decides.
No kernel may reach another device: no remote copies, remote signals or barrier semaphores. Data moves between devices by JAX's collectives and lax.ppermute only.
A program may use at most 64 MiB of HBM per device.

v0:
```python
import jax
import jax.numpy as jnp
from jax import lax
from jax.sharding import PartitionSpec as P

ITERS = 2


FULL_PRECISION = lax.Precision.HIGHEST


def sent_to_all(shard, axis):
    devices = lax.axis_size(axis)
    return lax.all_to_all(
        jnp.broadcast_to(shard[None], (devices, *shard.shape)), axis, 0, 0, tiled=True
    )


def over_copies(shard, axis):
    return sent_to_all(shard, axis).sum(axis=0)


def split_up(shard, dim, devices):
    lengths = shard.shape
    parts = shard.reshape(*lengths[:dim], devices, lengths[dim] // devices, *lengths[dim + 1 :])
    return jnp.moveaxis(parts, dim, 0)


def sent_and_summed(shard, axis, dim):
    devices = lax.axis_size(axis)
    parts = lax.all_to_all(split_up(shard, dim, devices), axis, 0, 0, tiled=True)
    return jnp.sum(parts, axis=0)


def mean_inner(left, right):
    length = lax.axis_size("col") * left.shape[1]
    return over_copies(jnp.dot(left, right.T, precision=FULL_PRECISION), "col") / length


def normalize(block):
    factor = jnp.linalg.cholesky(mean_inner(block, block))
    return (lax.linalg.triangular_solve(factor, block, left_side=True, lower=True), factor)


def on_device(start_block, energies, hamiltonian):
    row_index = lax.axis_index("row")
    col_index = lax.axis_index("col")
    row_count = lax.axis_size("row")
    col_count = lax.axis_size("col")
    slot_count = hamiltonian.shape[0]
    width = hamiltonian.shape[2]
    vec_count = start_block.shape[0]
    blocks = hamiltonian[:, 0]
    block_rows = row_index + row_count * jnp.arange(slot_count, dtype=jnp.int32)
    weight = jnp.where(
        block_rows < col_index,
        jnp.float32(1.0),
        jnp.where(block_rows == col_index, jnp.float32(0.5), jnp.float32(0.0)),
    )
    selector = (block_rows[:, None] == jnp.arange(col_count, dtype=jnp.int32)[None, :]).astype(
        jnp.float32
    )
    current, factor = normalize(start_block)
    previous = jnp.zeros_like(current)
    last_factor = jnp.zeros((vec_count, vec_count), jnp.float32)
    history = []
    for iteration in range(ITERS):
        whole = lax.all_gather(current, "col", axis=1, tiled=True).reshape(
            vec_count, col_count, width
        )
        chosen = jnp.take(whole, block_rows, axis=1) * weight[None, :, None]
        downward = jnp.einsum("psk,skl->pl", chosen, blocks, precision=FULL_PRECISION)
        across = (
            jnp.einsum("pl,skl->spk", current, blocks, precision=FULL_PRECISION)
            * weight[:, None, None]
        )
        spread = jnp.einsum("sj,spk->pjk", selector, across, precision=FULL_PRECISION).reshape(
            vec_count, col_count * width
        )
        mine = sent_and_summed(spread, "col", 1)
        column_total = over_copies(downward + mine, "row")
        residual_block = (
            column_total
            + energies[None, :] * current
            - jnp.dot(last_factor.T, previous, precision=FULL_PRECISION)
        )
        diagonal_block = mean_inner(residual_block, current)
        residual_block = residual_block - jnp.dot(diagonal_block, current, precision=FULL_PRECISION)
        following, new_factor = normalize(residual_block)
        history.append(jnp.stack([diagonal_block, new_factor]))
        previous, current, last_factor = (current, following, new_factor)
    return (jnp.stack(history), current)


def solution(mesh):
    placed = (P(None, "col"), P("col"), P("row", "col", None, None))
    return jax.shard_map(
        on_device, mesh=mesh, in_specs=placed, out_specs=(P(), P(None, "col")), check_vma=False
    )
```

profile of v0, /device:TPU:2, one launch (start us, length us, event | category | flops | bytes accessed | tf_op | source)
XLA Modules:
  0.0 340.1 jit_solution(10457580670392844726)
XLA Ops:
  9.2 9.0 %all-to-all-start = ((f32[32,1,1024]{2,1,0:T(1,128)}), f32[32,1,1024]{2,1,0:T(1,128)S(1)}, u32[]{:S(2)}, u32[]{:S(2)}) async-start(f32[32,1,1024]{2,1,0:T(1,128)} %reshape.114), calls=%async_computation | async-start | bytes 262144 | tf_op jit(solution)/shard_map/all_to_all | solution.py:14
  18.3 7.4 %all-to-all-done = f32[32,1,1024]{2,1,0:T(1,128)S(1)} async-done(((f32[32,1,1024]{2,1,0:T(1,128)}), f32[32,1,1024]{2,1,0:T(1,128)S(1)}, u32[]{:S(2)}, u32[]{:S(2)}) %all-to-all-start) | async-done | bytes 131104 | tf_op jit(solution)/shard_map/all_to_all | solution.py:14
  27.6 2.9 cholesky.59
  35.2 6.1 %fusion.11 = f32[4,32,512]{2,1,0:T(8,128)S(1)} fusion(f32[4,1,512,512]{3,2,1,0:T(8,128)} %param.10, f32[4]{0:T(128)S(1)} %compare_select_fusion.2, f32[32,512]{1,0:T(8,128)} %fusion.54), kind=kOutput, calls=%fused_computation.13 | convolution fusion | flops 402718720 | bytes 4522000 | tf_op jit(solution)/shard_map/pl,skl->spk/dot_general | solution.py:74
  42.4 2.6 copy.39
  45.0 5.1 %all-to-all-start.1 = ((f32[32,32,512]{2,1,0:T(8,128)}), f32[32,32,512]{2,1,0:T(8,128)S(1)}, u32[]{:S(2)}, u32[]{:S(2)}) async-start(f32[32,32,512]{2,1,0:T(8,128)} %copy.39), calls=%async_computation.1 | async-start | bytes 4194304 | tf_op jit(solution)/shard_map/all_to_all | solution.py:31
  50.2 57.2 %all-gather.3.cloned.1.call-done = f32[32,16384]{1,0:T(8,128)} async-done(((f32[32,512]{1,0:T(8,128)}), f32[32,16384]{1,0:T(8,128)}) %all-gather.3.cloned.1.call-update) | async-done | bytes 2097168 | tf_op jit(solution)/shard_map/all_gather | solution.py:68
  107.4 3.2 copy.56
  112.9 4.7 %fusion.29 = f32[32,512]{1,0:T(8,128)S(1)} fusion(f32[32,512]{1,0:T(8,128)S(1)} %reduce_sum.82, f32[4,1,512,512]{3,2,1,0:T(8,128)} %param.10, f32[4,32,512]{2,1,0:T(8,128)S(1)} %gather_fusion, f32[4]{0:T(128)S(1)} %compare_select_fusion.2, pred[4]{0:T(512)(128)(4,1)S(1)} %compare_and_fusion), kind=kOutput, calls=%fused_computation.23 | convolution fusion | flops 402800640 | bytes 4587540 | tf_op jit(solution)/shard_map/psk,skl->pl/dot_general | solution.py:72
  117.7 24.5 %all_to_all.45 = f32[8,32,512]{2,1,0:T(8,128)S(1)} all-to-all(f32[8,32,512]{2,1,0:T(8,128)S(1)} %broadcast_in_dim.42), channel_id=1, replica_groups=mesh['row'=8,'col'=32] {'row'}, dimensions={0} | all-to-all | bytes 1048576 | tf_op jit(solution)/shard_map/all_to_all | solution.py:14
  143.0 17.5 %all_to_all.46 = f32[32,1,1024]{2,1,0:T(1,128)S(1)} all-to-all(f32[32,1,1024]{2,1,0:T(1,128)S(1)} %reshape.116), channel_id=1, replica_groups=mesh['row'=8,'col'=32] {'col'}, dimensions={0} | all-to-all | bytes 262144 | tf_op jit(solution)/shard_map/all_to_all | solution.py:14
  162.3 12.1 %all_to_all.47 = f32[32,1,1024]{2,1,0:T(1,128)S(1)} all-to-all(f32[32,1,1024]{2,1,0:T(1,128)S(1)} %reshape.118), channel_id=1, replica_groups=mesh['row'=8,'col'=32] {'col'}, dimensions={0} | all-to-all | bytes 262144 | tf_op jit(solution)/shard_map/all_to_all | solution.py:14
  175.8 2.9 cholesky.70
  182.8 6.0 %fusion.17 = f32[4,32,512]{2,1,0:T(8,128)S(1)} fusion(f32[4,1,512,512]{3,2,1,0:T(8,128)} %param.10, f32[4]{0:T(128)S(1)} %compare_select_fusion.2, f32[32,512]{1,0:T(8,128)S(1)} %fusion.51), kind=kOutput, calls=%fused_computation.15 | convolution fusion | flops 402718720 | bytes 4522000 | tf_op jit(solution)/shard_map/pl,skl->spk/dot_general | solution.py:74
  190.0 2.6 copy.44
  192.5 5.1 %all-to-all-start.5 = ((f32[32,32,512]{2,1,0:T(8,128)}), f32[32,32,512]{2,1,0:T(8,128)S(1)}, u32[]{:S(2)}, u32[]{:S(2)}) async-start(f32[32,32,512]{2,1,0:T(8,128)} %copy.44), calls=%async_computation.5 | async-start | bytes 4194304 | tf_op jit(solution)/shard_map/all_to_all | solution.py:31
  197.7 59.2 %all-gather.5.cloned.1.call-done = f32[32,16384]{1,0:T(8,128)} async-done(((f32[32,512]{1,0:T(8,128)}), f32[32,16384]{1,0:T(8,128)}) %all-gather.5.cloned.1.call-update) | async-done | bytes 2097168 | tf_op jit(solution)/shard_map/all_gather | solution.py:68
  256.8 3.2 copy.55
  262.3 4.7 %fusion.26 = f32[32,512]{1,0:T(8,128)S(1)} fusion(f32[32,512]{1,0:T(8,128)S(1)} %reduce_sum.86, f32[4,1,512,512]{3,2,1,0:T(8,128)} %param.10, f32[4,32,512]{2,1,0:T(8,128)S(1)} %gather_fusion.1, f32[4]{0:T(128)S(1)} %compare_select_fusion.2, pred[4]{0:T(512)(128)(4,1)S(1)} %compare_and_fusion), kind=kOutput, calls=%fused_computation.22 | convolution fusion | flops 402800640 | bytes 4587540 | tf_op jit(solution)/shard_map/psk,skl->pl/dot_general | solution.py:72
  267.1 25.5 %all_to_all.48 = f32[8,32,512]{2,1,0:T(8,128)S(1)} all-to-all(f32[8,32,512]{2,1,0:T(8,128)S(1)} %broadcast_in_dim.46), channel_id=1, replica_groups=mesh['row'=8,'col'=32] {'row'}, dimensions={0} | all-to-all | bytes 1048576 | tf_op jit(solution)/shard_map/all_to_all | solution.py:14
  294.0 14.5 %all_to_all.49 = f32[32,1,1024]{2,1,0:T(1,128)S(1)} all-to-all(f32[32,1,1024]{2,1,0:T(1,128)S(1)} %reshape.120), channel_id=1, replica_groups=mesh['row'=8,'col'=32] {'col'}, dimensions={0} | all-to-all | bytes 262144 | tf_op jit(solution)/shard_map/all_to_all | solution.py:14
  311.1 5.0 %all-to-all-start.8 = ((f32[32,1,1024]{2,1,0:T(1,128)}), f32[32,1,1024]{2,1,0:T(1,128)S(1)}, u32[]{:S(2)}, u32[]{:S(2)}) async-start(f32[32,1,1024]{2,1,0:T(1,128)} %reshape.122), calls=%async_computation.8 | async-start | bytes 262144 | tf_op jit(solution)/shard_map/all_to_all | solution.py:14
  316.1 7.6 %all-to-all-done.8 = f32[32,1,1024]{2,1,0:T(1,128)S(1)} async-done(((f32[32,1,1024]{2,1,0:T(1,128)}), f32[32,1,1024]{2,1,0:T(1,128)S(1)}, u32[]{:S(2)}, u32[]{:S(2)}) %all-to-all-start.8) | async-done | bytes 131104 | tf_op jit(solution)/shard_map/all_to_all | solution.py:14
  325.0 2.9 cholesky.81
  (97 shorter events, 34.0 us)
Async XLA Ops:
  7.2 0.8 copy-start
  9.2 16.5 %all-to-all-start = ((f32[32,1,1024]{2,1,0:T(1,128)}), f32[32,1,1024]{2,1,0:T(1,128)S(1)}, u32[]{:S(2)}, u32[]{:S(2)}) async-start(f32[32,1,1024]{2,1,0:T(1,128)} %reshape.114), calls=%async_computation | async-start | bytes 262144 | tf_op jit(solution)/shard_map/all_to_all | solution.py:14
  18.2 89.2 %all-gather.3.cloned.1.call-start = ((), (), s32[]{:S(2)}) async-start(), calls=%async_computation.9 | async-start | bytes 2162688 | tf_op jit(solution)/shard_map/all_gather | solution.py:68
  45.0 67.8 %all-to-all-start.1 = ((f32[32,32,512]{2,1,0:T(8,128)}), f32[32,32,512]{2,1,0:T(8,128)S(1)}, u32[]{:S(2)}, u32[]{:S(2)}) async-start(f32[32,32,512]{2,1,0:T(8,128)} %copy.39), calls=%async_computation.1 | async-start | bytes 4194304 | tf_op jit(solution)/shard_map/all_to_all | solution.py:31
  50.1 206.7 %all-gather.5.cloned.1.call-start = ((), (), s32[]{:S(2)}) async-start(), calls=%async_computation.10 | async-start | bytes 2162688 | tf_op jit(solution)/shard_map/all_gather | solution.py:68
  117.6 24.7 %copy-start.1 = (f32[32,512]{1,0:T(8,128)S(1)}, f32[32,512]{1,0:T(8,128)}, u32[]{:S(2)}) copy-start(f32[32,512]{1,0:T(8,128)} %fusion.54) | copy-start | bytes 196612
  117.6 24.7 %copy-start.4 = (f32[512]{0:T(512)S(1)}, f32[512]{0:T(512)}, u32[]{:S(2)}) copy-start(f32[512]{0:T(512)} %param.9) | copy-start | bytes 6148
  182.7 6.1 %copy-start.2 = (f32[32,512]{1,0:T(8,128)}, f32[32,512]{1,0:T(8,128)S(1)}, u32[]{:S(2)}) copy-start(f32[32,512]{1,0:T(8,128)S(1)} %fusion.51) | copy-start | bytes 196612
  192.5 69.6 %all-to-all-start.5 = ((f32[32,32,512]{2,1,0:T(8,128)}), f32[32,32,512]{2,1,0:T(8,128)S(1)}, u32[]{:S(2)}, u32[]{:S(2)}) async-start(f32[32,32,512]{2,1,0:T(8,128)} %copy.44), calls=%async_computation.5 | async-start | bytes 4194304 | tf_op jit(solution)/shard_map/all_to_all | solution.py:31
  267.0 25.6 %copy-start.3 = (f32[32,512]{1,0:T(8,128)S(1)}, f32[32,512]{1,0:T(8,128)}, u32[]{:S(2)}) copy-start(f32[32,512]{1,0:T(8,128)} %copy-done.2) | copy-start | bytes 196612
  311.1 12.6 %all-to-all-start.8 = ((f32[32,1,1024]{2,1,0:T(1,128)}), f32[32,1,1024]{2,1,0:T(1,128)S(1)}, u32[]{:S(2)}, u32[]{:S(2)}) async-start(f32[32,1,1024]{2,1,0:T(1,128)} %reshape.122), calls=%async_computation.8 | async-start | bytes 262144 | tf_op jit(solution)/shard_map/all_to_all | solution.py:14
Sparse Core Ops, SparseCore 0:
  35.3 72.0 all-gather.2
  189.0 67.8 all-gather.4
where the time goes:
time: 343 us; the launch traced here: 340 us
  waiting for transfers between devices  131 us (38%)
  blocking collectives  94.2 us (27%)
  matrix products  28.2 us (8%)
  other arithmetic  26.1 us (8%)
  starting transfers between devices  24.3 us (7%)
  local copies, waits for them, and re-layouts  21.3 us (6%)
  between operations  14.6 us (4%)
    all_gather x2, waiting for transfers between devices, on_device(): lax.all_gather(current, 'col', axis=1, tiled=True)  116 us
    all_to_all x5, blocking collectives, sent_to_all(): lax.all_to_all(jnp.broadcast_to(shard[None], (devices, *shard.shape)), ax...  94.2 us
    all_to_all x2, waiting for transfers between devices, sent_to_all(): lax.all_to_all(jnp.broadcast_to(shard[None], (devices, *shard.shape)), ax...  15 us
    all_to_all x2, starting transfers between devices, sent_to_all(): lax.all_to_all(jnp.broadcast_to(shard[None], (devices, *shard.shape)), ax...  14 us
    dot_general x2, matrix products, on_device(): jnp.einsum('pl,skl->spk', current, blocks, precision=FULL_PRECISION)  12.1 us
    another operation x9, other arithmetic, normalize(): factor = jnp.linalg.cholesky(mean_inner(block, block))  10.8 us
    all_to_all x2, starting transfers between devices, sent_and_summed(): lax.all_to_all(split_up(shard, dim, devices), axis, 0, 0, tiled=True)  10.2 us
    dot_general x2, matrix products, on_device(): jnp.einsum('psk,skl->pl', chosen, blocks, precision=FULL_PRECISION)  9.36 us
  transfers between devices with their start and end apart: 6, of which 4 were waited for; matrix products, arithmetic and copies ran while one was open for 7% of the time, Pallas kernels for 0%

commit v1 on v0

v1 whole, which is shorter than its diff:
```python
import jax
import jax.numpy as jnp
from jax import lax
from jax.sharding import Mesh
from jax.sharding import PartitionSpec as P

SHIFT = 5.5
FULL = lax.Precision.HIGHEST
BLOCKS = lax.Precision.HIGH

SIZES = (2, 4, 4, 4, 2)
NAMES = ("zh", "y", "z", "x", "co")
ROW = ("zh", "y")
COL = ("z", "x", "co")

PLACE = (
    (5, 3, 2, 4, 7, 1, 0, 6),
    (2, 4, 5, 3, 0, 6, 7, 1),
    (0, 1, 7, 6, 2, 3, 5, 4),
    (7, 0, 4, 6, 2, 3, 1, 5),
    (3, 5, 4, 2, 1, 0, 6, 7),
    (4, 2, 3, 5, 1, 0, 6, 7),
    (6, 0, 1, 7, 4, 2, 3, 5),
    (1, 7, 6, 0, 3, 5, 4, 2),
)


def to_row_group():
    pairs = []
    for row in range(8):
        for z in range(4):
            for j in range(8):
                far = (row // 4) != (j // 4)
                z_to = (z + 2) % 4 if far else z
                pairs.append((row * 32 + z * 8 + j, j * 32 + z_to * 8 + PLACE[j][row]))
    return pairs


def from_row_group():
    return [(b, a) for a, b in to_row_group()]


def far_table():
    table = [[0.0] * 8 for _ in range(8)]
    for j in range(8):
        for row in range(8):
            table[j][PLACE[j][row]] = float((row // 4) != (j // 4))
    return table


def inverse_of_lower(factor):
    eye = jnp.eye(factor.shape[0], dtype=factor.dtype)
    return lax.linalg.triangular_solve(factor, eye, left_side=True, lower=True)


def mm(a, b):
    return jnp.dot(a, b, precision=FULL)


def recurrence(gram):
    n = gram.shape[0] // 3
    eye = jnp.eye(n, dtype=jnp.float32)
    g = [[gram[i * n : (i + 1) * n, k * n : (k + 1) * n] for k in range(3)] for i in range(3)]
    lower0 = jnp.linalg.cholesky(g[0][0])
    t0 = inverse_of_lower(lower0)
    a0 = mm(mm(t0, g[1][0]), t0.T)
    zero = jnp.zeros_like(t0)
    p1 = jnp.concatenate([-mm(a0, t0), t0, zero], axis=1)
    g1 = mm(mm(p1, gram), p1.T)
    lower1 = jnp.linalg.cholesky(g1)
    t1 = inverse_of_lower(lower1)
    q1 = mm(t1, p1)
    w1 = jnp.concatenate([-mm(lower1.T, t0), q1[:, :n], q1[:, n : 2 * n]], axis=1)
    a1 = mm(mm(w1, gram), q1.T)
    w1 = w1 - mm(a1, q1)
    g2 = mm(mm(w1, gram), w1.T)
    lower2 = jnp.linalg.cholesky(g2)
    q2 = mm(inverse_of_lower(lower2), w1)
    history = jnp.stack(
        [jnp.stack([a0 + SHIFT * eye, lower1]), jnp.stack([a1 + SHIFT * eye, lower2])]
    )
    return history, q2


def on_device(start_block, energies, hamiltonian):
    vecs, width = start_block.shape
    half = width // 2
    row = lax.axis_index(ROW)
    col = lax.axis_index(COL)
    z = lax.axis_index("z")
    core = lax.axis_index("co")
    place = lax.axis_index(("x", "co"))
    blocks = hamiltonian[:, 0]
    slots = blocks.shape[0]
    block_rows = row + 8 * jnp.arange(slots, dtype=jnp.int32)
    weight = jnp.where(block_rows < col, 1.0, jnp.where(block_rows == col, 0.5, 0.0)).astype(
        jnp.float32
    )[:, None, None]
    lead = (row == 0).astype(jnp.float32) * (energies - SHIFT)
    table = jnp.array(far_table(), jnp.float32).reshape(-1)
    far = jnp.sum(table * (jnp.arange(64) == row * 8 + place).astype(jnp.float32)) > 0.5
    slot = jnp.where(far, (z + 2) % 4, z)
    in_slot = (jnp.arange(slots) == slot)[:, None, None]
    every = NAMES

    def down(four, own):
        product = jnp.einsum("spk,skl->pl", four * weight, blocks, precision=BLOCKS)
        return product + lead[None, :] * own

    def across(own):
        return jnp.einsum("pl,skl->spk", own, blocks, precision=BLOCKS) * weight

    def total(acrosses, downs):
        arrived = lax.ppermute(downs, every, to_row_group())
        part = acrosses + jnp.where(in_slot, arrived[None], 0.0)
        part = part.reshape(slots * vecs // 8, 8, width)
        low, high = part[..., :half], part[..., half:]
        mine = jnp.where(core == 0, low, high)
        other = jnp.where(core == 0, high, low)
        mine = mine + lax.ppermute(other, "co", [(0, 1), (1, 0)])
        piece = lax.all_to_all(mine, ("z", "x"), 0, 0, tiled=True).sum(axis=0)
        whole = lax.all_to_all(
            jnp.broadcast_to(piece[None], mine.shape), ("z", "x"), 0, 0, tiled=True
        )
        facing = lax.ppermute(whole, "co", [(0, 1), (1, 0)])
        low = jnp.where(core == 0, whole, facing)
        high = jnp.where(core == 0, facing, whole)
        return jnp.concatenate([low, high], axis=-1).reshape(slots, vecs, width)

    def to_column(four):
        mine = jnp.sum(jnp.where(in_slot, four, 0.0), axis=0)
        return lax.ppermute(mine, every, from_row_group())

    moved = lax.ppermute(start_block, every, to_row_group())
    x4 = lax.all_to_all(
        jnp.broadcast_to(moved[None], (slots, vecs, width)), "z", 0, 0, tiled=True
    )
    x4 = jnp.where(far, jnp.roll(x4, 2, axis=0), x4)
    x = start_block
    y4 = total(across(x), down(x4, x))
    y = to_column(y4)
    z4 = total(across(y), down(y4, y))
    zz = to_column(z4)

    basis4 = jnp.concatenate([x4, y4, z4], axis=1)
    gram = jnp.einsum("spk,sqk->pq", basis4, basis4, precision=FULL)
    gram = lax.all_to_all(
        jnp.broadcast_to(gram[None], (8, *gram.shape)), ROW, 0, 0, tiled=True
    ).sum(axis=0)
    gram = gram / (32 * width)
    history, q2 = recurrence(gram)
    following = mm(q2, jnp.concatenate([x, y, zz], axis=0))
    return history, following


def solution(mesh):
    fine = Mesh(mesh.devices.reshape(SIZES), NAMES)
    placed = (P(None, COL), P(COL), P(ROW, COL, None, None))
    return jax.shard_map(
        on_device, mesh=fine, in_specs=placed, out_specs=(P(), P(None, COL)), check_vma=False
    )
```

time: 343 us -> 171 us (0.50)
  waiting for transfers between devices: 131 us -> 42.3 us
  blocking collectives: 94.2 us -> 61.1 us
  local copies, waits for them, and re-layouts: 21.3 us -> 1.84 us
  between operations: 14.6 us -> 1.69 us
  matrix products: 28.2 us -> 16.5 us
    all_gather x2 -> x0, waiting for transfers between devices: 116 us -> none  [on_device(): lax.all_gather(current, 'col', axis=1, tiled=True)]
    all_to_all x5 -> x4, blocking collectives: 94.2 us -> 61.1 us  [the longest x2 37.2 us: total(): piece = lax.all_to_all(mine, ('z', 'x'), 0, 0, tiled=True).sum(axis=0)]
    ppermute x0 -> x9, waiting for transfers between devices: none -> 27 us  [the longest x2 11.1 us: total(): arrived = lax.ppermute(downs, every, to_row_group())]
    all_to_all x4 -> x2, starting transfers between devices: 24.3 us -> 11.5 us  [the longest x1 5.89 us: on_device(): lax.all_to_all(jnp.broadcast_to(moved[None], (slots, vecs, width)), 'z',...]
    ppermute x0 -> x9, starting transfers between devices: none -> 10.9 us  [the longest x2 4.99 us: to_column(): return lax.ppermute(mine, every, from_row_group())]
    dot_general x15 -> x19, matrix products: 26.1 us -> 15.8 us  [the longest x2 7.23 us: down(): product = jnp.einsum('spk,skl->pl', four * weight, blocks, precision=BLOCKS)]
    reshape x2 -> x0, local copies, waits for them, and re-layouts: 6.33 us -> none  [on_device(): lax.all_gather(current, 'col', axis=1, tiled=True)]
    dot_general x2, local copies, waits for them, and re-layouts: 5.14 us -> 0.14 us  [mm(): return jnp.dot(a, b, precision=FULL)]
  transfers between devices with their start and end apart: 6 -> 11, of which waited for: 4 -> 10; matrix products, arithmetic and copies ran while one was open for 7% -> 16% of each run, Pallas kernels for 0% -> 0%
where the time goes in v1:
time: 171 us; the launch traced here: 169 us
  blocking collectives  61.1 us (36%)
  waiting for transfers between devices  42.3 us (25%)
  other arithmetic  23.2 us (14%)
  starting transfers between devices  22.4 us (13%)
  matrix products  16.5 us (10%)
  local copies, waits for them, and re-layouts  1.84 us (1%)
    all_to_all x2, blocking collectives, total(): piece = lax.all_to_all(mine, ('z', 'x'), 0, 0, tiled=True).sum(axis=0)  37.2 us
    all_to_all x2, blocking collectives, total(): lax.all_to_all(jnp.broadcast_to(piece[None], mine.shape), ('z', 'x'), 0,...  23.9 us
    ppermute x2, waiting for transfers between devices, total(): arrived = lax.ppermute(downs, every, to_row_group())  11.1 us
    all_to_all x1, waiting for transfers between devices, on_device(): lax.all_to_all(jnp.broadcast_to(gram[None], (8, *gram.shape)), ROW, 0, 0,...  9.84 us
    another operation x5, other arithmetic, inverse_of_lower(): return lax.linalg.triangular_solve(factor, eye, left_side=True, lower=True)  8.61 us
    dot_general x2, matrix products, down(): product = jnp.einsum('spk,skl->pl', four * weight, blocks, precision=BLOCKS)  7.23 us
    ppermute x2, waiting for transfers between devices, to_column(): return lax.ppermute(mine, every, from_row_group())  6.59 us
    all_to_all x1, starting transfers between devices, on_device(): lax.all_to_all(jnp.broadcast_to(moved[None], (slots, vecs, width)), 'z',...  5.89 us
  transfers between devices with their start and end apart: 11, of which 10 were waited for; matrix products, arithmetic and copies ran while one was open for 16% of the time, Pallas kernels for 0%

profile of v1, /device:TPU:2, one launch (start us, length us, event | category | flops | bytes accessed | tf_op | source)
XLA Modules:
  0.0 169.1 jit_solution(10973344390655046058)
XLA Ops:
  0.6 3.3 %collective-permute-start = (f32[32,512]{1,0:T(8,128)}, f32[32,512]{1,0:T(8,128)S(1)}, u32[]{:S(2)}, u32[]{:S(2)}) collective-permute-start(f32[32,512]{1,0:T(8,128)} %param.7), channel_id=1, source_target_pairs={{0,5},{1,34},{2,64},{3,103},{4,147},{5,180},{6,214},{7,241},{8,13}... | collective-permute-start | bytes 196616 | tf_op jit(solution)/shard_map/ppermute | solution.py:134
  3.9 4.0 %collective-permute-done = f32[32,512]{1,0:T(8,128)S(1)} collective-permute-done((f32[32,512]{1,0:T(8,128)}, f32[32,512]{1,0:T(8,128)S(1)}, u32[]{:S(2)}, u32[]{:S(2)}) %collective-permute-start) | collective-permute-done | bytes 65568 | tf_op jit(solution)/shard_map/ppermute | solution.py:134
  8.6 5.9 %all-to-all-start = ((f32[4,32,512]{2,1,0:T(8,128)}), f32[4,32,512]{2,1,0:T(8,128)S(1)}, u32[]{:S(2)}, u32[]{:S(2)}) async-start(f32[4,32,512]{2,1,0:T(8,128)} %broadcast_in_dim.85), calls=%async_computation | async-start | bytes 524288 | tf_op jit(solution)/shard_map/all_to_all | solution.py:135
  17.1 5.5 %all-to-all-done = f32[4,32,512]{2,1,0:T(8,128)S(1)} async-done(((f32[4,32,512]{2,1,0:T(8,128)}), f32[4,32,512]{2,1,0:T(8,128)S(1)}, u32[]{:S(2)}, u32[]{:S(2)}) %all-to-all-start) | async-done | bytes 262176 | tf_op jit(solution)/shard_map/all_to_all | solution.py:135
  22.7 3.7 %fusion.29 = f32[32,512]{1,0:T(8,128)S(1)} fusion(f32[4,1,512,512]{3,2,1,0:T(8,128)} %param.9, f32[4,32,512]{2,1,0:T(8,128)S(1)} %maximum_select_fusion, f32[4]{0:T(128)S(1)} %compare_select_fusion.1, f32[32,512]{1,0:T(8,128)} %param.7, f32[512]{0:T(512)S(1)} %add_multiply_fusion), kind=kOutput, calls=%fused_computation.15 | convolution fusion | flops 201424896 | bytes 4589584 | tf_op jit(solution)/shard_map/spk,skl->pl/dot_general | solution.py:107
  26.4 2.3 %collective-permute-start.1 = (f32[32,512]{1,0:T(8,128)S(1)}, f32[32,512]{1,0:T(8,128)S(1)}, u32[]{:S(2)}, u32[]{:S(2)}) collective-permute-start(f32[32,512]{1,0:T(8,128)S(1)} %fusion.29), channel_id=1, source_target_pairs={{0,5},{1,34},{2,64},{3,103},{4,147},{5,180},{6,214},{7,241},{8,13}... | collective-permute-start | bytes 196616 | tf_op jit(solution)/shard_map/ppermute | solution.py:114
  28.7 4.5 %collective-permute-done.1 = f32[32,512]{1,0:T(8,128)S(1)} collective-permute-done((f32[32,512]{1,0:T(8,128)S(1)}, f32[32,512]{1,0:T(8,128)S(1)}, u32[]{:S(2)}, u32[]{:S(2)}) %collective-permute-start.1) | collective-permute-done | bytes 65568 | tf_op jit(solution)/shard_map/ppermute | solution.py:114
  36.6 19.7 %all_to_all.30 = f32[16,8,256]{2,1,0:T(8,128)S(1)} all-to-all(f32[16,8,256]{2,1,0:T(8,128)S(1)} %select_add_fusion.2), channel_id=1, replica_groups=mesh['zh'=2,'y'=4,'z'=4,'x'=4,'co'=2] {'z','x'}, dimensions={0} | all-to-all | bytes 262144 | tf_op jit(solution)/shard_map/all_to_all | solution.py:121
  56.4 12.1 %all_to_all.31 = f32[16,8,256]{2,1,0:T(8,128)S(1)} all-to-all(f32[16,8,256]{2,1,0:T(8,128)S(1)} %broadcast_in_dim.92), channel_id=1, replica_groups=mesh['zh'=2,'y'=4,'z'=4,'x'=4,'co'=2] {'z','x'}, dimensions={0} | all-to-all | bytes 262144 | tf_op jit(solution)/shard_map/all_to_all | solution.py:122
  70.5 6.6 %collective-permute-done.4 = f32[32,512]{1,0:T(8,128)S(1)} collective-permute-done((f32[32,512]{1,0:T(8,128)S(1)}, f32[32,512]{1,0:T(8,128)S(1)}, u32[]{:S(2)}, u32[]{:S(2)}) %collective-permute-start.4) | collective-permute-done | bytes 65568 | tf_op jit(solution)/shard_map/ppermute | solution.py:132
  77.1 3.5 %fusion.38 = f32[32,512]{1,0:T(8,128)S(1)} fusion(f32[4,1,512,512]{3,2,1,0:T(8,128)} %param.9, f32[4,32,512]{2,1,0:T(8,128)S(1)} %bitcast.120, f32[4]{0:T(128)S(1)} %compare_select_fusion.1, f32[32,512]{1,0:T(8,128)S(1)} %collective-permute-done.4, f32[512]{0:T(512)S(1)} %add_multiply_fusion), kind=kOutput, calls=%fused_computation.30 | convolution fusion | flops 201424896 | bytes 4589584 | tf_op jit(solution)/shard_map/spk,skl->pl/dot_general | solution.py:107
  80.8 6.6 %collective-permute-done.5 = f32[32,512]{1,0:T(8,128)S(1)} collective-permute-done((f32[32,512]{1,0:T(8,128)S(1)}, f32[32,512]{1,0:T(8,128)S(1)}, u32[]{:S(2)}, u32[]{:S(2)}) %collective-permute-start.5) | collective-permute-done | bytes 65568 | tf_op jit(solution)/shard_map/ppermute | solution.py:114
  87.4 2.0 %fusion.20 = f32[4,32,512]{2,1,0:T(8,128)S(1)} fusion(f32[4,1,512,512]{3,2,1,0:T(8,128)S(1)} %copy-done.1, f32[32,512]{1,0:T(8,128)S(1)} %collective-permute-done.5, f32[4]{0:T(128)S(1)} %compare_select_fusion.1, pred[4]{0:T(512)(128)(4,1)S(1)} %iota_compare_fusion.5, f32[32,512]{1,0:T(8,128)S(1)} %collective-permute-done.4), kind=kOutput, calls=%fused_computation.12 | convolution fusion | flops 201523200 | bytes 4587540 | tf_op jit(solution)/shard_map/pl,skl->spk/dot_general | solution.py:111
  90.9 17.5 %all_to_all.32 = f32[16,8,256]{2,1,0:T(8,128)S(1)} all-to-all(f32[16,8,256]{2,1,0:T(8,128)S(1)} %select_add_fusion.1), channel_id=1, replica_groups=mesh['zh'=2,'y'=4,'z'=4,'x'=4,'co'=2] {'z','x'}, dimensions={0} | all-to-all | bytes 262144 | tf_op jit(solution)/shard_map/all_to_all | solution.py:121
  108.4 11.8 %all_to_all.33 = f32[16,8,256]{2,1,0:T(8,128)S(1)} all-to-all(f32[16,8,256]{2,1,0:T(8,128)S(1)} %broadcast_in_dim.94), channel_id=1, replica_groups=mesh['zh'=2,'y'=4,'z'=4,'x'=4,'co'=2] {'z','x'}, dimensions={0} | all-to-all | bytes 262144 | tf_op jit(solution)/shard_map/all_to_all | solution.py:122
  123.1 5.6 %all-to-all-start.5 = ((f32[8,96,96]{2,1,0:T(8,128)}), f32[8,96,96]{2,1,0:T(8,128)S(1)}, u32[]{:S(2)}, u32[]{:S(2)}) async-start(f32[8,96,96]{2,1,0:T(8,128)} %broadcast_in_dim.95), calls=%async_computation.5 | async-start | bytes 786432 | tf_op jit(solution)/shard_map/all_to_all | solution.py:147
  128.8 4.5 %collective-permute-start.8 = (f32[32,512]{1,0:T(8,128)S(1)}, f32[32,512]{1,0:T(8,128)S(1)}, u32[]{:S(2)}, u32[]{:S(2)}) collective-permute-start(f32[32,512]{1,0:T(8,128)S(1)} %select_reduce_fusion), channel_id=1, source_target_pairs={{5,0},{34,1},{64,2},{103,3},{147,4},{180,5},{214,6},{241,7},{13,8}... | collective-permute-start | bytes 196616 | tf_op jit(solution)/shard_map/ppermute | solution.py:132
  133.4 9.8 %all-to-all-done.5 = f32[8,96,96]{2,1,0:T(8,128)S(1)} async-done(((f32[8,96,96]{2,1,0:T(8,128)}), f32[8,96,96]{2,1,0:T(8,128)S(1)}, u32[]{:S(2)}, u32[]{:S(2)}) %all-to-all-start.5) | async-done | bytes 294944 | tf_op jit(solution)/shard_map/all_to_all | solution.py:147
  143.4 2.9 %cholesky.59 = f32[32,32]{1,0:T(8,128)S(1)} custom-call(f32[32,32]{1,0:T(8,128)S(1)} %fusion.72), custom_call_target="Cholesky" | custom-call | tf_op jit(solution)/shard_map/jit(cholesky)/cholesky | solution.py:64
  147.7 2.4 %custom-call.7 = f32[1,32,32]{1,2,0:T(8,128)S(1)} custom-call(f32[1,32,32]{2,1,0:T(8,128)S(1)} %fusion.62), custom_call_target="InvertDiagBlocksLowerTriangular" | custom-call | tf_op jit(solution)/shard_map/triangular_solve/custom-call.0 | solution.py:53
  151.5 2.9 %cholesky.70 = f32[32,32]{1,0:T(8,128)S(1)} custom-call(f32[32,32]{1,0:T(8,128)S(1)} %fusion.70), custom_call_target="Cholesky" | custom-call | tf_op jit(solution)/shard_map/jit(cholesky)/cholesky | solution.py:70
  156.6 2.4 %custom-call.8 = f32[1,32,32]{1,2,0:T(8,128)S(1)} custom-call(f32[1,32,32]{2,1,0:T(8,128)S(1)} %get-tuple-element.13), custom_call_target="InvertDiagBlocksLowerTriangular" | custom-call | tf_op jit(solution)/shard_map/triangular_solve/custom-call.0 | solution.py:53
  160.5 2.9 %cholesky.81 = f32[32,32]{1,0:T(8,128)S(1)} custom-call(f32[32,32]{1,0:T(8,128)S(1)} %fusion.68), custom_call_target="Cholesky" | custom-call | tf_op jit(solution)/shard_map/jit(cholesky)/cholesky | solution.py:77
  164.8 2.4 %custom-call.9 = f32[1,32,32]{1,2,0:T(8,128)S(1)} custom-call(f32[1,32,32]{2,1,0:T(8,128)S(1)} %get-tuple-element.10), custom_call_target="InvertDiagBlocksLowerTriangular" | custom-call | tf_op jit(solution)/shard_map/triangular_solve/custom-call.0 | solution.py:53
  (82 shorter events, 22.5 us)
Async XLA Ops:
  0.6 32.6 %copy-start.2 = (f32[32,512]{1,0:T(8,128)S(1)}, f32[32,512]{1,0:T(8,128)}, u32[]{:S(2)}) copy-start(f32[32,512]{1,0:T(8,128)} %param.7) | copy-start | bytes 196612
  0.6 7.2 %collective-permute-start = (f32[32,512]{1,0:T(8,128)}, f32[32,512]{1,0:T(8,128)S(1)}, u32[]{:S(2)}, u32[]{:S(2)}) collective-permute-start(f32[32,512]{1,0:T(8,128)} %param.7), channel_id=1, source_target_pairs={{0,5},{1,34},{2,64},{3,103},{4,147},{5,180},{6,214},{7,241},{8,13}... | collective-permute-start | bytes 196616 | tf_op jit(solution)/shard_map/ppermute | solution.py:134
  8.6 14.1 %all-to-all-start = ((f32[4,32,512]{2,1,0:T(8,128)}), f32[4,32,512]{2,1,0:T(8,128)S(1)}, u32[]{:S(2)}, u32[]{:S(2)}) async-start(f32[4,32,512]{2,1,0:T(8,128)} %broadcast_in_dim.85), calls=%async_computation | async-start | bytes 524288 | tf_op jit(solution)/shard_map/all_to_all | solution.py:135
  22.7 10.5 %copy-start = (f32[4,1,512,512]{3,2,1,0:T(8,128)S(1)}, f32[4,1,512,512]{3,2,1,0:T(8,128)}, u32[]{:S(2)}) copy-start(f32[4,1,512,512]{3,2,1,0:T(8,128)} %param.9) | copy-start | bytes 12582916
  26.4 6.8 %collective-permute-start.1 = (f32[32,512]{1,0:T(8,128)S(1)}, f32[32,512]{1,0:T(8,128)S(1)}, u32[]{:S(2)}, u32[]{:S(2)}) collective-permute-start(f32[32,512]{1,0:T(8,128)S(1)} %fusion.29), channel_id=1, source_target_pairs={{0,5},{1,34},{2,64},{3,103},{4,147},{5,180},{6,214},{7,241},{8,13}... | collective-permute-start | bytes 196616 | tf_op jit(solution)/shard_map/ppermute | solution.py:114
  35.1 1.4 collective-permute-start.2
  56.4 31.0 %copy-start.1 = (f32[4,1,512,512]{3,2,1,0:T(8,128)S(1)}, f32[4,1,512,512]{3,2,1,0:T(8,128)}, u32[]{:S(2)}) copy-start(f32[4,1,512,512]{3,2,1,0:T(8,128)} %param.9) | copy-start | bytes 12582916
  68.5 1.3 collective-permute-start.3
  70.0 7.1 %collective-permute-start.4 = (f32[32,512]{1,0:T(8,128)S(1)}, f32[32,512]{1,0:T(8,128)S(1)}, u32[]{:S(2)}, u32[]{:S(2)}) collective-permute-start(f32[32,512]{1,0:T(8,128)S(1)} %select_reduce_fusion.1), channel_id=1, source_target_pairs={{5,0},{34,1},{64,2},{103,3},{147,4},{180,5},{214,6},{241,7},{13,8}... | collective-permute-start | bytes 196616 | tf_op jit(solution)/shard_map/ppermute | solution.py:132
  80.6 6.8 %collective-permute-start.5 = (f32[32,512]{1,0:T(8,128)S(1)}, f32[32,512]{1,0:T(8,128)S(1)}, u32[]{:S(2)}, u32[]{:S(2)}) collective-permute-start(f32[32,512]{1,0:T(8,128)S(1)} %fusion.38), channel_id=1, source_target_pairs={{0,5},{1,34},{2,64},{3,103},{4,147},{5,180},{6,214},{7,241},{8,13}... | collective-permute-start | bytes 196616 | tf_op jit(solution)/shard_map/ppermute | solution.py:114
  89.4 1.4 collective-permute-start.6
  120.2 1.3 collective-permute-start.7
  123.1 20.0 %all-to-all-start.5 = ((f32[8,96,96]{2,1,0:T(8,128)}), f32[8,96,96]{2,1,0:T(8,128)S(1)}, u32[]{:S(2)}, u32[]{:S(2)}) async-start(f32[8,96,96]{2,1,0:T(8,128)} %broadcast_in_dim.95), calls=%async_computation.5 | async-start | bytes 786432 | tf_op jit(solution)/shard_map/all_to_all | solution.py:147
  128.8 39.4 %collective-permute-start.8 = (f32[32,512]{1,0:T(8,128)S(1)}, f32[32,512]{1,0:T(8,128)S(1)}, u32[]{:S(2)}, u32[]{:S(2)}) collective-permute-start(f32[32,512]{1,0:T(8,128)S(1)} %select_reduce_fusion), channel_id=1, source_target_pairs={{5,0},{34,1},{64,2},{103,3},{147,4},{180,5},{214,6},{241,7},{13,8}... | collective-permute-start | bytes 196616 | tf_op jit(solution)/shard_map/ppermute | solution.py:132

commit v2 on v1

v2 whole, which is shorter than its diff:
```python
import functools

import jax
import jax.numpy as jnp
from jax import lax
from jax.experimental import pallas as pl
from jax.experimental.pallas import tpu as pltpu
from jax.sharding import Mesh
from jax.sharding import PartitionSpec as P

SHIFT = 5.5
FULL = lax.Precision.HIGHEST
BLOCKS = lax.Precision.HIGH

SIZES = (2, 4, 4, 4, 2)
NAMES = ("zh", "y", "z", "x", "co")
ROW = ("zh", "y")
COL = ("z", "x", "co")

PLACE = (
    (5, 3, 2, 4, 7, 1, 0, 6),
    (2, 4, 5, 3, 0, 6, 7, 1),
    (0, 1, 7, 6, 2, 3, 5, 4),
    (7, 0, 4, 6, 2, 3, 1, 5),
    (3, 5, 4, 2, 1, 0, 6, 7),
    (4, 2, 3, 5, 1, 0, 6, 7),
    (6, 0, 1, 7, 4, 2, 3, 5),
    (1, 7, 6, 0, 3, 5, 4, 2),
)


def to_row_group():
    pairs = []
    for row in range(8):
        for z in range(4):
            for j in range(8):
                far = (row // 4) != (j // 4)
                z_to = (z + 2) % 4 if far else z
                pairs.append((row * 32 + z * 8 + j, j * 32 + z_to * 8 + PLACE[j][row]))
    return pairs


def from_row_group():
    return [(b, a) for a, b in to_row_group()]


def far_table():
    table = [[0.0] * 8 for _ in range(8)]
    for j in range(8):
        for row in range(8):
            table[j][PLACE[j][row]] = float((row // 4) != (j // 4))
    return table


def mm(a, b):
    return jnp.dot(a, b, precision=FULL, preferred_element_type=jnp.float32)
def mmt(a, b):
    return lax.dot_general(a, b, (((1,), (1,)), ((), ())), precision=FULL, preferred_element_type=jnp.float32)


def factor_and_inverse(g):
    n = g.shape[0]
    down = lax.broadcasted_iota(jnp.int32, (n, 2 * n), 0)
    along = lax.broadcasted_iota(jnp.int32, (n, 2 * n), 1)
    same = (down == along)[:, :n]
    diagonal = jnp.where(same, g, 0.0)
    root = jnp.sqrt(jnp.sum(diagonal, axis=0, keepdims=True))
    root_down = jnp.sqrt(jnp.sum(diagonal, axis=1, keepdims=True))
    wide = jnp.concatenate([g / root, jnp.where(same, 1.0, 0.0)], axis=1) / root_down
    for k in range(0, n - 2, 2):
        r0 = jnp.broadcast_to(wide[k : k + 1, :], (8, 2 * n))
        r1 = jnp.broadcast_to(wide[k + 1 : k + 2, :], (8, 2 * n))
        a = jnp.broadcast_to(r0[:, k : k + 1], r0.shape)
        b = jnp.broadcast_to(r0[:, k + 1 : k + 2], r0.shape)
        c = jnp.broadcast_to(r1[:, k + 1 : k + 2], r0.shape)
        c0 = jnp.broadcast_to(wide[:, k : k + 1], wide.shape)
        c1 = jnp.broadcast_to(wide[:, k + 1 : k + 2], wide.shape)
        det = 1.0 / (a * c - b * b)
        s0 = jnp.concatenate([(r0 * c - r1 * b) * det] * (n // 8), axis=0)
        s1 = jnp.concatenate([(r1 * a - r0 * b) * det] * (n // 8), axis=0)
        wide = jnp.where(down > k + 1, wide - (c0 * s0 + c1 * s1), wide)
    above = jnp.roll(wide, 1, axis=0)
    left = down - 1 == along
    b = jnp.sum(jnp.where(left, wide, 0.0), axis=1, keepdims=True)
    a = jnp.sum(jnp.where(left, above, 0.0), axis=1, keepdims=True)
    wide = jnp.where(lax.rem(down, 2) == 1, wide - (b / a) * above, wide)
    pivot = jnp.sum(jnp.where(down == along, wide, 0.0), axis=1, keepdims=True)
    wide = wide * (1.0 / jnp.sqrt(pivot))
    upper = jnp.where(down <= along, wide, 0.0)[:, :n] * root
    return jnp.transpose(upper), wide[:, n:]


def finish(scale, grams_ref, x_ref, y_ref, z_ref, hist_ref, out_ref, g_ref, p_ref, v_ref):
    n = 32
    part = jnp.sum(grams_ref[...], axis=0) * scale
    at = 0
    for i in range(3):
        for k in range(i + 1):
            block = part[:, at * n : (at + 1) * n]
            g_ref[i * n : (i + 1) * n, k * n : (k + 1) * n] = block
            if k < i:
                g_ref[k * n : (k + 1) * n, i * n : (i + 1) * n] = jnp.transpose(block)
            at += 1
    v_ref[0:n] = x_ref[...]
    v_ref[n : 2 * n] = y_ref[...]
    v_ref[2 * n :] = z_ref[...]
    eye = jnp.where(
        lax.broadcasted_iota(jnp.int32, (n, n), 0) == lax.broadcasted_iota(jnp.int32, (n, n), 1),
        SHIFT,
        0.0,
    )
    low0, t0 = factor_and_inverse(g_ref[0:n, 0:n])
    a0 = mmt(mm(t0, g_ref[n : 2 * n, 0:n]), t0)
    hist_ref[0, 0] = a0 + eye
    m0 = mm(a0, t0)
    p_ref[:, 0:n] = -m0
    p_ref[:, n : 2 * n] = t0
    p1 = p_ref[:, 0 : 2 * n]
    low1, t1 = factor_and_inverse(mmt(mm(p1, g_ref[0 : 2 * n, 0 : 2 * n]), p1))
    hist_ref[0, 1] = low1
    q1 = mm(t1, p1)
    d0 = lax.dot_general(
        low1, t0, (((0,), (0,)), ((), ())), precision=FULL, preferred_element_type=jnp.float32
    )
    p_ref[:, 0:n] = -d0
    p_ref[:, n : 3 * n] = q1
    w1 = p_ref[...]
    a1 = mmt(mm(w1, g_ref[:, 0 : 2 * n]), q1)
    hist_ref[1, 0] = a1 + eye
    p_ref[:, 0 : 2 * n] = mm(a1, q1)
    w1 = jnp.concatenate([w1[:, 0 : 2 * n] - p_ref[:, 0 : 2 * n], w1[:, 2 * n :]], axis=1)
    low2, t2 = factor_and_inverse(mmt(mm(w1, g_ref[...]), w1))
    hist_ref[1, 1] = low2
    out_ref[...] = mm(t2, mm(w1, v_ref[...]))


def close(grams, x, y, z, length):
    vecs = x.shape[0]
    return pl.pallas_call(
        functools.partial(finish, 1.0 / length),
        out_shape=(
            jax.ShapeDtypeStruct((2, 2, vecs, vecs), jnp.float32),
            jax.ShapeDtypeStruct(x.shape, jnp.float32),
        ),
        scratch_shapes=[
            pltpu.VMEM((3 * vecs, 3 * vecs), jnp.float32),
            pltpu.VMEM((vecs, 3 * vecs), jnp.float32),
            pltpu.VMEM((3 * vecs, x.shape[1]), jnp.float32),
        ],
        name="recurrence",
    )(grams, x, y, z)


def on_device(start_block, energies, hamiltonian):
    vecs, width = start_block.shape
    col_count = lax.axis_size(COL)
    half = width // 2
    row = lax.axis_index(ROW)
    col = lax.axis_index(COL)
    z = lax.axis_index("z")
    core = lax.axis_index("co")
    place = lax.axis_index(("x", "co"))
    blocks = hamiltonian[:, 0]
    slots = blocks.shape[0]
    block_rows = row + 8 * jnp.arange(slots, dtype=jnp.int32)
    weight = jnp.where(block_rows < col, 1.0, jnp.where(block_rows == col, 0.5, 0.0)).astype(
        jnp.float32
    )[:, None, None]
    lead = jnp.where(place == row, energies - SHIFT, 0.0)
    own_slot = (jnp.arange(slots) == z)[:, None, None]
    table = jnp.array(far_table(), jnp.float32).reshape(-1)
    far = jnp.sum(table * (jnp.arange(64) == row * 8 + place).astype(jnp.float32)) > 0.5
    slot = jnp.where(far, (z + 2) % 4, z)
    in_slot = (jnp.arange(slots) == slot)[:, None, None]
    every = NAMES

    def down(four):
        return jnp.einsum("spk,skl->pl", four * weight, blocks, precision=BLOCKS)

    def across(own):
        product = jnp.einsum("pl,skl->spk", own, blocks, precision=BLOCKS) * weight
        return product + jnp.where(own_slot, (lead[None, :] * own)[None], 0.0)

    def total(acrosses, downs):
        arrived = lax.ppermute(downs, every, to_row_group())
        part = acrosses + jnp.where(in_slot, arrived[None], 0.0)
        part = part.reshape(slots * vecs // 8, 8, width)
        low, high = part[..., :half], part[..., half:]
        mine = jnp.where(core == 0, low, high)
        other = jnp.where(core == 0, high, low)
        mine = mine + lax.ppermute(other, "co", [(0, 1), (1, 0)])
        piece = lax.all_to_all(mine, ("z", "x"), 0, 0, tiled=True).sum(axis=0)
        whole = lax.all_to_all(
            jnp.broadcast_to(piece[None], mine.shape), ("z", "x"), 0, 0, tiled=True
        )
        facing = lax.ppermute(whole, "co", [(0, 1), (1, 0)])
        low = jnp.where(core == 0, whole, facing)
        high = jnp.where(core == 0, facing, whole)
        return jnp.concatenate([low, high], axis=-1).reshape(slots, vecs, width)

    def slot_of(four):
        return jnp.sum(jnp.where(in_slot, four, 0.0), axis=0)

    def inner(left, right):
        return jnp.einsum("spk,sqk->pq", left, right, precision=FULL)

    moved = lax.ppermute(start_block, every, to_row_group())
    x4 = lax.all_to_all(
        jnp.broadcast_to(moved[None], (slots, vecs, width)), "z", 0, 0, tiled=True
    )
    x4 = jnp.where(far, jnp.roll(x4, 2, axis=0), x4)
    x = start_block
    y4 = total(across(x), down(x4))
    y = lax.ppermute(slot_of(y4), every, from_row_group())
    xy4 = jnp.concatenate([x4, y4], axis=1)
    z4 = total(across(y), down(y4))
    grams = jnp.concatenate([inner(x4, x4), inner(y4, xy4), inner(z4, xy4), inner(z4, z4)], axis=1)
    back = lax.ppermute(
        jnp.concatenate([slot_of(z4), grams], axis=1), every, from_row_group()
    )
    zz, grams = back[:, :width], back[:, width:]
    grams = lax.all_to_all(
        jnp.broadcast_to(grams[None], (8, *grams.shape)), ("x", "co"), 0, 0, tiled=True
    )
    return close(grams, x, y, zz, col_count * width)


def solution(mesh):
    fine = Mesh(mesh.devices.reshape(SIZES), NAMES)
    placed = (P(None, COL), P(COL), P(ROW, COL, None, None))
    return jax.shard_map(
        on_device, mesh=fine, in_specs=placed, out_specs=(P(), P(None, COL)), check_vma=False
    )
```

time: 171 us -> 152 us (0.89)
  other arithmetic: 23.2 us -> 3.29 us
  Pallas kernels: 0 us -> 10.8 us
  waiting for transfers between devices: 42.3 us -> 33.3 us
  matrix products: 16.5 us -> 12.9 us
  blocking collectives: 61.1 us -> 64.2 us
    another operation x19 -> x0, other arithmetic: 20.7 us -> none  [the longest x5 8.61 us: inverse_of_lower(): return lax.linalg.triangular_solve(factor, eye, left_side=True, lower=True)]
    pallas_call x0 -> x1, Pallas kernels: none -> 10.8 us  [close(): pl.pallas_call(functools.partial(finish, 1.0 / length), out_shape=(jax.Sh...]
    ppermute x2, starting transfers between devices: 4.99 us -> 0.58 us  [the longest x1 0.49 us: on_device(): y = lax.ppermute(slot_of(y4), every, from_row_group())]
    all_to_all x1, waiting for transfers between devices: 9.84 us -> 5.46 us  [on_device(): lax.all_to_all(jnp.broadcast_to(grams[None], (8, *grams.shape)), ('x', 'c...]
    ppermute x2, waiting for transfers between devices: 11.1 us -> 7.09 us  [total(): arrived = lax.ppermute(downs, every, to_row_group())]
    ppermute x2, starting transfers between devices: 2.45 us -> 6.4 us  [total(): arrived = lax.ppermute(downs, every, to_row_group())]
    all_to_all x2, blocking collectives: 37.2 us -> 40.3 us  [total(): piece = lax.all_to_all(mine, ('z', 'x'), 0, 0, tiled=True).sum(axis=0)]
    dot_general x19 -> x8, matrix products: 15.8 us -> 12.9 us  [the longest x2 7.23 us: down(): return jnp.einsum('spk,skl->pl', four * weight, blocks, precision=BLOCKS)]
  transfers between devices with their start and end apart: 11 -> 11, of which waited for: 10 -> 10; matrix products, arithmetic and copies ran while one was open for 16% -> 5% of each run, Pallas kernels for 0% -> 0%
where the time goes in v2:
time: 152 us; the launch traced here: 150 us
  blocking collectives  64.2 us (42%)
  waiting for transfers between devices  33.3 us (22%)
  starting transfers between devices  21.4 us (14%)
  matrix products  12.9 us (8%)
  Pallas kernels  10.8 us (7%)
  other arithmetic  3.29 us (2%)
  local copies, waits for them, and re-layouts  2.91 us (2%)
    all_to_all x2, blocking collectives, total(): piece = lax.all_to_all(mine, ('z', 'x'), 0, 0, tiled=True).sum(axis=0)  40.3 us
    all_to_all x2, blocking collectives, total(): lax.all_to_all(jnp.broadcast_to(piece[None], mine.shape), ('z', 'x'), 0,...  23.9 us
    pallas_call x1, Pallas kernels, close(): pl.pallas_call(functools.partial(finish, 1.0 / length), out_shape=(jax.Sh...  10.8 us
    ppermute x1, waiting for transfers between devices, on_device(): lax.ppermute(jnp.concatenate([slot_of(z4), grams], axis=1), every, from_r...  7.67 us
    dot_general x2, matrix products, down(): return jnp.einsum('spk,skl->pl', four * weight, blocks, precision=BLOCKS)  7.23 us
    ppermute x2, waiting for transfers between devices, total(): arrived = lax.ppermute(downs, every, to_row_group())  7.09 us
    ppermute x2, starting transfers between devices, total(): arrived = lax.ppermute(downs, every, to_row_group())  6.4 us
    all_to_all x1, starting transfers between devices, on_device(): lax.all_to_all(jnp.broadcast_to(moved[None], (slots, vecs, width)), 'z',...  5.89 us
  transfers between devices with their start and end apart: 11, of which 10 were waited for; matrix products, arithmetic and copies ran while one was open for 5% of the time, Pallas kernels for 0%

profile of v2, /device:TPU:2, one launch (start us, length us, event | category | flops | bytes accessed | tf_op | source)
XLA Modules:
  0.0 150.4 jit_solution(5753845053181346017)
XLA Ops:
  0.6 3.3 %collective-permute-start = (f32[32,512]{1,0:T(8,128)}, f32[32,512]{1,0:T(8,128)S(1)}, u32[]{:S(2)}, u32[]{:S(2)}) collective-permute-start(f32[32,512]{1,0:T(8,128)} %x_ref.1), channel_id=1, source_target_pairs={{0,5},{1,34},{2,64},{3,103},{4,147},{5,180},{6,214},{7,241},{8,13}... | collective-permute-start | bytes 196616 | tf_op jit(solution)/shard_map/ppermute | solution.py:207
  4.6 3.3 %collective-permute-done = f32[32,512]{1,0:T(8,128)S(1)} collective-permute-done((f32[32,512]{1,0:T(8,128)}, f32[32,512]{1,0:T(8,128)S(1)}, u32[]{:S(2)}, u32[]{:S(2)}) %collective-permute-start) | collective-permute-done | bytes 65568 | tf_op jit(solution)/shard_map/ppermute | solution.py:207
  8.6 5.9 %all-to-all-start = ((f32[4,32,512]{2,1,0:T(8,128)}), f32[4,32,512]{2,1,0:T(8,128)S(1)}, u32[]{:S(2)}, u32[]{:S(2)}) async-start(f32[4,32,512]{2,1,0:T(8,128)} %broadcast_in_dim.118), calls=%async_computation | async-start | bytes 524288 | tf_op jit(solution)/shard_map/all_to_all | solution.py:208
  14.5 1.3 select_reduce_fusion.2
  17.3 5.4 %all-to-all-done = f32[4,32,512]{2,1,0:T(8,128)S(1)} async-done(((f32[4,32,512]{2,1,0:T(8,128)}), f32[4,32,512]{2,1,0:T(8,128)S(1)}, u32[]{:S(2)}, u32[]{:S(2)}) %all-to-all-start) | async-done | bytes 262176 | tf_op jit(solution)/shard_map/all_to_all | solution.py:208
  22.7 3.7 %fusion.29 = f32[32,512]{1,0:T(8,128)S(1)} fusion(f32[4,1,512,512]{3,2,1,0:T(8,128)} %param.6, f32[4,32,512]{2,1,0:T(8,128)S(1)} %maximum_select_fusion, f32[4]{0:T(128)S(1)} %compare_select_fusion.1), kind=kOutput, calls=%fused_computation.15 | convolution fusion | flops 201392128 | bytes 4522000 | tf_op jit(solution)/shard_map/spk,skl->pl/dot_general | solution.py:178
  26.4 2.3 %collective-permute-start.1 = (f32[32,512]{1,0:T(8,128)S(1)}, f32[32,512]{1,0:T(8,128)S(1)}, u32[]{:S(2)}, u32[]{:S(2)}) collective-permute-start(f32[32,512]{1,0:T(8,128)S(1)} %fusion.29), channel_id=1, source_target_pairs={{0,5},{1,34},{2,64},{3,103},{4,147},{5,180},{6,214},{7,241},{8,13}... | collective-permute-start | bytes 196616 | tf_op jit(solution)/shard_map/ppermute | solution.py:185
  28.7 4.5 %collective-permute-done.1 = f32[32,512]{1,0:T(8,128)S(1)} collective-permute-done((f32[32,512]{1,0:T(8,128)S(1)}, f32[32,512]{1,0:T(8,128)S(1)}, u32[]{:S(2)}, u32[]{:S(2)}) %collective-permute-start.1) | collective-permute-done | bytes 65568 | tf_op jit(solution)/shard_map/ppermute | solution.py:185
  33.2 1.9 %select_add_fusion = f32[4,32,512]{2,1,0:T(8,128)S(1)} fusion(f32[32,512]{1,0:T(8,128)S(1)} %collective-permute-done.1, f32[4,1,512,512]{3,2,1,0:T(8,128)S(1)} %copy-done, f32[32,512]{1,0:T(8,128)S(1)} %broadcast_multiply_fusion.1, f32[4]{0:T(128)S(1)} %compare_select_fusion.1, pred[4]{0:T(512)(128)(4,1)S(1)} %get-tuple-element.8, ...), kind=kOutput, calls=%fused_computation.28 | convolution fusion | flops 201654272 | bytes 4653080 | tf_op jit(solution)/shard_map/pl,skl->spk/dot_general | solution.py:181
  35.3 1.3 collective-permute-done.2
  36.6 19.7 %all_to_all.30 = f32[16,8,256]{2,1,0:T(8,128)S(1)} all-to-all(f32[16,8,256]{2,1,0:T(8,128)S(1)} %select_add_fusion.2), channel_id=1, replica_groups=mesh['zh'=2,'y'=4,'z'=4,'x'=4,'co'=2] {'z','x'}, dimensions={0} | all-to-all | bytes 262144 | tf_op jit(solution)/shard_map/all_to_all | solution.py:192
  56.4 12.1 %all_to_all.31 = f32[16,8,256]{2,1,0:T(8,128)S(1)} all-to-all(f32[16,8,256]{2,1,0:T(8,128)S(1)} %broadcast_in_dim.120), channel_id=1, replica_groups=mesh['zh'=2,'y'=4,'z'=4,'x'=4,'co'=2] {'z','x'}, dimensions={0} | all-to-all | bytes 262144 | tf_op jit(solution)/shard_map/all_to_all | solution.py:193
  68.5 1.3 collective-permute-done.3
  70.5 3.5 %fusion.32 = f32[32,512]{1,0:T(8,128)S(1)} fusion(f32[4,1,512,512]{3,2,1,0:T(8,128)} %param.6, f32[4,32,512]{2,1,0:T(8,128)S(1)} %bitcast.74, f32[4]{0:T(128)S(1)} %compare_select_fusion.1), kind=kOutput, calls=%fused_computation.16 | convolution fusion | flops 201392128 | bytes 4522000 | tf_op jit(solution)/shard_map/spk,skl->pl/dot_general | solution.py:178
  74.0 4.1 %collective-permute-start.5 = (f32[32,512]{1,0:T(8,128)S(1)}, f32[32,512]{1,0:T(8,128)S(1)}, u32[]{:S(2)}, u32[]{:S(2)}) collective-permute-start(f32[32,512]{1,0:T(8,128)S(1)} %fusion.32), channel_id=1, source_target_pairs={{0,5},{1,34},{2,64},{3,103},{4,147},{5,180},{6,214},{7,241},{8,13}... | collective-permute-start | bytes 196616 | tf_op jit(solution)/shard_map/ppermute | solution.py:185
  78.2 2.6 %collective-permute-done.5 = f32[32,512]{1,0:T(8,128)S(1)} collective-permute-done((f32[32,512]{1,0:T(8,128)S(1)}, f32[32,512]{1,0:T(8,128)S(1)}, u32[]{:S(2)}, u32[]{:S(2)}) %collective-permute-start.5) | collective-permute-done | bytes 65568 | tf_op jit(solution)/shard_map/ppermute | solution.py:185
  80.8 2.0 %fusion.26 = f32[4,32,512]{2,1,0:T(8,128)S(1)} fusion(f32[4,1,512,512]{3,2,1,0:T(8,128)S(1)} %copy-done.1, f32[32,512]{1,0:T(8,128)S(1)} %collective-permute-done.5, f32[32,512]{1,0:T(8,128)S(1)} %broadcast_multiply_fusion, f32[4]{0:T(128)S(1)} %compare_select_fusion.1, pred[4]{0:T(512)(128)(4,1)S(1)} %get-tuple-element.8, ...), kind=kOutput, calls=%fused_computation.14 | convolution fusion | flops 201654272 | bytes 4653080 | tf_op jit(solution)/shard_map/pl,skl->spk/dot_general | solution.py:181
  82.9 1.3 collective-permute-done.6
  84.3 20.5 %all_to_all.32 = f32[16,8,256]{2,1,0:T(8,128)S(1)} all-to-all(f32[16,8,256]{2,1,0:T(8,128)S(1)} %select_add_fusion.1), channel_id=1, replica_groups=mesh['zh'=2,'y'=4,'z'=4,'x'=4,'co'=2] {'z','x'}, dimensions={0} | all-to-all | bytes 262144 | tf_op jit(solution)/shard_map/all_to_all | solution.py:192
  104.9 11.8 %all_to_all.33 = f32[16,8,256]{2,1,0:T(8,128)S(1)} all-to-all(f32[16,8,256]{2,1,0:T(8,128)S(1)} %broadcast_in_dim.123), channel_id=1, replica_groups=mesh['zh'=2,'y'=4,'z'=4,'x'=4,'co'=2] {'z','x'}, dimensions={0} | all-to-all | bytes 262144 | tf_op jit(solution)/shard_map/all_to_all | solution.py:193
  119.3 7.7 %collective-permute-done.8 = f32[32,704]{1,0:T(8,128)S(1)} collective-permute-done((f32[32,704]{1,0:T(8,128)S(1)}, f32[32,704]{1,0:T(8,128)S(1)}, u32[]{:S(2)}, u32[]{:S(2)}) %collective-permute-start.8) | collective-permute-done | bytes 90144 | tf_op jit(solution)/shard_map/ppermute | solution.py:218
  127.7 5.1 %all-to-all-start.5 = ((f32[8,32,192]{2,1,0:T(8,128)}), f32[8,32,192]{2,1,0:T(8,128)S(1)}, u32[]{:S(2)}, u32[]{:S(2)}) async-start(f32[8,32,192]{2,1,0:T(8,128)} %broadcast_in_dim.124), calls=%async_computation.5 | async-start | bytes 524288 | tf_op jit(solution)/shard_map/all_to_all | solution.py:222
  133.4 5.5 %all-to-all-done.5.grams_ref = f32[8,32,192]{2,1,0:T(8,128)S(1)} async-done(((f32[8,32,192]{2,1,0:T(8,128)}), f32[8,32,192]{2,1,0:T(8,128)S(1)}, u32[]{:S(2)}, u32[]{:S(2)}) %all-to-all-start.5) | async-done | bytes 196640 | tf_op jit(solution)/shard_map/all_to_all | solution.py:222
  139.5 10.8 %recurrence.1 = (f32[2,2,32,32]{3,2,1,0:T(8,128)}, f32[32,512]{1,0:T(8,128)}) custom-call(f32[8,32,192]{2,1,0:T(8,128)} %copy-done.2, f32[32,512]{1,0:T(8,128)} %x_ref.1, f32[32,512]{1,0:T(8,128)} %copy-done.4, f32[32,512]{1,0:T(8,128)} %slice.41.z_ref), custom_call_target="tpu_custom_call" | custom-call | tf_op jit(solution)/shard_map/recurrence/pallas_call | solution.py:139
  (48 shorter events, 7.9 us)
Async XLA Ops:
  0.6 32.6 %copy-start.3 = (f32[32,512]{1,0:T(8,128)S(1)}, f32[32,512]{1,0:T(8,128)}, u32[]{:S(2)}) copy-start(f32[32,512]{1,0:T(8,128)} %x_ref.1) | copy-start | bytes 196612
  0.6 7.2 %collective-permute-start = (f32[32,512]{1,0:T(8,128)}, f32[32,512]{1,0:T(8,128)S(1)}, u32[]{:S(2)}, u32[]{:S(2)}) collective-permute-start(f32[32,512]{1,0:T(8,128)} %x_ref.1), channel_id=1, source_target_pairs={{0,5},{1,34},{2,64},{3,103},{4,147},{5,180},{6,214},{7,241},{8,13}... | collective-permute-start | bytes 196616 | tf_op jit(solution)/shard_map/ppermute | solution.py:207
  8.6 14.1 %all-to-all-start = ((f32[4,32,512]{2,1,0:T(8,128)}), f32[4,32,512]{2,1,0:T(8,128)S(1)}, u32[]{:S(2)}, u32[]{:S(2)}) async-start(f32[4,32,512]{2,1,0:T(8,128)} %broadcast_in_dim.118), calls=%async_computation | async-start | bytes 524288 | tf_op jit(solution)/shard_map/all_to_all | solution.py:208
  22.7 10.5 %copy-start = (f32[4,1,512,512]{3,2,1,0:T(8,128)S(1)}, f32[4,1,512,512]{3,2,1,0:T(8,128)}, u32[]{:S(2)}) copy-start(f32[4,1,512,512]{3,2,1,0:T(8,128)} %param.6) | copy-start | bytes 12582916
  26.4 6.8 %collective-permute-start.1 = (f32[32,512]{1,0:T(8,128)S(1)}, f32[32,512]{1,0:T(8,128)S(1)}, u32[]{:S(2)}, u32[]{:S(2)}) collective-permute-start(f32[32,512]{1,0:T(8,128)S(1)} %fusion.29), channel_id=1, source_target_pairs={{0,5},{1,34},{2,64},{3,103},{4,147},{5,180},{6,214},{7,241},{8,13}... | collective-permute-start | bytes 196616 | tf_op jit(solution)/shard_map/ppermute | solution.py:185
  35.2 1.4 collective-permute-start.2
  56.4 24.4 %copy-start.1 = (f32[4,1,512,512]{3,2,1,0:T(8,128)S(1)}, f32[4,1,512,512]{3,2,1,0:T(8,128)}, u32[]{:S(2)}) copy-start(f32[4,1,512,512]{3,2,1,0:T(8,128)} %param.6) | copy-start | bytes 12582916
  68.5 1.3 collective-permute-start.3
  70.0 8.2 %collective-permute-start.4 = (f32[32,512]{1,0:T(8,128)S(1)}, f32[32,512]{1,0:T(8,128)S(1)}, u32[]{:S(2)}, u32[]{:S(2)}) collective-permute-start(f32[32,512]{1,0:T(8,128)S(1)} %select_reduce_fusion.1), channel_id=1, source_target_pairs={{5,0},{34,1},{64,2},{103,3},{147,4},{180,5},{214,6},{241,7},{13,8}... | collective-permute-start | bytes 196616 | tf_op jit(solution)/shard_map/ppermute | solution.py:214
  74.0 6.8 %collective-permute-start.5 = (f32[32,512]{1,0:T(8,128)S(1)}, f32[32,512]{1,0:T(8,128)S(1)}, u32[]{:S(2)}, u32[]{:S(2)}) collective-permute-start(f32[32,512]{1,0:T(8,128)S(1)} %fusion.32), channel_id=1, source_target_pairs={{0,5},{1,34},{2,64},{3,103},{4,147},{5,180},{6,214},{7,241},{8,13}... | collective-permute-start | bytes 196616 | tf_op jit(solution)/shard_map/ppermute | solution.py:185
  78.2 40.0 %copy-start.4 = (f32[32,512]{1,0:T(8,128)}, f32[32,512]{1,0:T(8,128)S(1)}, u32[]{:S(2)}) copy-start(f32[32,512]{1,0:T(8,128)S(1)} %collective-permute-done.4.y_ref) | copy-start | bytes 196612
  82.8 1.4 collective-permute-start.6
  116.7 1.3 collective-permute-start.7
  119.2 7.8 %collective-permute-start.8 = (f32[32,704]{1,0:T(8,128)S(1)}, f32[32,704]{1,0:T(8,128)S(1)}, u32[]{:S(2)}, u32[]{:S(2)}) collective-permute-start(f32[32,704]{1,0:T(8,128)S(1)} %concatenate.20), channel_id=1, source_target_pairs={{5,0},{34,1},{64,2},{103,3},{147,4},{180,5},{214,6},{241,7},{13,8}... | collective-permute-start | bytes 270344 | tf_op jit(solution)/shard_map/ppermute | solution.py:218
  127.7 11.1 %all-to-all-start.5 = ((f32[8,32,192]{2,1,0:T(8,128)}), f32[8,32,192]{2,1,0:T(8,128)S(1)}, u32[]{:S(2)}, u32[]{:S(2)}) async-start(f32[8,32,192]{2,1,0:T(8,128)} %broadcast_in_dim.124), calls=%async_computation.5 | async-start | bytes 524288 | tf_op jit(solution)/shard_map/all_to_all | solution.py:222
  138.8 0.7 copy-start.2

commit v3 on v2

--- a/solution.py
+++ b/solution.py
@@ -92,7 +92,7 @@
 
 def finish(scale, grams_ref, x_ref, y_ref, z_ref, hist_ref, out_ref, g_ref, p_ref, v_ref):
     n = 32
-    part = jnp.sum(grams_ref[...], axis=0) * scale
+    part = grams_ref[...] * scale
     at = 0
     for i in range(3):
         for k in range(i + 1):
@@ -175,7 +175,8 @@
     every = NAMES
 
     def down(four):
-        return jnp.einsum("spk,skl->pl", four * weight, blocks, precision=BLOCKS)
+        left = jnp.concatenate([four[s] * weight[s] for s in range(slots)], axis=1)
+        return jnp.dot(left, blocks.reshape(slots * width, width), precision=BLOCKS)
 
     def across(own):
         product = jnp.einsum("pl,skl->spk", own, blocks, precision=BLOCKS) * weight
@@ -183,6 +184,7 @@
 
     def total(acrosses, downs):
         arrived = lax.ppermute(downs, every, to_row_group())
+        acrosses = lax.optimization_barrier(acrosses)
         part = acrosses + jnp.where(in_slot, arrived[None], 0.0)
         part = part.reshape(slots * vecs // 8, 8, width)
         low, high = part[..., :half], part[..., half:]
@@ -205,23 +207,28 @@
         return jnp.einsum("spk,sqk->pq", left, right, precision=FULL)
 
     moved = lax.ppermute(start_block, every, to_row_group())
-    x4 = lax.all_to_all(
-        jnp.broadcast_to(moved[None], (slots, vecs, width)), "z", 0, 0, tiled=True
-    )
-    x4 = jnp.where(far, jnp.roll(x4, 2, axis=0), x4)
+    near = lax.ppermute(moved, "z", [(0, 1), (1, 0), (2, 3), (3, 2)])
+    odd = lax.rem(z, 2) == 1
+    two = jnp.stack([jnp.where(odd, near, moved), jnp.where(odd, moved, near)])
+    over = lax.ppermute(two, "z", [(0, 2), (2, 0), (1, 3), (3, 1)])
+    upper = (z >= 2) != far
+    x4 = jnp.concatenate([jnp.where(upper, over, two), jnp.where(upper, two, over)])
     x = start_block
     y4 = total(across(x), down(x4))
     y = lax.ppermute(slot_of(y4), every, from_row_group())
-    xy4 = jnp.concatenate([x4, y4], axis=1)
-    z4 = total(across(y), down(y4))
-    grams = jnp.concatenate([inner(x4, x4), inner(y4, xy4), inner(z4, xy4), inner(z4, z4)], axis=1)
+    downs = down(y4)
+    acrosses, gx, gy = lax.optimization_barrier(
+        (across(y), inner(x4, x4), inner(y4, jnp.concatenate([x4, y4], axis=1)))
+    )
+    z4 = total(acrosses, downs)
+    gz = inner(z4, jnp.concatenate([x4, y4, z4], axis=1))
     back = lax.ppermute(
-        jnp.concatenate([slot_of(z4), grams], axis=1), every, from_row_group()
+        jnp.concatenate([slot_of(z4), gx, gy, gz], axis=1), every, from_row_group()
     )
     zz, grams = back[:, :width], back[:, width:]
-    grams = lax.all_to_all(
-        jnp.broadcast_to(grams[None], (8, *grams.shape)), ("x", "co"), 0, 0, tiled=True
-    )
+    grams = grams + lax.ppermute(grams, "co", [(0, 1), (1, 0)])
+    grams = grams + lax.ppermute(grams, "x", [(0, 1), (1, 0), (2, 3), (3, 2)])
+    grams = grams + lax.ppermute(grams, "x", [(0, 3), (3, 0), (1, 2), (2, 1)])
     return close(grams, x, y, zz, col_count * width)
 
 

time: 152 us -> 154 us (1.013)
  other arithmetic: 3.29 us -> 8.6 us
  starting transfers between devices: 21.4 us -> 17.9 us
  waiting for transfers between devices: 33.3 us -> 29.9 us
  blocking collectives: 64.2 us -> 66.5 us
  matrix products: 12.9 us -> 14.9 us
  local copies, waits for them, and re-layouts: 2.91 us -> 1.31 us
    all_to_all x2 -> x0, starting transfers between devices: 10.9 us -> none  [the longest x1 5.89 us: on_device(): lax.all_to_all(jnp.broadcast_to(moved[None], (slots, vecs, width)), 'z',...]
    all_to_all x2 -> x0, waiting for transfers between devices: 10.8 us -> none  [the longest x1 5.46 us: on_device(): lax.all_to_all(jnp.broadcast_to(grams[None], (8, *grams.shape)), ('x', 'c...]
    ppermute x1 -> x6, waiting for transfers between devices: 7.67 us -> 17.6 us  [the longest x1 7.67 us: on_device(): lax.ppermute(jnp.concatenate([slot_of(z4), gx, gy, gz], axis=1), every, f...]
    ppermute x1 -> x6, starting transfers between devices: 0.09 us -> 6.79 us  [the longest x1 3.36 us: on_device(): over = lax.ppermute(two, 'z', [(0, 2), (2, 0), (1, 3), (3, 1)])]
    mul x0 -> x2, other arithmetic: none -> 5.14 us  [down(): left = jnp.concatenate([four[s] * weight[s] for s in range(slots)], axis=1)]
    all_to_all x2, blocking collectives: 40.3 us -> 42.6 us  [total(): piece = lax.all_to_all(mine, ('z', 'x'), 0, 0, tiled=True).sum(axis=0)]
    dot_general x2, matrix products: 3.93 us -> 6.11 us  [across(): product = jnp.einsum('pl,skl->spk', own, blocks, precision=BLOCKS) * weight]
    ppermute x2, waiting for transfers between devices: 7.09 us -> 4.98 us  [total(): arrived = lax.ppermute(downs, every, to_row_group())]
  transfers between devices with their start and end apart: 11 -> 14, of which waited for: 10 -> 12; matrix products, arithmetic and copies ran while one was open for 5% -> 9% of each run, Pallas kernels for 0% -> 0%
where the time goes in v3:
time: 154 us; the launch traced here: 151 us
  blocking collectives  66.5 us (43%)
  waiting for transfers between devices  29.9 us (19%)
  starting transfers between devices  17.9 us (12%)
  matrix products  14.9 us (10%)
  Pallas kernels  10.7 us (7%)
  other arithmetic  8.6 us (6%)
  between operations  1.57 us (1%)
    all_to_all x2, blocking collectives, total(): piece = lax.all_to_all(mine, ('z', 'x'), 0, 0, tiled=True).sum(axis=0)  42.6 us
    all_to_all x2, blocking collectives, total(): lax.all_to_all(jnp.broadcast_to(piece[None], mine.shape), ('z', 'x'), 0,...  23.9 us
    pallas_call x1, Pallas kernels, close(): pl.pallas_call(functools.partial(finish, 1.0 / length), out_shape=(jax.Sh...  10.7 us
    ppermute x1, waiting for transfers between devices, on_device(): lax.ppermute(jnp.concatenate([slot_of(z4), gx, gy, gz], axis=1), every, f...  7.67 us
    dot_general x2, matrix products, down(): return jnp.dot(left, blocks.reshape(slots * width, width), precision=BLOCKS)  6.98 us
    ppermute x2, starting transfers between devices, total(): arrived = lax.ppermute(downs, every, to_row_group())  6.67 us
    dot_general x2, matrix products, across(): product = jnp.einsum('pl,skl->spk', own, blocks, precision=BLOCKS) * weight  6.11 us
    mul x2, other arithmetic, down(): left = jnp.concatenate([four[s] * weight[s] for s in range(slots)], axis=1)  5.14 us
  transfers between devices with their start and end apart: 14, of which 12 were waited for; matrix products, arithmetic and copies ran while one was open for 9% of the time, Pallas kernels for 0%

profile of v3, /device:TPU:2, one launch (start us, length us, event | category | flops | bytes accessed | tf_op | source)
XLA Modules:
  0.0 151.4 jit_solution(11198531126619243619)
XLA Ops:
  0.6 3.3 %collective-permute-start = (f32[32,512]{1,0:T(8,128)}, f32[32,512]{1,0:T(8,128)S(1)}, u32[]{:S(2)}, u32[]{:S(2)}) collective-permute-start(f32[32,512]{1,0:T(8,128)} %x_ref.1), channel_id=1, source_target_pairs={{0,5},{1,34},{2,64},{3,103},{4,147},{5,180},{6,214},{7,241},{8,13}... | collective-permute-start | bytes 196616 | tf_op jit(solution)/shard_map/ppermute | solution.py:209
  5.4 2.4 %collective-permute-done = f32[32,512]{1,0:T(8,128)S(1)} collective-permute-done((f32[32,512]{1,0:T(8,128)}, f32[32,512]{1,0:T(8,128)S(1)}, u32[]{:S(2)}, u32[]{:S(2)}) %collective-permute-start) | collective-permute-done | bytes 65568 | tf_op jit(solution)/shard_map/ppermute | solution.py:209
  7.9 1.9 %collective-permute-start.1 = (f32[32,512]{1,0:T(8,128)S(1)}, f32[32,512]{1,0:T(8,128)S(1)}, u32[]{:S(2)}, u32[]{:S(2)}) collective-permute-start(f32[32,512]{1,0:T(8,128)S(1)} %collective-permute-done), channel_id=1, source_target_pairs={{0,8},{8,0},{16,24},{24,16},{1,9},{9,1},{17,25},{25,17},{2,10},{10... | collective-permute-start | bytes 196616 | tf_op jit(solution)/shard_map/ppermute | solution.py:210
  9.8 4.1 %fusion.10 = f32[4,32,512]{2,1,0:T(8,128)S(1)} fusion(f32[4,1,512,512]{3,2,1,0:T(8,128)} %param.6, f32[32,512]{1,0:T(8,128)S(1)} %broadcast_multiply_fusion.1, f32[4]{0:T(128)S(1)} %compare_select_fusion.1, pred[4]{0:T(512)(128)(4,1)S(1)} %iota_compare_fusion, f32[32,512]{1,0:T(8,128)} %x_ref.1), kind=kOutput, calls=%fused_computation.6 | convolution fusion | flops 201523200 | bytes 4587540 | tf_op jit(solution)/shard_map/pl,skl->spk/dot_general | solution.py:182
  14.0 3.4 %collective-permute-start.2 = (f32[2,32,512]{2,1,0:T(8,128)S(1)}, f32[2,32,512]{2,1,0:T(8,128)S(1)}, u32[]{:S(2)}, u32[]{:S(2)}) collective-permute-start(f32[2,32,512]{2,1,0:T(8,128)S(1)} %pad_maximum_fusion.2), channel_id=1, source_target_pairs={{0,16},{16,0},{8,24},{24,8},{1,17},{17,1},{9,25},{25,9},{2,18},{18... | collective-permute-start | bytes 393224 | tf_op jit(solution)/shard_map/ppermute | solution.py:213
  19.2 2.9 %collective-permute-done.2 = f32[2,32,512]{2,1,0:T(8,128)S(1)} collective-permute-done((f32[2,32,512]{2,1,0:T(8,128)S(1)}, f32[2,32,512]{2,1,0:T(8,128)S(1)}, u32[]{:S(2)}, u32[]{:S(2)}) %collective-permute-start.2) | collective-permute-done | bytes 131104 | tf_op jit(solution)/shard_map/ppermute | solution.py:213
  22.2 2.6 %fusion.66 = (f32[32,512]{1,0:T(8,128)S(1)}, f32[32,512]{1,0:T(8,128)S(1)}, f32[32,512]{1,0:T(8,128)S(1)}, f32[32,512]{1,0:T(8,128)S(1)}) fusion(f32[2,32,512]{2,1,0:T(8,128)S(1)} %get-tuple-element.17, f32[]{:T(128)} %bitcast.9, f32[]{:T(128)} %bitcast.11, f32[]{:T(128)} %bitcast.7, f32[2,32,512]{2,1,0:T(8,128)S(1)} %get-tuple-element.16, f32[]{:T(128)} %bitcast.5), kind=kLoop, calls=%fused_computation.79 | loop fusion | flops 65536 | bytes 524304 | tf_op jit(solution)/shard_map/mul | solution.py:178
  24.8 3.5 %fusion.34 = f32[32,512]{1,0:T(8,128)S(1)} fusion(f32[2048,512]{1,0:T(8,128)} %bitcast.74, f32[32,512]{1,0:T(8,128)S(1)} %get-tuple-element.21, f32[32,512]{1,0:T(8,128)S(1)} %get-tuple-element.20, f32[32,512]{1,0:T(8,128)S(1)} %get-tuple-element.28, f32[32,512]{1,0:T(8,128)S(1)} %get-tuple-element.29), kind=kOutput, calls=%fused_computation.34 | convolution fusion | flops 201523200 | bytes 4521984 | tf_op jit(solution)/shard_map/dot_general | solution.py:179
  28.3 2.7 %collective-permute-start.3 = (f32[32,512]{1,0:T(8,128)S(1)}, f32[32,512]{1,0:T(8,128)S(1)}, u32[]{:S(2)}, u32[]{:S(2)}) collective-permute-start(f32[32,512]{1,0:T(8,128)S(1)} %fusion.34), channel_id=1, source_target_pairs={{0,5},{1,34},{2,64},{3,103},{4,147},{5,180},{6,214},{7,241},{8,13}... | collective-permute-start | bytes 196616 | tf_op jit(solution)/shard_map/ppermute | solution.py:186
  31.0 4.0 %collective-permute-done.3 = f32[32,512]{1,0:T(8,128)S(1)} collective-permute-done((f32[32,512]{1,0:T(8,128)S(1)}, f32[32,512]{1,0:T(8,128)S(1)}, u32[]{:S(2)}, u32[]{:S(2)}) %collective-permute-start.3) | collective-permute-done | bytes 65568 | tf_op jit(solution)/shard_map/ppermute | solution.py:186
  36.6 21.0 %all_to_all.20 = f32[16,8,256]{2,1,0:T(8,128)S(1)} all-to-all(f32[16,8,256]{2,1,0:T(8,128)S(1)} %select_add_fusion.3), channel_id=1, replica_groups=mesh['zh'=2,'y'=4,'z'=4,'x'=4,'co'=2] {'z','x'}, dimensions={0} | all-to-all | bytes 262144 | tf_op jit(solution)/shard_map/all_to_all | solution.py:194
  57.7 12.1 %all_to_all.21 = f32[16,8,256]{2,1,0:T(8,128)S(1)} all-to-all(f32[16,8,256]{2,1,0:T(8,128)S(1)} %broadcast_in_dim.107), channel_id=1, replica_groups=mesh['zh'=2,'y'=4,'z'=4,'x'=4,'co'=2] {'z','x'}, dimensions={0} | all-to-all | bytes 262144 | tf_op jit(solution)/shard_map/all_to_all | solution.py:195
  71.2 2.6 %fusion.55 = (f32[32,512]{1,0:T(8,128)S(1)}, f32[32,512]{1,0:T(8,128)S(1)}, f32[32,512]{1,0:T(8,128)S(1)}, f32[32,512]{1,0:T(8,128)S(1)}) fusion(f32[16,8,256]{2,1,0:T(8,128)S(1)} %get-tuple-element.14, f32[16,8,256]{2,1,0:T(8,128)S(1)} %get-tuple-element.15, f32[]{:T(128)} %bitcast.5, f32[]{:T(128)} %bitcast.7, f32[]{:T(128)} %bitcast.9, f32[]{:T(128)} %bitcast.11), kind=kLoop, calls=%fused_computation.66 | loop fusion | flops 131072 | bytes 524304 | tf_op jit(solution)/shard_map/mul | solution.py:178
  74.7 3.5 %fusion.45 = f32[32,512]{1,0:T(8,128)S(1)} fusion(f32[2048,512]{1,0:T(8,128)} %bitcast.75, f32[32,512]{1,0:T(8,128)S(1)} %get-tuple-element.13, f32[32,512]{1,0:T(8,128)S(1)} %get-tuple-element.12, f32[32,512]{1,0:T(8,128)S(1)} %get-tuple-element.11, f32[32,512]{1,0:T(8,128)S(1)} %get-tuple-element.10), kind=kOutput, calls=%fused_computation.45 | convolution fusion | flops 201523200 | bytes 4521984 | tf_op jit(solution)/shard_map/dot_general | solution.py:179
  78.8 3.9 %collective-permute-start.7 = (f32[32,512]{1,0:T(8,128)S(1)}, f32[32,512]{1,0:T(8,128)S(1)}, u32[]{:S(2)}, u32[]{:S(2)}) collective-permute-start(f32[32,512]{1,0:T(8,128)S(1)} %fusion.45), channel_id=1, source_target_pairs={{0,5},{1,34},{2,64},{3,103},{4,147},{5,180},{6,214},{7,241},{8,13}... | collective-permute-start | bytes 196616 | tf_op jit(solution)/shard_map/ppermute | solution.py:186
  82.7 2.0 %fusion.19 = f32[4,32,512]{2,1,0:T(8,128)S(1)} fusion(f32[4,1,512,512]{3,2,1,0:T(8,128)S(1)} %copy-done, f32[32,512]{1,0:T(8,128)S(1)} %broadcast_multiply_fusion, f32[4]{0:T(128)S(1)} %compare_select_fusion.1, pred[4]{0:T(512)(128)(4,1)S(1)} %iota_compare_fusion, f32[32,512]{1,0:T(8,128)S(1)} %collective-permute-done.6.y_ref), kind=kOutput, calls=%fused_computation.9 | convolution fusion | flops 201523200 | bytes 4587540 | tf_op jit(solution)/shard_map/pl,skl->spk/dot_general | solution.py:182
  85.9 1.3 collective-permute-done.8
  87.3 21.5 %all_to_all.22 = f32[16,8,256]{2,1,0:T(8,128)S(1)} all-to-all(f32[16,8,256]{2,1,0:T(8,128)S(1)} %select_add_fusion.2), channel_id=1, replica_groups=mesh['zh'=2,'y'=4,'z'=4,'x'=4,'co'=2] {'z','x'}, dimensions={0} | all-to-all | bytes 262144 | tf_op jit(solution)/shard_map/all_to_all | solution.py:194
  108.8 11.8 %all_to_all.23 = f32[16,8,256]{2,1,0:T(8,128)S(1)} all-to-all(f32[16,8,256]{2,1,0:T(8,128)S(1)} %broadcast_in_dim.110), channel_id=1, replica_groups=mesh['zh'=2,'y'=4,'z'=4,'x'=4,'co'=2] {'z','x'}, dimensions={0} | all-to-all | bytes 262144 | tf_op jit(solution)/shard_map/all_to_all | solution.py:195
  120.7 1.3 collective-permute-done.9
  123.3 7.7 %collective-permute-done.10 = f32[32,704]{1,0:T(8,128)S(1)} collective-permute-done((f32[32,704]{1,0:T(8,128)S(1)}, f32[32,704]{1,0:T(8,128)S(1)}, u32[]{:S(2)}, u32[]{:S(2)}) %collective-permute-start.10) | collective-permute-done | bytes 90144 | tf_op jit(solution)/shard_map/ppermute | solution.py:225
  132.2 3.9 %collective-permute-done.12 = f32[32,192]{1,0:T(8,128)S(1)} collective-permute-done((f32[32,192]{1,0:T(8,128)S(1)}, f32[32,192]{1,0:T(8,128)S(1)}, u32[]{:S(2)}, u32[]{:S(2)}) %collective-permute-start.12) | collective-permute-done | bytes 24608 | tf_op jit(solution)/shard_map/ppermute | solution.py:230
  137.9 2.1 %collective-permute-done.13 = f32[32,192]{1,0:T(8,128)S(1)} collective-permute-done((f32[32,192]{1,0:T(8,128)S(1)}, f32[32,192]{1,0:T(8,128)S(1)}, u32[]{:S(2)}, u32[]{:S(2)}) %collective-permute-start.13) | collective-permute-done | bytes 24608 | tf_op jit(solution)/shard_map/ppermute | solution.py:231
  140.6 10.7 %recurrence.1 = (f32[2,2,32,32]{3,2,1,0:T(8,128)}, f32[32,512]{1,0:T(8,128)}) custom-call(f32[32,192]{1,0:T(8,128)} %add.75.grams_ref, f32[32,512]{1,0:T(8,128)} %x_ref.1, f32[32,512]{1,0:T(8,128)} %copy-done.1, f32[32,512]{1,0:T(8,128)} %slice.101.z_ref), custom_call_target="tpu_custom_call" | custom-call | tf_op jit(solution)/shard_map/recurrence/pallas_call | solution.py:139
  (57 shorter events, 13.4 us)
Async XLA Ops:
  0.6 16.7 %copy-start.2 = (f32[8,8]{1,0:T(8,128)S(1)}, f32[8,8]{1,0:T(8,128)}, u32[]{:S(2)}) copy-start(f32[8,8]{1,0:T(8,128)} %constant.55.clone) | copy-start | bytes 772
  0.6 7.2 %collective-permute-start = (f32[32,512]{1,0:T(8,128)}, f32[32,512]{1,0:T(8,128)S(1)}, u32[]{:S(2)}, u32[]{:S(2)}) collective-permute-start(f32[32,512]{1,0:T(8,128)} %x_ref.1), channel_id=1, source_target_pairs={{0,5},{1,34},{2,64},{3,103},{4,147},{5,180},{6,214},{7,241},{8,13}... | collective-permute-start | bytes 196616 | tf_op jit(solution)/shard_map/ppermute | solution.py:209
  7.9 6.1 %collective-permute-start.1 = (f32[32,512]{1,0:T(8,128)S(1)}, f32[32,512]{1,0:T(8,128)S(1)}, u32[]{:S(2)}, u32[]{:S(2)}) collective-permute-start(f32[32,512]{1,0:T(8,128)S(1)} %collective-permute-done), channel_id=1, source_target_pairs={{0,8},{8,0},{16,24},{24,16},{1,9},{9,1},{17,25},{25,17},{2,10},{10... | collective-permute-start | bytes 196616 | tf_op jit(solution)/shard_map/ppermute | solution.py:210
  14.0 8.2 %collective-permute-start.2 = (f32[2,32,512]{2,1,0:T(8,128)S(1)}, f32[2,32,512]{2,1,0:T(8,128)S(1)}, u32[]{:S(2)}, u32[]{:S(2)}) collective-permute-start(f32[2,32,512]{2,1,0:T(8,128)S(1)} %pad_maximum_fusion.2), channel_id=1, source_target_pairs={{0,16},{16,0},{8,24},{24,8},{1,17},{17,1},{9,25},{25,9},{2,18},{18... | collective-permute-start | bytes 393224 | tf_op jit(solution)/shard_map/ppermute | solution.py:213
  28.3 6.8 %collective-permute-start.3 = (f32[32,512]{1,0:T(8,128)S(1)}, f32[32,512]{1,0:T(8,128)S(1)}, u32[]{:S(2)}, u32[]{:S(2)}) collective-permute-start(f32[32,512]{1,0:T(8,128)S(1)} %fusion.34), channel_id=1, source_target_pairs={{0,5},{1,34},{2,64},{3,103},{4,147},{5,180},{6,214},{7,241},{8,13}... | collective-permute-start | bytes 196616 | tf_op jit(solution)/shard_map/ppermute | solution.py:186
  35.2 1.4 collective-permute-start.4
  57.7 25.0 %copy-start = (f32[4,1,512,512]{3,2,1,0:T(8,128)S(1)}, f32[4,1,512,512]{3,2,1,0:T(8,128)}, u32[]{:S(2)}) copy-start(f32[4,1,512,512]{3,2,1,0:T(8,128)} %param.6) | copy-start | bytes 12582916
  69.8 1.3 collective-permute-start.5
  73.9 8.8 %collective-permute-start.6 = (f32[32,512]{1,0:T(8,128)S(1)}, f32[32,512]{1,0:T(8,128)S(1)}, u32[]{:S(2)}, u32[]{:S(2)}) collective-permute-start(f32[32,512]{1,0:T(8,128)S(1)} %select_reduce_fusion.1), channel_id=1, source_target_pairs={{5,0},{34,1},{64,2},{103,3},{147,4},{180,5},{214,6},{241,7},{13,8}... | collective-permute-start | bytes 196616 | tf_op jit(solution)/shard_map/ppermute | solution.py:218
  78.8 6.9 %collective-permute-start.7 = (f32[32,512]{1,0:T(8,128)S(1)}, f32[32,512]{1,0:T(8,128)S(1)}, u32[]{:S(2)}, u32[]{:S(2)}) collective-permute-start(f32[32,512]{1,0:T(8,128)S(1)} %fusion.45), channel_id=1, source_target_pairs={{0,5},{1,34},{2,64},{3,103},{4,147},{5,180},{6,214},{7,241},{8,13}... | collective-permute-start | bytes 196616 | tf_op jit(solution)/shard_map/ppermute | solution.py:186
  82.7 40.3 %copy-start.1 = (f32[32,512]{1,0:T(8,128)}, f32[32,512]{1,0:T(8,128)S(1)}, u32[]{:S(2)}) copy-start(f32[32,512]{1,0:T(8,128)S(1)} %collective-permute-done.6.y_ref) | copy-start | bytes 196612
  85.8 1.4 collective-permute-start.8
  120.7 1.3 collective-permute-start.9
  123.2 7.8 %collective-permute-start.10 = (f32[32,704]{1,0:T(8,128)S(1)}, f32[32,704]{1,0:T(8,128)S(1)}, u32[]{:S(2)}, u32[]{:S(2)}) collective-permute-start(f32[32,704]{1,0:T(8,128)S(1)} %pad_maximum_fusion.3), channel_id=1, source_target_pairs={{5,0},{34,1},{64,2},{103,3},{147,4},{180,5},{214,6},{241,7},{13,8}... | collective-permute-start | bytes 270344 | tf_op jit(solution)/shard_map/ppermute | solution.py:225
  130.9 1.2 collective-permute-start.11
  132.2 3.9 %collective-permute-start.12 = (f32[32,192]{1,0:T(8,128)S(1)}, f32[32,192]{1,0:T(8,128)S(1)}, u32[]{:S(2)}, u32[]{:S(2)}) collective-permute-start(f32[32,192]{1,0:T(8,128)S(1)} %slice_add_fusion), channel_id=1, source_target_pairs={{0,2},{2,0},{4,6},{6,4},{1,3},{3,1},{5,7},{7,5},{8,10},{10,8},{12,... | collective-permute-start | bytes 73736 | tf_op jit(solution)/shard_map/ppermute | solution.py:230
  136.1 3.9 %collective-permute-start.13 = (f32[32,192]{1,0:T(8,128)S(1)}, f32[32,192]{1,0:T(8,128)S(1)}, u32[]{:S(2)}, u32[]{:S(2)}) collective-permute-start(f32[32,192]{1,0:T(8,128)S(1)} %add.74), channel_id=1, source_target_pairs={{0,6},{6,0},{2,4},{4,2},{1,7},{7,1},{3,5},{5,3},{8,14},{14,8},{10,... | collective-permute-start | bytes 73736 | tf_op jit(solution)/shard_map/ppermute | solution.py:231

commit v4 on v3

--- a/solution.py
+++ b/solution.py
@@ -134,6 +134,94 @@
     out_ref[...] = mm(t2, mm(w1, v_ref[...]))
 
 
+def parts_of(v):
+    high = v.astype(jnp.bfloat16)
+    return high, (v - high.astype(jnp.float32)).astype(jnp.bfloat16)
+
+
+def split_blocks(weight_ref, blocks_ref, high_ref, low_ref, held, arrived):
+    slots, width = blocks_ref.shape[0], blocks_ref.shape[1]
+    copies = [
+        pltpu.make_async_copy(blocks_ref.at[s], held.at[s], arrived.at[s]) for s in range(slots)
+    ]
+    for copy in copies:
+        copy.start()
+    for s in range(slots):
+        copies[s].wait()
+        rows = pl.ds(s * width, width)
+        high_ref[rows, :], low_ref[rows, :] = parts_of(held[s] * weight_ref[s])
+
+
+def dot3(left, high, low, contract):
+    rows = left[0].shape[0]
+    dims = (((1,), (contract,)), ((), ()))
+    both = lax.dot_general(
+        jnp.concatenate(left, axis=0), high, dims, preferred_element_type=jnp.float32
+    )
+    rest = lax.dot_general(left[0], low, dims, preferred_element_type=jnp.float32)
+    return both[:rows] + (both[rows:] + rest)
+
+
+def down_kernel(four_ref, high_ref, low_ref, out_ref):
+    slots, _, width = four_ref.shape
+    total = None
+    for s in range(slots):
+        rows = pl.ds(s * width, width)
+        term = dot3(parts_of(four_ref[s]), high_ref[rows, :], low_ref[rows, :], 0)
+        total = term if total is None else total + term
+    out_ref[...] = total
+
+
+def across_kernel(lead_ref, own_ref, high_ref, low_ref, out_ref):
+    slots, _, width = out_ref.shape
+    left = parts_of(own_ref[...])
+    for s in range(slots):
+        rows = pl.ds(s * width, width)
+        term = dot3(left, high_ref[rows, :], low_ref[rows, :], 1)
+        out_ref[s] = term + lead_ref[pl.ds(s, 1), :] * own_ref[...]
+
+
+def gram_kernel(*refs):
+    *four_refs, out_ref, flat_ref = refs
+    slots, vecs, width = four_refs[0].shape
+    for i, four_ref in enumerate(four_refs):
+        for s in range(slots):
+            flat_ref[i * vecs : (i + 1) * vecs, s * width : (s + 1) * width] = four_ref[s]
+    out_ref[...] = mmt(flat_ref[(len(four_refs) - 1) * vecs :, :], flat_ref[...])
+
+
+LIMIT = pltpu.CompilerParams(vmem_limit_bytes=16 * 2**20)
+IN_VMEM = pl.BlockSpec(memory_space=pltpu.VMEM)
+
+
+def grams_of(*fours):
+    slots, vecs, width = fours[0].shape
+    return pl.pallas_call(
+        gram_kernel,
+        in_specs=[IN_VMEM] * len(fours),
+        out_specs=IN_VMEM,
+        out_shape=pltpu.VMEM((vecs, len(fours) * vecs), jnp.float32),
+        scratch_shapes=[pltpu.VMEM((len(fours) * vecs, slots * width), jnp.float32)],
+        compiler_params=LIMIT,
+        name="gram",
+    )(*fours)
+
+
+def spread_kernel(parts_ref, out_ref):
+    out_ref[...] = jnp.broadcast_to(jnp.sum(parts_ref[...], axis=0)[None], out_ref.shape)
+
+
+def sum_spread(parts):
+    return pl.pallas_call(
+        spread_kernel,
+        in_specs=[IN_VMEM],
+        out_specs=IN_VMEM,
+        out_shape=pltpu.VMEM(parts.shape, jnp.float32),
+        compiler_params=LIMIT,
+        name="sum_spread",
+    )(parts)
+
+
 def close(grams, x, y, z, length):
     vecs = x.shape[0]
     return pl.pallas_call(
@@ -147,6 +235,7 @@
             pltpu.VMEM((vecs, 3 * vecs), jnp.float32),
             pltpu.VMEM((3 * vecs, x.shape[1]), jnp.float32),
         ],
+        compiler_params=LIMIT,
         name="recurrence",
     )(grams, x, y, z)
 
@@ -165,22 +254,47 @@
     block_rows = row + 8 * jnp.arange(slots, dtype=jnp.int32)
     weight = jnp.where(block_rows < col, 1.0, jnp.where(block_rows == col, 0.5, 0.0)).astype(
         jnp.float32
-    )[:, None, None]
-    lead = jnp.where(place == row, energies - SHIFT, 0.0)
-    own_slot = (jnp.arange(slots) == z)[:, None, None]
+    )
+    own_slot = (jnp.arange(slots) == z) & (place == row)
+    lead = jnp.where(own_slot[:, None], (energies - SHIFT)[None, :], 0.0)
     table = jnp.array(far_table(), jnp.float32).reshape(-1)
     far = jnp.sum(table * (jnp.arange(64) == row * 8 + place).astype(jnp.float32)) > 0.5
     slot = jnp.where(far, (z + 2) % 4, z)
     in_slot = (jnp.arange(slots) == slot)[:, None, None]
     every = NAMES
 
+    high, low = pl.pallas_call(
+        split_blocks,
+        in_specs=[pl.BlockSpec(memory_space=pltpu.SMEM), pl.BlockSpec(memory_space=pl.ANY)],
+        out_specs=(IN_VMEM, IN_VMEM),
+        out_shape=(pltpu.VMEM((slots * width, width), jnp.bfloat16),) * 2,
+        scratch_shapes=[
+            pltpu.VMEM(blocks.shape, jnp.float32),
+            pltpu.SemaphoreType.DMA((slots,)),
+        ],
+        compiler_params=LIMIT,
+        name="split_blocks",
+    )(weight, blocks)
+
     def down(four):
-        left = jnp.concatenate([four[s] * weight[s] for s in range(slots)], axis=1)
-        return jnp.dot(left, blocks.reshape(slots * width, width), precision=BLOCKS)
+        return pl.pallas_call(
+            down_kernel,
+            in_specs=[IN_VMEM] * 3,
+            out_specs=IN_VMEM,
+            out_shape=pltpu.VMEM((vecs, width), jnp.float32),
+            compiler_params=LIMIT,
+            name="down",
+        )(four, high, low)
 
     def across(own):
-        product = jnp.einsum("pl,skl->spk", own, blocks, precision=BLOCKS) * weight
-        return product + jnp.where(own_slot, (lead[None, :] * own)[None], 0.0)
+        return pl.pallas_call(
+            across_kernel,
+            in_specs=[IN_VMEM] * 4,
+            out_specs=IN_VMEM,
+            out_shape=pltpu.VMEM((slots, vecs, width), jnp.float32),
+            compiler_params=LIMIT,
+            name="across",
+        )(lead, own, high, low)
 
     def total(acrosses, downs):
         arrived = lax.ppermute(downs, every, to_row_group())
@@ -191,10 +305,8 @@
         mine = jnp.where(core == 0, low, high)
         other = jnp.where(core == 0, high, low)
         mine = mine + lax.ppermute(other, "co", [(0, 1), (1, 0)])
-        piece = lax.all_to_all(mine, ("z", "x"), 0, 0, tiled=True).sum(axis=0)
-        whole = lax.all_to_all(
-            jnp.broadcast_to(piece[None], mine.shape), ("z", "x"), 0, 0, tiled=True
-        )
+        pieces = lax.all_to_all(mine, ("z", "x"), 0, 0, tiled=True)
+        whole = lax.all_to_all(sum_spread(pieces), ("z", "x"), 0, 0, tiled=True)
         facing = lax.ppermute(whole, "co", [(0, 1), (1, 0)])
         low = jnp.where(core == 0, whole, facing)
         high = jnp.where(core == 0, facing, whole)
@@ -202,9 +314,6 @@
 
     def slot_of(four):
         return jnp.sum(jnp.where(in_slot, four, 0.0), axis=0)
-
-    def inner(left, right):
-        return jnp.einsum("spk,sqk->pq", left, right, precision=FULL)
 
     moved = lax.ppermute(start_block, every, to_row_group())
     near = lax.ppermute(moved, "z", [(0, 1), (1, 0), (2, 3), (3, 2)])
@@ -218,10 +327,10 @@
     y = lax.ppermute(slot_of(y4), every, from_row_group())
     downs = down(y4)
     acrosses, gx, gy = lax.optimization_barrier(
-        (across(y), inner(x4, x4), inner(y4, jnp.concatenate([x4, y4], axis=1)))
+        (across(y), grams_of(x4), grams_of(x4, y4))
     )
     z4 = total(acrosses, downs)
-    gz = inner(z4, jnp.concatenate([x4, y4, z4], axis=1))
+    gz = grams_of(x4, y4, z4)
     back = lax.ppermute(
         jnp.concatenate([slot_of(z4), gx, gy, gz], axis=1), every, from_row_group()
     )

time: 154 us -> 138 us (0.90)
  matrix products: 14.9 us -> 0 us
  Pallas kernels: 10.7 us -> 17.4 us
  blocking collectives: 66.5 us -> 60.6 us
  other arithmetic: 8.6 us -> 2.78 us
  waiting for transfers between devices: 29.9 us -> 35.5 us
  starting transfers between devices: 17.9 us -> 16 us
    dot_general x7 -> x0, matrix products: 14.9 us -> none  [the longest x2 6.98 us: down(): return jnp.dot(left, blocks.reshape(slots * width, width), precision=BLOCKS)]
    pallas_call x0 -> x10, Pallas kernels: none -> 7.6 us  [the longest x2 2.66 us: across(): pl.pallas_call(across_kernel, in_specs=[IN_VMEM] * 4, out_specs=IN_VMEM,...]
    mul x4 -> x0, other arithmetic: 5.99 us -> none  [the longest x2 5.14 us: down(): left = jnp.concatenate([four[s] * weight[s] for s in range(slots)], axis=1)]
    all_to_all x4, blocking collectives: 66.5 us -> 60.6 us  [the longest x2 36.9 us: total(): pieces = lax.all_to_all(mine, ('z', 'x'), 0, 0, tiled=True)]
    ppermute x1, waiting for transfers between devices: 0.01 us -> 2.87 us  [on_device(): near = lax.ppermute(moved, 'z', [(0, 1), (1, 0), (2, 3), (3, 2)])]
    ppermute x1, waiting for transfers between devices: 2.43 us -> 0.01 us  [on_device(): moved = lax.ppermute(start_block, every, to_row_group())]
    ppermute x1, waiting for transfers between devices: 2.95 us -> 5.18 us  [on_device(): over = lax.ppermute(two, 'z', [(0, 2), (2, 0), (1, 3), (3, 1)])]
    unnamed x6 -> x4, local copies, waits for them, and re-layouts: 0.02 us -> 2.19 us
  transfers between devices with their start and end apart: 14 -> 14, of which waited for: 12 -> 12; matrix products, arithmetic and copies ran while one was open for 9% -> 2% of each run, Pallas kernels for 0% -> 4%
where the time goes in v4:
time: 138 us; the launch traced here: 136 us
  blocking collectives  60.6 us (44%)
  waiting for transfers between devices  35.5 us (26%)
  Pallas kernels  17.4 us (13%)
  starting transfers between devices  16 us (12%)
  other arithmetic  2.78 us (2%)
  local copies, waits for them, and re-layouts  2.2 us (2%)
  between operations  1.48 us (1%)
    all_to_all x2, blocking collectives, total(): pieces = lax.all_to_all(mine, ('z', 'x'), 0, 0, tiled=True)  36.9 us
    all_to_all x2, blocking collectives, total(): whole = lax.all_to_all(sum_spread(pieces), ('z', 'x'), 0, 0, tiled=True)  23.7 us
    pallas_call x1, Pallas kernels, close(): pl.pallas_call(functools.partial(finish, 1.0 / length), out_shape=(jax.Sh...  9.83 us
    ppermute x1, waiting for transfers between devices, on_device(): lax.ppermute(jnp.concatenate([slot_of(z4), gx, gy, gz], axis=1), every, f...  7.67 us
    ppermute x2, waiting for transfers between devices, total(): arrived = lax.ppermute(downs, every, to_row_group())  5.54 us
    ppermute x1, waiting for transfers between devices, on_device(): over = lax.ppermute(two, 'z', [(0, 2), (2, 0), (1, 3), (3, 1)])  5.18 us
    ppermute x2, starting transfers between devices, total(): arrived = lax.ppermute(downs, every, to_row_group())  5.11 us
    ppermute x1, waiting for transfers between devices, on_device(): grams = grams + lax.ppermute(grams, 'x', [(0, 1), (1, 0), (2, 3), (3, 2)])  3.91 us
  transfers between devices with their start and end apart: 14, of which 12 were waited for; matrix products, arithmetic and copies ran while one was open for 2% of the time, Pallas kernels for 4%

profile of v4, /device:TPU:2, one launch (start us, length us, event | category | flops | bytes accessed | tf_op | source)
XLA Modules:
  0.0 136.0 jit_solution(634153729862222923)
XLA Ops:
  0.6 3.3 %collective-permute-start = (f32[32,512]{1,0:T(8,128)}, f32[32,512]{1,0:T(8,128)S(1)}, u32[]{:S(2)}, u32[]{:S(2)}) collective-permute-start(f32[32,512]{1,0:T(8,128)} %x_ref.1), channel_id=1, source_target_pairs={{0,5},{1,34},{2,64},{3,103},{4,147},{5,180},{6,214},{7,241},{8,13}... | collective-permute-start | bytes 196616 | tf_op jit(solution)/shard_map/ppermute | solution.py:318
  6.5 2.2 %copy-done = f32[4,1,512,512]{3,2,1,0:T(8,128)S(1)} copy-done((f32[4,1,512,512]{3,2,1,0:T(8,128)S(1)}, f32[4,1,512,512]{3,2,1,0:T(8,128)}, u32[]{:S(2)}) %copy-start) | copy-done | bytes 4194328
  8.7 1.7 %split_blocks.1 = (bf16[2048,512]{1,0:T(8,128)(2,1)S(1)}, bf16[2048,512]{1,0:T(8,128)(2,1)S(1)}) custom-call(f32[4]{0:T(128)S(1)} %compare_select_fusion.1.weight_ref, f32[4,512,512]{2,1,0:T(8,128)S(1)} %bitcast.17), custom_call_target="tpu_custom_call" | custom-call | tf_op jit(solution)/shard_map/split_blocks/pallas_call | solution.py:266
  10.4 2.0 %collective-permute-start.1 = (f32[32,512]{1,0:T(8,128)S(1)}, f32[32,512]{1,0:T(8,128)S(1)}, u32[]{:S(2)}, u32[]{:S(2)}) collective-permute-start(f32[32,512]{1,0:T(8,128)S(1)} %collective-permute-done), channel_id=1, source_target_pairs={{0,8},{8,0},{16,24},{24,16},{1,9},{9,1},{17,25},{25,17},{2,10},{10... | collective-permute-start | bytes 196616 | tf_op jit(solution)/shard_map/ppermute | solution.py:319
  12.4 2.9 %collective-permute-done.1 = f32[32,512]{1,0:T(8,128)S(1)} collective-permute-done((f32[32,512]{1,0:T(8,128)S(1)}, f32[32,512]{1,0:T(8,128)S(1)}, u32[]{:S(2)}, u32[]{:S(2)}) %collective-permute-start.1) | collective-permute-done | bytes 65568 | tf_op jit(solution)/shard_map/ppermute | solution.py:319
  15.3 3.4 %collective-permute-start.2 = (f32[2,32,512]{2,1,0:T(8,128)S(1)}, f32[2,32,512]{2,1,0:T(8,128)S(1)}, u32[]{:S(2)}, u32[]{:S(2)}) collective-permute-start(f32[2,32,512]{2,1,0:T(8,128)S(1)} %pad_maximum_fusion.3), channel_id=1, source_target_pairs={{0,16},{16,0},{8,24},{24,8},{1,17},{17,1},{9,25},{25,9},{2,18},{18... | collective-permute-start | bytes 393224 | tf_op jit(solution)/shard_map/ppermute | solution.py:322
  18.7 1.3 across.2
  20.1 5.2 %collective-permute-done.2 = f32[2,32,512]{2,1,0:T(8,128)S(1)} collective-permute-done((f32[2,32,512]{2,1,0:T(8,128)S(1)}, f32[2,32,512]{2,1,0:T(8,128)S(1)}, u32[]{:S(2)}, u32[]{:S(2)}) %collective-permute-start.2) | collective-permute-done | bytes 131104 | tf_op jit(solution)/shard_map/ppermute | solution.py:322
  27.3 5.5 %collective-permute-done.3 = f32[32,512]{1,0:T(8,128)S(1)} collective-permute-done((f32[32,512]{1,0:T(8,128)S(1)}, f32[32,512]{1,0:T(8,128)S(1)}, u32[]{:S(2)}, u32[]{:S(2)}) %collective-permute-start.3) | collective-permute-done | bytes 65568 | tf_op jit(solution)/shard_map/ppermute | solution.py:300
  33.0 1.3 collective-permute-done.4
  34.4 19.9 %all_to_all.20.parts_ref = f32[16,8,256]{2,1,0:T(8,128)S(1)} all-to-all(f32[16,8,256]{2,1,0:T(8,128)S(1)} %select_add_fusion.3), channel_id=1, replica_groups=mesh['zh'=2,'y'=4,'z'=4,'x'=4,'co'=2] {'z','x'}, dimensions={0} | all-to-all | bytes 262144 | tf_op jit(solution)/shard_map/all_to_all | solution.py:308
  54.3 11.8 %all_to_all.21 = f32[16,8,256]{2,1,0:T(8,128)S(1)} all-to-all(f32[16,8,256]{2,1,0:T(8,128)S(1)} %sum_spread.2), channel_id=1, replica_groups=mesh['zh'=2,'y'=4,'z'=4,'x'=4,'co'=2] {'z','x'}, dimensions={0} | all-to-all | bytes 262144 | tf_op jit(solution)/shard_map/all_to_all | solution.py:309
  66.1 1.3 collective-permute-done.5
  69.0 3.9 %collective-permute-start.7 = (f32[32,512]{1,0:T(8,128)S(1)}, f32[32,512]{1,0:T(8,128)S(1)}, u32[]{:S(2)}, u32[]{:S(2)}) collective-permute-start(f32[32,512]{1,0:T(8,128)S(1)} %down.3), channel_id=1, source_target_pairs={{0,5},{1,34},{2,64},{3,103},{4,147},{5,180},{6,214},{7,241},{8,13}... | collective-permute-start | bytes 196616 | tf_op jit(solution)/shard_map/ppermute | solution.py:300
  73.8 1.3 collective-permute-done.6.own_ref.y_ref
  75.2 1.3 across.3
  76.7 1.3 collective-permute-done.8
  78.1 17.0 %all_to_all.22.parts_ref = f32[16,8,256]{2,1,0:T(8,128)S(1)} all-to-all(f32[16,8,256]{2,1,0:T(8,128)S(1)} %select_add_fusion.2), channel_id=1, replica_groups=mesh['zh'=2,'y'=4,'z'=4,'x'=4,'co'=2] {'z','x'}, dimensions={0} | all-to-all | bytes 262144 | tf_op jit(solution)/shard_map/all_to_all | solution.py:308
  95.2 11.8 %all_to_all.23 = f32[16,8,256]{2,1,0:T(8,128)S(1)} all-to-all(f32[16,8,256]{2,1,0:T(8,128)S(1)} %sum_spread.3), channel_id=1, replica_groups=mesh['zh'=2,'y'=4,'z'=4,'x'=4,'co'=2] {'z','x'}, dimensions={0} | all-to-all | bytes 262144 | tf_op jit(solution)/shard_map/all_to_all | solution.py:309
  107.0 1.3 collective-permute-done.9
  109.4 7.7 %collective-permute-done.10 = f32[32,704]{1,0:T(8,128)S(1)} collective-permute-done((f32[32,704]{1,0:T(8,128)S(1)}, f32[32,704]{1,0:T(8,128)S(1)}, u32[]{:S(2)}, u32[]{:S(2)}) %collective-permute-start.10) | collective-permute-done | bytes 90144 | tf_op jit(solution)/shard_map/ppermute | solution.py:334
  118.3 3.9 %collective-permute-done.12 = f32[32,192]{1,0:T(8,128)S(1)} collective-permute-done((f32[32,192]{1,0:T(8,128)S(1)}, f32[32,192]{1,0:T(8,128)S(1)}, u32[]{:S(2)}, u32[]{:S(2)}) %collective-permute-start.12) | collective-permute-done | bytes 24608 | tf_op jit(solution)/shard_map/ppermute | solution.py:339
  123.5 2.7 %collective-permute-done.13 = f32[32,192]{1,0:T(8,128)S(1)} collective-permute-done((f32[32,192]{1,0:T(8,128)S(1)}, f32[32,192]{1,0:T(8,128)S(1)}, u32[]{:S(2)}, u32[]{:S(2)}) %collective-permute-start.13) | collective-permute-done | bytes 24608 | tf_op jit(solution)/shard_map/ppermute | solution.py:340
  126.2 9.8 %recurrence.1 = (f32[2,2,32,32]{3,2,1,0:T(8,128)}, f32[32,512]{1,0:T(8,128)}) custom-call(f32[32,192]{1,0:T(8,128)S(1)} %add.63.grams_ref, f32[32,512]{1,0:T(8,128)S(1)} %copy-done.1, f32[32,512]{1,0:T(8,128)S(1)} %collective-permute-done.6.own_ref.y_ref, f32[32,512]{1,0:T(8,128)S(1)} %slice.29.z_ref), custom_call_target="tpu_custom_call" | custom-call | tf_op jit(solution)/shard_map/recurrence/pallas_call | solution.py:227
  (51 shorter events, 10.6 us)
Async XLA Ops:
  0.6 9.8 %collective-permute-start = (f32[32,512]{1,0:T(8,128)}, f32[32,512]{1,0:T(8,128)S(1)}, u32[]{:S(2)}, u32[]{:S(2)}) collective-permute-start(f32[32,512]{1,0:T(8,128)} %x_ref.1), channel_id=1, source_target_pairs={{0,5},{1,34},{2,64},{3,103},{4,147},{5,180},{6,214},{7,241},{8,13}... | collective-permute-start | bytes 196616 | tf_op jit(solution)/shard_map/ppermute | solution.py:318
  6.5 2.2 %copy-start = (f32[4,1,512,512]{3,2,1,0:T(8,128)S(1)}, f32[4,1,512,512]{3,2,1,0:T(8,128)}, u32[]{:S(2)}) copy-start(f32[4,1,512,512]{3,2,1,0:T(8,128)} %param.6) | copy-start | bytes 12582916
  8.7 10.0 %copy-start.1 = (f32[32,512]{1,0:T(8,128)S(1)}, f32[32,512]{1,0:T(8,128)}, u32[]{:S(2)}) copy-start(f32[32,512]{1,0:T(8,128)} %x_ref.1) | copy-start | bytes 196612
  10.4 4.9 %collective-permute-start.1 = (f32[32,512]{1,0:T(8,128)S(1)}, f32[32,512]{1,0:T(8,128)S(1)}, u32[]{:S(2)}, u32[]{:S(2)}) collective-permute-start(f32[32,512]{1,0:T(8,128)S(1)} %collective-permute-done), channel_id=1, source_target_pairs={{0,8},{8,0},{16,24},{24,16},{1,9},{9,1},{17,25},{25,17},{2,10},{10... | collective-permute-start | bytes 196616 | tf_op jit(solution)/shard_map/ppermute | solution.py:319
  15.3 9.9 %collective-permute-start.2 = (f32[2,32,512]{2,1,0:T(8,128)S(1)}, f32[2,32,512]{2,1,0:T(8,128)S(1)}, u32[]{:S(2)}, u32[]{:S(2)}) collective-permute-start(f32[2,32,512]{2,1,0:T(8,128)S(1)} %pad_maximum_fusion.3), channel_id=1, source_target_pairs={{0,16},{16,0},{8,24},{24,8},{1,17},{17,1},{9,25},{25,9},{2,18},{18... | collective-permute-start | bytes 393224 | tf_op jit(solution)/shard_map/ppermute | solution.py:322
  26.1 6.7 %collective-permute-start.3 = (f32[32,512]{1,0:T(8,128)S(1)}, f32[32,512]{1,0:T(8,128)S(1)}, u32[]{:S(2)}, u32[]{:S(2)}) collective-permute-start(f32[32,512]{1,0:T(8,128)S(1)} %down.2), channel_id=1, source_target_pairs={{0,5},{1,34},{2,64},{3,103},{4,147},{5,180},{6,214},{7,241},{8,13}... | collective-permute-start | bytes 196616 | tf_op jit(solution)/shard_map/ppermute | solution.py:300
  32.9 1.4 %collective-permute-start.4 = (f32[16,8,256]{2,1,0:T(8,128)S(1)}, f32[16,8,256]{2,1,0:T(8,128)S(1)}, u32[]{:S(2)}, u32[]{:S(2)}) collective-permute-start(f32[16,8,256]{2,1,0:T(8,128)S(1)} %slice_select_fusion.1), channel_id=1, source_target_pairs={{0,1},{1,0},{2,3},{3,2},{4,5},{5,4},{6,7},{7,6},{8,9},{9,8},{10,11... | collective-permute-start | bytes 393224 | tf_op jit(solution)/shard_map/ppermute | solution.py:307
  66.1 1.3 collective-permute-start.5
  67.6 7.5 %collective-permute-start.6 = (f32[32,512]{1,0:T(8,128)S(1)}, f32[32,512]{1,0:T(8,128)S(1)}, u32[]{:S(2)}, u32[]{:S(2)}) collective-permute-start(f32[32,512]{1,0:T(8,128)S(1)} %select_reduce_fusion.1), channel_id=1, source_target_pairs={{5,0},{34,1},{64,2},{103,3},{147,4},{180,5},{214,6},{241,7},{13,8}... | collective-permute-start | bytes 196616 | tf_op jit(solution)/shard_map/ppermute | solution.py:327
  69.0 7.5 %collective-permute-start.7 = (f32[32,512]{1,0:T(8,128)S(1)}, f32[32,512]{1,0:T(8,128)S(1)}, u32[]{:S(2)}, u32[]{:S(2)}) collective-permute-start(f32[32,512]{1,0:T(8,128)S(1)} %down.3), channel_id=1, source_target_pairs={{0,5},{1,34},{2,64},{3,103},{4,147},{5,180},{6,214},{7,241},{8,13}... | collective-permute-start | bytes 196616 | tf_op jit(solution)/shard_map/ppermute | solution.py:300
  76.6 1.4 %collective-permute-start.8 = (f32[16,8,256]{2,1,0:T(8,128)S(1)}, f32[16,8,256]{2,1,0:T(8,128)S(1)}, u32[]{:S(2)}, u32[]{:S(2)}) collective-permute-start(f32[16,8,256]{2,1,0:T(8,128)S(1)} %slice_select_fusion), channel_id=1, source_target_pairs={{0,1},{1,0},{2,3},{3,2},{4,5},{5,4},{6,7},{7,6},{8,9},{9,8},{10,11... | collective-permute-start | bytes 393224 | tf_op jit(solution)/shard_map/ppermute | solution.py:307
  107.0 1.3 collective-permute-start.9
  109.3 7.8 %collective-permute-start.10 = (f32[32,704]{1,0:T(8,128)S(1)}, f32[32,704]{1,0:T(8,128)S(1)}, u32[]{:S(2)}, u32[]{:S(2)}) collective-permute-start(f32[32,704]{1,0:T(8,128)S(1)} %pad_maximum_fusion.4), channel_id=1, source_target_pairs={{5,0},{34,1},{64,2},{103,3},{147,4},{180,5},{214,6},{241,7},{13,8}... | collective-permute-start | bytes 270344 | tf_op jit(solution)/shard_map/ppermute | solution.py:334
  117.1 1.2 collective-permute-start.11
  118.3 3.9 %collective-permute-start.12 = (f32[32,192]{1,0:T(8,128)S(1)}, f32[32,192]{1,0:T(8,128)S(1)}, u32[]{:S(2)}, u32[]{:S(2)}) collective-permute-start(f32[32,192]{1,0:T(8,128)S(1)} %slice_add_fusion), channel_id=1, source_target_pairs={{0,2},{2,0},{4,6},{6,4},{1,3},{3,1},{5,7},{7,5},{8,10},{10,8},{12,... | collective-permute-start | bytes 73736 | tf_op jit(solution)/shard_map/ppermute | solution.py:339
  122.2 3.9 %collective-permute-start.13 = (f32[32,192]{1,0:T(8,128)S(1)}, f32[32,192]{1,0:T(8,128)S(1)}, u32[]{:S(2)}, u32[]{:S(2)}) collective-permute-start(f32[32,192]{1,0:T(8,128)S(1)} %add.62), channel_id=1, source_target_pairs={{0,6},{6,0},{2,4},{4,2},{1,7},{7,1},{3,5},{5,3},{8,14},{14,8},{10,... | collective-permute-start | bytes 73736 | tf_op jit(solution)/shard_map/ppermute | solution.py:340

commit v5 on v4

--- a/solution.py
+++ b/solution.py
@@ -44,12 +44,8 @@
     return [(b, a) for a, b in to_row_group()]
 
 
-def far_table():
-    table = [[0.0] * 8 for _ in range(8)]
-    for j in range(8):
-        for row in range(8):
-            table[j][PLACE[j][row]] = float((row // 4) != (j // 4))
-    return table
+def far_bits(row):
+    return sum(((r // 4) != (row // 4)) << PLACE[row][r] for r in range(8))
 
 
 def mm(a, b):
@@ -90,47 +86,62 @@
     return jnp.transpose(upper), wide[:, n:]
 
 
-def finish(scale, grams_ref, x_ref, y_ref, z_ref, hist_ref, out_ref, g_ref, p_ref, v_ref):
-    n = 32
-    part = grams_ref[...] * scale
-    at = 0
-    for i in range(3):
-        for k in range(i + 1):
-            block = part[:, at * n : (at + 1) * n]
-            g_ref[i * n : (i + 1) * n, k * n : (k + 1) * n] = block
-            if k < i:
-                g_ref[k * n : (k + 1) * n, i * n : (i + 1) * n] = jnp.transpose(block)
-            at += 1
-    v_ref[0:n] = x_ref[...]
-    v_ref[n : 2 * n] = y_ref[...]
-    v_ref[2 * n :] = z_ref[...]
+def first_step(scale, gram_ref, history_ref, first_ref, second_ref):
+    n = gram_ref.shape[0]
+    g00 = gram_ref[:, 0:n] * scale
+    g10 = gram_ref[:, n : 2 * n] * scale
+    low0, t0 = factor_and_inverse(g00)
+    a0 = mmt(mm(t0, g10), t0)
+    history_ref[0] = a0
+    second_ref[:, 0:n] = -mm(a0, t0)
+    second_ref[:, n : 2 * n] = t0
+    p1 = second_ref[...]
+    whole = jnp.concatenate(
+        [
+            jnp.concatenate([g00, jnp.transpose(g10)], axis=1),
+            gram_ref[:, n : 3 * n] * scale,
+        ],
+        axis=0,
+    )
+    low1, t1 = factor_and_inverse(mmt(mm(p1, whole), p1))
+    history_ref[1] = low1
+    q1 = mm(t1, p1)
+    second_ref[...] = q1
+    first_ref[:, 0:n] = -lax.dot_general(
+        low1, t0, (((0,), (0,)), ((), ())), precision=FULL, preferred_element_type=jnp.float32
+    )
+    first_ref[:, n : 3 * n] = q1
+
+
+def last_step(
+    scale, gram_ref, gram2_ref, history0_ref, image_ref, second_ref, x_ref, y_ref, z_ref,
+    history_ref, out_ref, g_ref, p_ref, v_ref,
+):
+    n = gram_ref.shape[0]
     eye = jnp.where(
         lax.broadcasted_iota(jnp.int32, (n, n), 0) == lax.broadcasted_iota(jnp.int32, (n, n), 1),
         SHIFT,
         0.0,
     )
-    low0, t0 = factor_and_inverse(g_ref[0:n, 0:n])
-    a0 = mmt(mm(t0, g_ref[n : 2 * n, 0:n]), t0)
-    hist_ref[0, 0] = a0 + eye
-    m0 = mm(a0, t0)
-    p_ref[:, 0:n] = -m0
-    p_ref[:, n : 2 * n] = t0
-    p1 = p_ref[:, 0 : 2 * n]
-    low1, t1 = factor_and_inverse(mmt(mm(p1, g_ref[0 : 2 * n, 0 : 2 * n]), p1))
-    hist_ref[0, 1] = low1
-    q1 = mm(t1, p1)
-    d0 = lax.dot_general(
-        low1, t0, (((0,), (0,)), ((), ())), precision=FULL, preferred_element_type=jnp.float32
-    )
-    p_ref[:, 0:n] = -d0
-    p_ref[:, n : 3 * n] = q1
-    w1 = p_ref[...]
+    g_ref[0:n, 0:n] = gram_ref[:, 0:n] * scale
+    g_ref[n : 2 * n, 0 : 2 * n] = gram_ref[:, n : 3 * n] * scale
+    g_ref[0:n, n : 2 * n] = jnp.transpose(gram_ref[:, n : 2 * n]) * scale
+    g_ref[2 * n :, :] = gram2_ref[...] * scale
+    g_ref[0:n, 2 * n :] = jnp.transpose(gram2_ref[:, 0:n]) * scale
+    g_ref[n : 2 * n, 2 * n :] = jnp.transpose(gram2_ref[:, n : 2 * n]) * scale
+    history_ref[0, 0] = history0_ref[0] + eye
+    history_ref[0, 1] = history0_ref[1]
+    w1 = image_ref[...]
+    q1 = second_ref[...]
     a1 = mmt(mm(w1, g_ref[:, 0 : 2 * n]), q1)
-    hist_ref[1, 0] = a1 + eye
-    p_ref[:, 0 : 2 * n] = mm(a1, q1)
-    w1 = jnp.concatenate([w1[:, 0 : 2 * n] - p_ref[:, 0 : 2 * n], w1[:, 2 * n :]], axis=1)
+    history_ref[1, 0] = a1 + eye
+    p_ref[...] = mm(a1, q1)
+    w1 = jnp.concatenate([w1[:, 0 : 2 * n] - p_ref[...], w1[:, 2 * n :]], axis=1)
     low2, t2 = factor_and_inverse(mmt(mm(w1, g_ref[...]), w1))
-    hist_ref[1, 1] = low2
+    history_ref[1, 1] = low2
+    v_ref[0:n] = x_ref[...]
+    v_ref[n : 2 * n] = y_ref[...]
+    v_ref[2 * n :] = z_ref[...]
     out_ref[...] = mm(t2, mm(w1, v_ref[...]))
 
 
@@ -172,13 +183,14 @@
     out_ref[...] = total
 
 
-def across_kernel(lead_ref, own_ref, high_ref, low_ref, out_ref):
+def across_kernel(leads_ref, energies_ref, own_ref, high_ref, low_ref, out_ref):
     slots, _, width = out_ref.shape
     left = parts_of(own_ref[...])
+    lead = (energies_ref[...] - SHIFT) * own_ref[...]
     for s in range(slots):
         rows = pl.ds(s * width, width)
         term = dot3(left, high_ref[rows, :], low_ref[rows, :], 1)
-        out_ref[s] = term + lead_ref[pl.ds(s, 1), :] * own_ref[...]
+        out_ref[s] = term + leads_ref[s] * lead
 
 
 def gram_kernel(*refs):
@@ -222,22 +234,51 @@
     )(parts)
 
 
-def close(grams, x, y, z, length):
+def begin(gram, length):
+    vecs = gram.shape[0]
+    return pl.pallas_call(
+        functools.partial(first_step, 1.0 / length),
+        in_specs=[IN_VMEM],
+        out_specs=(IN_VMEM,) * 3,
+        out_shape=(
+            pltpu.VMEM((2, vecs, vecs), jnp.float32),
+            pltpu.VMEM((vecs, 3 * vecs), jnp.float32),
+            pltpu.VMEM((vecs, 2 * vecs), jnp.float32),
+        ),
+        compiler_params=LIMIT,
+        cost_estimate=pl.CostEstimate(flops=6 * 10**9, bytes_accessed=10**5, transcendentals=0),
+        name="first_step",
+    )(gram)
+
+
+def close(gram, gram2, history0, image, second, x, y, z, length):
     vecs = x.shape[0]
     return pl.pallas_call(
-        functools.partial(finish, 1.0 / length),
+        functools.partial(last_step, 1.0 / length),
         out_shape=(
             jax.ShapeDtypeStruct((2, 2, vecs, vecs), jnp.float32),
             jax.ShapeDtypeStruct(x.shape, jnp.float32),
         ),
         scratch_shapes=[
             pltpu.VMEM((3 * vecs, 3 * vecs), jnp.float32),
-            pltpu.VMEM((vecs, 3 * vecs), jnp.float32),
+            pltpu.VMEM((vecs, 2 * vecs), jnp.float32),
             pltpu.VMEM((3 * vecs, x.shape[1]), jnp.float32),
         ],
         compiler_params=LIMIT,
-        name="recurrence",
-    )(grams, x, y, z)
+        name="last_step",
+    )(gram, gram2, history0, image, second, x, y, z)
+
+
+EXCHANGES = (
+    ("y", [(0, 1), (1, 0), (2, 3), (3, 2)]),
+    ("y", [(0, 3), (3, 0), (1, 2), (2, 1)]),
+    (("zh", "z"), [(h * 4 + z, (1 - h) * 4 + (z + 2) % 4) for h in range(2) for z in range(4)]),
+)
+
+
+def exchanged(value, step):
+    axis, pairs = EXCHANGES[step]
+    return value + lax.ppermute(value, axis, pairs)
 
 
 def on_device(start_block, energies, hamiltonian):
@@ -255,24 +296,30 @@
     weight = jnp.where(block_rows < col, 1.0, jnp.where(block_rows == col, 0.5, 0.0)).astype(
         jnp.float32
     )
-    own_slot = (jnp.arange(slots) == z) & (place == row)
-    lead = jnp.where(own_slot[:, None], (energies - SHIFT)[None, :], 0.0)
-    table = jnp.array(far_table(), jnp.float32).reshape(-1)
-    far = jnp.sum(table * (jnp.arange(64) == row * 8 + place).astype(jnp.float32)) > 0.5
+    leads = ((jnp.arange(slots) == z) & (place == row)).astype(jnp.float32)
+    bits = jnp.int32(0)
+    for r in range(8):
+        bits = jnp.where(row == r, jnp.int32(far_bits(r)), bits)
+    far = lax.shift_right_logical(bits, place) % 2 == 1
     slot = jnp.where(far, (z + 2) % 4, z)
+    odd = lax.rem(z, 2) == 1
+    upper = (z >= 2) != far
+    weight, leads, slot, odd, upper, first = lax.optimization_barrier(
+        (weight, leads, slot, odd, upper, core == 0)
+    )
     in_slot = (jnp.arange(slots) == slot)[:, None, None]
     every = NAMES
 
     high, low = pl.pallas_call(
         split_blocks,
-        in_specs=[pl.BlockSpec(memory_space=pltpu.SMEM), pl.BlockSpec(memory_space=pl.ANY)],
+        in_specs=[pl.BlockSpec(memory_space=pltpu.SMEM), pl.BlockSpec(memory_space=pltpu.HBM)],
         out_specs=(IN_VMEM, IN_VMEM),
         out_shape=(pltpu.VMEM((slots * width, width), jnp.bfloat16),) * 2,
         scratch_shapes=[
             pltpu.VMEM(blocks.shape, jnp.float32),
             pltpu.SemaphoreType.DMA((slots,)),
         ],
-        compiler_params=LIMIT,
+        compiler_params=pltpu.CompilerParams(vmem_limit_bytes=58 * 2**20),
         name="split_blocks",
     )(weight, blocks)
 
@@ -289,56 +336,59 @@
     def across(own):
         return pl.pallas_call(
             across_kernel,
-            in_specs=[IN_VMEM] * 4,
+            in_specs=[pl.BlockSpec(memory_space=pltpu.SMEM)] + [IN_VMEM] * 4,
             out_specs=IN_VMEM,
             out_shape=pltpu.VMEM((slots, vecs, width), jnp.float32),
             compiler_params=LIMIT,
             name="across",
-        )(lead, own, high, low)
-
-    def total(acrosses, downs):
+        )(leads, energies.reshape(1, width), own, high, low)
+
+    def total(acrosses, downs, gram=None):
         arrived = lax.ppermute(downs, every, to_row_group())
         acrosses = lax.optimization_barrier(acrosses)
         part = acrosses + jnp.where(in_slot, arrived[None], 0.0)
         part = part.reshape(slots * vecs // 8, 8, width)
         low, high = part[..., :half], part[..., half:]
-        mine = jnp.where(core == 0, low, high)
-        other = jnp.where(core == 0, high, low)
+        mine = jnp.where(first, low, high)
+        other = jnp.where(first, high, low)
         mine = mine + lax.ppermute(other, "co", [(0, 1), (1, 0)])
+        if gram is not None:
+            mine, gram = lax.optimization_barrier((mine, exchanged(gram, 0)))
         pieces = lax.all_to_all(mine, ("z", "x"), 0, 0, tiled=True)
         whole = lax.all_to_all(sum_spread(pieces), ("z", "x"), 0, 0, tiled=True)
+        if gram is not None:
+            whole, gram = lax.optimization_barrier((whole, gram))
+            gram = exchanged(gram, 1)
         facing = lax.ppermute(whole, "co", [(0, 1), (1, 0)])
-        low = jnp.where(core == 0, whole, facing)
-        high = jnp.where(core == 0, facing, whole)
-        return jnp.concatenate([low, high], axis=-1).reshape(slots, vecs, width)
+        low = jnp.where(first, whole, facing)
+        high = jnp.where(first, facing, whole)
+        four = jnp.concatenate([low, high], axis=-1).reshape(slots, vecs, width)
+        return four, gram
 
     def slot_of(four):
         return jnp.sum(jnp.where(in_slot, four, 0.0), axis=0)
 
     moved = lax.ppermute(start_block, every, to_row_group())
+    moved, high, low = lax.optimization_barrier((moved, high, low))
     near = lax.ppermute(moved, "z", [(0, 1), (1, 0), (2, 3), (3, 2)])
-    odd = lax.rem(z, 2) == 1
     two = jnp.stack([jnp.where(odd, near, moved), jnp.where(odd, moved, near)])
     over = lax.ppermute(two, "z", [(0, 2), (2, 0), (1, 3), (3, 1)])
-    upper = (z >= 2) != far
     x4 = jnp.concatenate([jnp.where(upper, over, two), jnp.where(upper, two, over)])
     x = start_block
-    y4 = total(across(x), down(x4))
+    y4, _ = total(across(x), down(x4))
     y = lax.ppermute(slot_of(y4), every, from_row_group())
     downs = down(y4)
-    acrosses, gx, gy = lax.optimization_barrier(
-        (across(y), grams_of(x4), grams_of(x4, y4))
-    )
-    z4 = total(acrosses, downs)
-    gz = grams_of(x4, y4, z4)
-    back = lax.ppermute(
-        jnp.concatenate([slot_of(z4), gx, gy, gz], axis=1), every, from_row_group()
-    )
-    zz, grams = back[:, :width], back[:, width:]
-    grams = grams + lax.ppermute(grams, "co", [(0, 1), (1, 0)])
-    grams = grams + lax.ppermute(grams, "x", [(0, 1), (1, 0), (2, 3), (3, 2)])
-    grams = grams + lax.ppermute(grams, "x", [(0, 3), (3, 0), (1, 2), (2, 1)])
-    return close(grams, x, y, zz, col_count * width)
+    y, x4_late, y4_late = lax.optimization_barrier((y, x4, y4))
+    acrosses = across(y)
+    gram = jnp.concatenate([grams_of(x4_late), grams_of(x4_late, y4_late)], axis=1)
+    z4, gram = total(acrosses, downs, gram)
+    gram2, gram = lax.optimization_barrier((grams_of(x4, y4, z4), gram))
+    gram = exchanged(gram, 2)
+    zz = lax.ppermute(slot_of(z4), every, from_row_group())
+    for step in range(len(EXCHANGES)):
+        gram2 = exchanged(gram2, step)
+    length = col_count * width
+    return close(gram, gram2, *begin(gram, length), x, y, zz, length)
 
 
 def solution(mesh):

time: 138 us -> 133 us (0.964); the launches traced: 136 us -> 133 us
  Pallas kernels: 17.4 us -> 20 us
  local copies, waits for them, and re-layouts: 2.2 us -> 0.01 us
  starting transfers between devices: 16 us -> 17.6 us
  waiting for transfers between devices: 35.5 us -> 34 us
  other arithmetic: 2.78 us -> 1.31 us
    ppermute x4 -> x7, starting transfers between devices: 1.51 us -> 4.34 us  [the longest x1 3.05 us: on_device(): zz = lax.ppermute(slot_of(z4), every, from_row_group())]
    unnamed x4, local copies, waits for them, and re-layouts: 2.19 us -> 0.01 us
    pallas_call x1, Pallas kernels: 1.65 us -> 3.07 us  [on_device(): pl.pallas_call(split_blocks, in_specs=[pl.BlockSpec(memory_space=pltpu.SM...]
    pallas_call x3 -> x4, Pallas kernels: 12.5 us -> 13.7 us  [the longest x1 5.66 us: begin(): pl.pallas_call(functools.partial(first_step, 1.0 / length), in_specs=[IN_...]
    ppermute x4 -> x7, waiting for transfers between devices: 15.3 us -> 14.5 us  [the longest x6 14.5 us: exchanged(): return value + lax.ppermute(value, axis, pairs)]
  transfers between devices with their start and end apart: 14 -> 17, of which waited for: 12 -> 11; matrix products, arithmetic and copies ran while one was open for 2% -> 1% of each run, Pallas kernels for 4% -> 11%
where the time goes in v5:
time: 133 us
  blocking collectives  59.4 us (45%)
  waiting for transfers between devices  34 us (26%)
  Pallas kernels  20 us (15%)
  starting transfers between devices  17.6 us (13%)
    all_to_all x2, blocking collectives, total(): pieces = lax.all_to_all(mine, ('z', 'x'), 0, 0, tiled=True)  35.7 us
    all_to_all x2, blocking collectives, total(): whole = lax.all_to_all(sum_spread(pieces), ('z', 'x'), 0, 0, tiled=True)  23.7 us
    ppermute x6, waiting for transfers between devices, exchanged(): return value + lax.ppermute(value, axis, pairs)  14.5 us
    ppermute x1, waiting for transfers between devices, on_device(): over = lax.ppermute(two, 'z', [(0, 2), (2, 0), (1, 3), (3, 1)])  6.48 us
    pallas_call x1, Pallas kernels, begin(): pl.pallas_call(functools.partial(first_step, 1.0 / length), in_specs=[IN_...  5.66 us
    ppermute x2, waiting for transfers between devices, total(): arrived = lax.ppermute(downs, every, to_row_group())  4.78 us
    pallas_call x1, Pallas kernels, close(): pl.pallas_call(functools.partial(last_step, 1.0 / length), out_shape=(jax...  4.28 us
    ppermute x2, starting transfers between devices, total(): arrived = lax.ppermute(downs, every, to_row_group())  4.01 us
  transfers between devices with their start and end apart: 17, of which 11 were waited for; matrix products, arithmetic and copies ran while one was open for 1% of the time, Pallas kernels for 11%

profile of v5, /device:TPU:2, one launch (start us, length us, event | category | flops | bytes accessed | tf_op | source)
XLA Modules:
  0.0 133.2 jit_solution(15168888286548578051)
XLA Ops:
  0.6 3.3 %collective-permute-start = (f32[32,512]{1,0:T(8,128)}, f32[32,512]{1,0:T(8,128)S(1)}, u32[]{:S(2)}, u32[]{:S(2)}) collective-permute-start(f32[32,512]{1,0:T(8,128)} %x_ref.1), channel_id=1, source_target_pairs={{0,5},{1,34},{2,64},{3,103},{4,147},{5,180},{6,214},{7,241},{8,13}... | collective-permute-start | bytes 196616 | tf_op jit(solution)/shard_map/ppermute | solution.py:371
  4.4 3.1 %split_blocks.1 = (bf16[2048,512]{1,0:T(8,128)(2,1)S(1)}, bf16[2048,512]{1,0:T(8,128)(2,1)S(1)}) custom-call(f32[4]{0:T(128)} %compare_select_fusion.1.weight_ref, f32[4,512,512]{2,1,0:T(8,128)} %bitcast.22), custom_call_target="tpu_custom_call" | custom-call | tf_op jit(solution)/shard_map/split_blocks/pallas_call | solution.py:313
  7.9 1.9 %collective-permute-start.1 = (f32[32,512]{1,0:T(8,128)S(1)}, f32[32,512]{1,0:T(8,128)S(1)}, u32[]{:S(2)}, u32[]{:S(2)}) collective-permute-start(f32[32,512]{1,0:T(8,128)S(1)} %collective-permute-done), channel_id=1, source_target_pairs={{0,8},{8,0},{16,24},{24,16},{1,9},{9,1},{17,25},{25,17},{2,10},{10... | collective-permute-start | bytes 196616 | tf_op jit(solution)/shard_map/ppermute | solution.py:373
  9.8 2.9 %collective-permute-done.1 = f32[32,512]{1,0:T(8,128)S(1)} collective-permute-done((f32[32,512]{1,0:T(8,128)S(1)}, f32[32,512]{1,0:T(8,128)S(1)}, u32[]{:S(2)}, u32[]{:S(2)}) %collective-permute-start.1) | collective-permute-done | bytes 65568 | tf_op jit(solution)/shard_map/ppermute | solution.py:373
  12.7 3.4 %collective-permute-start.2 = (f32[2,32,512]{2,1,0:T(8,128)S(1)}, f32[2,32,512]{2,1,0:T(8,128)S(1)}, u32[]{:S(2)}, u32[]{:S(2)}) collective-permute-start(f32[2,32,512]{2,1,0:T(8,128)S(1)} %pad_maximum_fusion.3), channel_id=1, source_target_pairs={{0,16},{16,0},{8,24},{24,8},{1,17},{17,1},{9,25},{25,9},{2,18},{18... | collective-permute-start | bytes 393224 | tf_op jit(solution)/shard_map/ppermute | solution.py:375
  16.1 6.5 %collective-permute-done.2 = f32[2,32,512]{2,1,0:T(8,128)S(1)} collective-permute-done((f32[2,32,512]{2,1,0:T(8,128)S(1)}, f32[2,32,512]{2,1,0:T(8,128)S(1)}, u32[]{:S(2)}, u32[]{:S(2)}) %collective-permute-start.2) | collective-permute-done | bytes 131104 | tf_op jit(solution)/shard_map/ppermute | solution.py:375
  23.5 1.9 %across.2 = f32[4,32,512]{2,1,0:T(8,128)S(1)} custom-call(f32[4]{0:T(128)S(1)} %and_convert_fusion.leads_ref, f32[1,512]{1,0:T(1,128)S(1)} %bitcast.20, f32[32,512]{1,0:T(8,128)S(1)} %copy-done, bf16[2048,512]{1,0:T(8,128)(2,1)S(1)} %get-tuple-element.33.high_ref, bf16[2048,512]{1,0:T(8,128)(2,1)S(1)} %get-tuple-element.34.low_ref), custom_call_target="tpu_custom_call" | custom-call | tf_op jit(solution)/shard_map/across/pallas_call | solution.py:337
  25.4 4.8 %collective-permute-done.3 = f32[32,512]{1,0:T(8,128)S(1)} collective-permute-done((f32[32,512]{1,0:T(8,128)S(1)}, f32[32,512]{1,0:T(8,128)S(1)}, u32[]{:S(2)}, u32[]{:S(2)}) %collective-permute-start.3) | collective-permute-done | bytes 65568 | tf_op jit(solution)/shard_map/ppermute | solution.py:347
  30.4 1.3 %collective-permute-done.4 = f32[16,8,256]{2,1,0:T(8,128)S(1)} collective-permute-done((f32[16,8,256]{2,1,0:T(8,128)S(1)}, f32[16,8,256]{2,1,0:T(8,128)S(1)}, u32[]{:S(2)}, u32[]{:S(2)}) %collective-permute-start.4) | collective-permute-done | bytes 131104 | tf_op jit(solution)/shard_map/ppermute | solution.py:354
  31.7 20.1 %all_to_all.20.parts_ref = f32[16,8,256]{2,1,0:T(8,128)S(1)} all-to-all(f32[16,8,256]{2,1,0:T(8,128)S(1)} %select_add_fusion.3), channel_id=1, replica_groups=mesh['zh'=2,'y'=4,'z'=4,'x'=4,'co'=2] {'z','x'}, dimensions={0} | all-to-all | bytes 262144 | tf_op jit(solution)/shard_map/all_to_all | solution.py:357
  51.8 11.8 %all_to_all.21 = f32[16,8,256]{2,1,0:T(8,128)S(1)} all-to-all(f32[16,8,256]{2,1,0:T(8,128)S(1)} %sum_spread.2), channel_id=1, replica_groups=mesh['zh'=2,'y'=4,'z'=4,'x'=4,'co'=2] {'z','x'}, dimensions={0} | all-to-all | bytes 262144 | tf_op jit(solution)/shard_map/all_to_all | solution.py:358
  63.7 1.3 %collective-permute-done.5 = f32[16,8,256]{2,1,0:T(8,128)S(1)} collective-permute-done((f32[16,8,256]{2,1,0:T(8,128)S(1)}, f32[16,8,256]{2,1,0:T(8,128)S(1)}, u32[]{:S(2)}, u32[]{:S(2)}) %collective-permute-start.5) | collective-permute-done | bytes 131104 | tf_op jit(solution)/shard_map/ppermute | solution.py:362
  66.5 4.0 %collective-permute-start.7 = (f32[32,512]{1,0:T(8,128)S(1)}, f32[32,512]{1,0:T(8,128)S(1)}, u32[]{:S(2)}, u32[]{:S(2)}) collective-permute-start(f32[32,512]{1,0:T(8,128)S(1)} %down.3), channel_id=1, source_target_pairs={{0,5},{1,34},{2,64},{3,103},{4,147},{5,180},{6,214},{7,241},{8,13}... | collective-permute-start | bytes 196616 | tf_op jit(solution)/shard_map/ppermute | solution.py:347
  70.5 2.2 %collective-permute-done.6.own_ref.y_ref = f32[32,512]{1,0:T(8,128)S(1)} collective-permute-done((f32[32,512]{1,0:T(8,128)S(1)}, f32[32,512]{1,0:T(8,128)S(1)}, u32[]{:S(2)}, u32[]{:S(2)}) %collective-permute-start.6) | collective-permute-done | bytes 65568 | tf_op jit(solution)/shard_map/ppermute | solution.py:379
  72.7 1.9 %across.3 = f32[4,32,512]{2,1,0:T(8,128)S(1)} custom-call(f32[4]{0:T(128)S(1)} %and_convert_fusion.leads_ref, f32[1,512]{1,0:T(1,128)S(1)} %bitcast.21, f32[32,512]{1,0:T(8,128)S(1)} %collective-permute-done.6.own_ref.y_ref, bf16[2048,512]{1,0:T(8,128)(2,1)S(1)} %get-tuple-element.33.high_ref, bf16[2048,512]{1,0:T(8,128)(2,1)S(1)} %get-tuple-element.34.low_ref), custom_call_target="tpu_custom_call" | custom-call | tf_op jit(solution)/shard_map/across/pallas_call | solution.py:337
  75.9 3.5 %collective-permute-done.9 = f32[32,96]{1,0:T(8,128)S(1)} collective-permute-done((f32[32,96]{1,0:T(8,128)S(1)}, f32[32,96]{1,0:T(8,128)S(1)}, u32[]{:S(2)}, u32[]{:S(2)}) %collective-permute-start.9) | collective-permute-done | bytes 12320 | tf_op jit(solution)/shard_map/ppermute | solution.py:281
  79.5 15.7 %all_to_all.22.parts_ref = f32[16,8,256]{2,1,0:T(8,128)S(1)} all-to-all(f32[16,8,256]{2,1,0:T(8,128)S(1)} %select_add_fusion.2), channel_id=1, replica_groups=mesh['zh'=2,'y'=4,'z'=4,'x'=4,'co'=2] {'z','x'}, dimensions={0} | all-to-all | bytes 262144 | tf_op jit(solution)/shard_map/all_to_all | solution.py:357
  95.2 11.8 %all_to_all.23 = f32[16,8,256]{2,1,0:T(8,128)S(1)} all-to-all(f32[16,8,256]{2,1,0:T(8,128)S(1)} %sum_spread.3), channel_id=1, replica_groups=mesh['zh'=2,'y'=4,'z'=4,'x'=4,'co'=2] {'z','x'}, dimensions={0} | all-to-all | bytes 262144 | tf_op jit(solution)/shard_map/all_to_all | solution.py:358
  107.0 4.9 %collective-permute-done.11 = f32[32,96]{1,0:T(8,128)S(1)} collective-permute-done((f32[32,96]{1,0:T(8,128)S(1)}, f32[32,96]{1,0:T(8,128)S(1)}, u32[]{:S(2)}, u32[]{:S(2)}) %collective-permute-start.11) | collective-permute-done | bytes 12320 | tf_op jit(solution)/shard_map/ppermute | solution.py:281
  112.9 3.6 %collective-permute-done.13 = f32[32,96]{1,0:T(8,128)S(1)} collective-permute-done((f32[32,96]{1,0:T(8,128)S(1)}, f32[32,96]{1,0:T(8,128)S(1)}, u32[]{:S(2)}, u32[]{:S(2)}) %collective-permute-start.13) | collective-permute-done | bytes 12320 | tf_op jit(solution)/shard_map/ppermute | solution.py:281
  116.7 3.0 %collective-permute-start.16 = (f32[32,512]{1,0:T(8,128)S(1)}, f32[32,512]{1,0:T(8,128)S(1)}, u32[]{:S(2)}, u32[]{:S(2)}) collective-permute-start(f32[32,512]{1,0:T(8,128)S(1)} %select_reduce_fusion), channel_id=1, source_target_pairs={{5,0},{34,1},{64,2},{103,3},{147,4},{180,5},{214,6},{241,7},{13,8}... | collective-permute-start | bytes 196616 | tf_op jit(solution)/shard_map/ppermute | solution.py:387
  119.7 2.4 %collective-permute-done.14 = f32[32,96]{1,0:T(8,128)S(1)} collective-permute-done((f32[32,96]{1,0:T(8,128)S(1)}, f32[32,96]{1,0:T(8,128)S(1)}, u32[]{:S(2)}, u32[]{:S(2)}) %collective-permute-start.14) | collective-permute-done | bytes 12320 | tf_op jit(solution)/shard_map/ppermute | solution.py:281
  123.2 5.7 %first_step.1 = (f32[2,32,32]{2,1,0:T(8,128)S(1)}, f32[32,96]{1,0:T(8,128)S(1)}, f32[32,64]{1,0:T(8,128)S(1)}) custom-call(f32[32,96]{1,0:T(8,128)S(1)} %add.70.gram_ref), custom_call_target="tpu_custom_call" | custom-call | flops 6000000000 | bytes 100000 | tf_op jit(solution)/shard_map/first_step/pallas_call | solution.py:239
  128.9 4.3 %last_step.1 = (f32[2,2,32,32]{3,2,1,0:T(8,128)}, f32[32,512]{1,0:T(8,128)}) custom-call(f32[32,96]{1,0:T(8,128)S(1)} %add.70.gram_ref, f32[32,96]{1,0:T(8,128)S(1)} %add.73.gram2_ref, f32[2,32,32]{2,1,0:T(8,128)S(1)} %get-tuple-element.45.history0_ref, f32[32,96]{1,0:T(8,128)S(1)} %get-tuple-element.46.image_ref, ...), custom_call_target="tpu_custom_call" | custom-call | tf_op jit(solution)/shard_map/last_step/pallas_call | solution.py:256
  (56 shorter events, 7.0 us)
Async XLA Ops:
  0.6 7.2 %collective-permute-start = (f32[32,512]{1,0:T(8,128)}, f32[32,512]{1,0:T(8,128)S(1)}, u32[]{:S(2)}, u32[]{:S(2)}) collective-permute-start(f32[32,512]{1,0:T(8,128)} %x_ref.1), channel_id=1, source_target_pairs={{0,5},{1,34},{2,64},{3,103},{4,147},{5,180},{6,214},{7,241},{8,13}... | collective-permute-start | bytes 196616 | tf_op jit(solution)/shard_map/ppermute | solution.py:371
  7.9 4.9 %collective-permute-start.1 = (f32[32,512]{1,0:T(8,128)S(1)}, f32[32,512]{1,0:T(8,128)S(1)}, u32[]{:S(2)}, u32[]{:S(2)}) collective-permute-start(f32[32,512]{1,0:T(8,128)S(1)} %collective-permute-done), channel_id=1, source_target_pairs={{0,8},{8,0},{16,24},{24,16},{1,9},{9,1},{17,25},{25,17},{2,10},{10... | collective-permute-start | bytes 196616 | tf_op jit(solution)/shard_map/ppermute | solution.py:373
  12.7 9.8 %collective-permute-start.2 = (f32[2,32,512]{2,1,0:T(8,128)S(1)}, f32[2,32,512]{2,1,0:T(8,128)S(1)}, u32[]{:S(2)}, u32[]{:S(2)}) collective-permute-start(f32[2,32,512]{2,1,0:T(8,128)S(1)} %pad_maximum_fusion.3), channel_id=1, source_target_pairs={{0,16},{16,0},{8,24},{24,8},{1,17},{17,1},{9,25},{25,9},{2,18},{18... | collective-permute-start | bytes 393224 | tf_op jit(solution)/shard_map/ppermute | solution.py:375
  22.6 0.9 copy-start
  22.6 0.9 copy-start.1
  23.5 6.7 %collective-permute-start.3 = (f32[32,512]{1,0:T(8,128)S(1)}, f32[32,512]{1,0:T(8,128)S(1)}, u32[]{:S(2)}, u32[]{:S(2)}) collective-permute-start(f32[32,512]{1,0:T(8,128)S(1)} %down.2), channel_id=1, source_target_pairs={{0,5},{1,34},{2,64},{3,103},{4,147},{5,180},{6,214},{7,241},{8,13}... | collective-permute-start | bytes 196616 | tf_op jit(solution)/shard_map/ppermute | solution.py:347
  30.3 1.4 %collective-permute-start.4 = (f32[16,8,256]{2,1,0:T(8,128)S(1)}, f32[16,8,256]{2,1,0:T(8,128)S(1)}, u32[]{:S(2)}, u32[]{:S(2)}) collective-permute-start(f32[16,8,256]{2,1,0:T(8,128)S(1)} %slice_select_fusion.1), channel_id=1, source_target_pairs={{0,1},{1,0},{2,3},{3,2},{4,5},{5,4},{6,7},{7,6},{8,9},{9,8},{10,11... | collective-permute-start | bytes 393224 | tf_op jit(solution)/shard_map/ppermute | solution.py:354
  63.7 1.3 %collective-permute-start.5 = (f32[16,8,256]{2,1,0:T(8,128)S(1)}, f32[16,8,256]{2,1,0:T(8,128)S(1)}, u32[]{:S(2)}, u32[]{:S(2)}) collective-permute-start(f32[16,8,256]{2,1,0:T(8,128)S(1)} %all_to_all.21), channel_id=1, source_target_pairs={{0,1},{1,0},{2,3},{3,2},{4,5},{5,4},{6,7},{7,6},{8,9},{9,8},{10,11... | collective-permute-start | bytes 393224 | tf_op jit(solution)/shard_map/ppermute | solution.py:362
  65.2 7.6 %collective-permute-start.6 = (f32[32,512]{1,0:T(8,128)S(1)}, f32[32,512]{1,0:T(8,128)S(1)}, u32[]{:S(2)}, u32[]{:S(2)}) collective-permute-start(f32[32,512]{1,0:T(8,128)S(1)} %select_reduce_fusion.1), channel_id=1, source_target_pairs={{5,0},{34,1},{64,2},{103,3},{147,4},{180,5},{214,6},{241,7},{13,8}... | collective-permute-start | bytes 196616 | tf_op jit(solution)/shard_map/ppermute | solution.py:379
  66.5 9.1 %collective-permute-start.7 = (f32[32,512]{1,0:T(8,128)S(1)}, f32[32,512]{1,0:T(8,128)S(1)}, u32[]{:S(2)}, u32[]{:S(2)}) collective-permute-start(f32[32,512]{1,0:T(8,128)S(1)} %down.3), channel_id=1, source_target_pairs={{0,5},{1,34},{2,64},{3,103},{4,147},{5,180},{6,214},{7,241},{8,13}... | collective-permute-start | bytes 196616 | tf_op jit(solution)/shard_map/ppermute | solution.py:347
  75.6 3.8 %collective-permute-start.9 = (f32[32,96]{1,0:T(8,128)S(1)}, f32[32,96]{1,0:T(8,128)S(1)}, u32[]{:S(2)}, u32[]{:S(2)}) collective-permute-start(f32[32,96]{1,0:T(8,128)S(1)} %pad_maximum_fusion.4), channel_id=1, source_target_pairs={{0,32},{32,0},{64,96},{96,64},{1,33},{33,1},{65,97},{97,65},{2,34}... | collective-permute-start | bytes 36872 | tf_op jit(solution)/shard_map/ppermute | solution.py:281
  75.8 3.7 %collective-permute-start.8 = (f32[16,8,256]{2,1,0:T(8,128)S(1)}, f32[16,8,256]{2,1,0:T(8,128)S(1)}, u32[]{:S(2)}, u32[]{:S(2)}) collective-permute-start(f32[16,8,256]{2,1,0:T(8,128)S(1)} %slice_select_fusion), channel_id=1, source_target_pairs={{0,1},{1,0},{2,3},{3,2},{4,5},{5,4},{6,7},{7,6},{8,9},{9,8},{10,11... | collective-permute-start | bytes 393224 | tf_op jit(solution)/shard_map/ppermute | solution.py:354
  107.0 5.0 %collective-permute-start.10 = (f32[16,8,256]{2,1,0:T(8,128)S(1)}, f32[16,8,256]{2,1,0:T(8,128)S(1)}, u32[]{:S(2)}, u32[]{:S(2)}) collective-permute-start(f32[16,8,256]{2,1,0:T(8,128)S(1)} %all_to_all.23), channel_id=1, source_target_pairs={{0,1},{1,0},{2,3},{3,2},{4,5},{5,4},{6,7},{7,6},{8,9},{9,8},{10,11... | collective-permute-start | bytes 393224 | tf_op jit(solution)/shard_map/ppermute | solution.py:362
  107.0 5.0 %collective-permute-start.11 = (f32[32,96]{1,0:T(8,128)S(1)}, f32[32,96]{1,0:T(8,128)S(1)}, u32[]{:S(2)}, u32[]{:S(2)}) collective-permute-start(f32[32,96]{1,0:T(8,128)S(1)} %fusion), channel_id=1, source_target_pairs={{0,96},{96,0},{32,64},{64,32},{1,97},{97,1},{33,65},{65,33},{2,98}... | collective-permute-start | bytes 36872 | tf_op jit(solution)/shard_map/ppermute | solution.py:281
  112.7 3.8 %collective-permute-start.13 = (f32[32,96]{1,0:T(8,128)S(1)}, f32[32,96]{1,0:T(8,128)S(1)}, u32[]{:S(2)}, u32[]{:S(2)}) collective-permute-start(f32[32,96]{1,0:T(8,128)S(1)} %gram.5), channel_id=1, source_target_pairs={{0,32},{32,0},{64,96},{96,64},{1,33},{33,1},{65,97},{97,65},{2,34}... | collective-permute-start | bytes 36872 | tf_op jit(solution)/shard_map/ppermute | solution.py:281
  112.8 6.9 %collective-permute-start.12 = (f32[32,96]{1,0:T(8,128)S(1)}, f32[32,96]{1,0:T(8,128)S(1)}, u32[]{:S(2)}, u32[]{:S(2)}) collective-permute-start(f32[32,96]{1,0:T(8,128)S(1)} %add.69), channel_id=1, source_target_pairs={{0,144},{8,152},{16,128},{24,136},{128,16},{136,24},{144,0},{152,8... | collective-permute-start | bytes 36872 | tf_op jit(solution)/shard_map/ppermute | solution.py:281
  116.6 5.6 %collective-permute-start.14 = (f32[32,96]{1,0:T(8,128)S(1)}, f32[32,96]{1,0:T(8,128)S(1)}, u32[]{:S(2)}, u32[]{:S(2)}) collective-permute-start(f32[32,96]{1,0:T(8,128)S(1)} %add.71), channel_id=1, source_target_pairs={{0,96},{96,0},{32,64},{64,32},{1,97},{97,1},{33,65},{65,33},{2,98}... | collective-permute-start | bytes 36872 | tf_op jit(solution)/shard_map/ppermute | solution.py:281
  116.7 12.3 %collective-permute-start.16 = (f32[32,512]{1,0:T(8,128)S(1)}, f32[32,512]{1,0:T(8,128)S(1)}, u32[]{:S(2)}, u32[]{:S(2)}) collective-permute-start(f32[32,512]{1,0:T(8,128)S(1)} %select_reduce_fusion), channel_id=1, source_target_pairs={{5,0},{34,1},{64,2},{103,3},{147,4},{180,5},{214,6},{241,7},{13,8}... | collective-permute-start | bytes 196616 | tf_op jit(solution)/shard_map/ppermute | solution.py:387
  122.1 6.8 %collective-permute-start.15 = (f32[32,96]{1,0:T(8,128)S(1)}, f32[32,96]{1,0:T(8,128)S(1)}, u32[]{:S(2)}, u32[]{:S(2)}) collective-permute-start(f32[32,96]{1,0:T(8,128)S(1)} %add.72), channel_id=1, source_target_pairs={{0,144},{8,152},{16,128},{24,136},{128,16},{136,24},{144,0},{152,8... | collective-permute-start | bytes 36872 | tf_op jit(solution)/shard_map/ppermute | solution.py:281

commit v6 on v5

--- a/solution.py
+++ b/solution.py
@@ -86,10 +86,10 @@
     return jnp.transpose(upper), wide[:, n:]
 
 
-def first_step(scale, gram_ref, history_ref, first_ref, second_ref):
-    n = gram_ref.shape[0]
-    g00 = gram_ref[:, 0:n] * scale
-    g10 = gram_ref[:, n : 2 * n] * scale
+def first_step(scale, both_ref, history_ref, first_ref, second_ref):
+    n = both_ref.shape[0]
+    g00 = both_ref[:, 3 * n : 4 * n] * scale
+    g10 = both_ref[:, 4 * n : 5 * n] * scale
     low0, t0 = factor_and_inverse(g00)
     a0 = mmt(mm(t0, g10), t0)
     history_ref[0] = a0
@@ -99,7 +99,7 @@
     whole = jnp.concatenate(
         [
             jnp.concatenate([g00, jnp.transpose(g10)], axis=1),
-            gram_ref[:, n : 3 * n] * scale,
+            both_ref[:, 4 * n :] * scale,
         ],
         axis=0,
     )
@@ -114,21 +114,22 @@
 
 
 def last_step(
-    scale, gram_ref, gram2_ref, history0_ref, image_ref, second_ref, x_ref, y_ref, z_ref,
+    scale, both_ref, half_ref, history0_ref, image_ref, second_ref, x_ref, y_ref, z_ref,
     history_ref, out_ref, g_ref, p_ref, v_ref,
 ):
-    n = gram_ref.shape[0]
+    n = both_ref.shape[0]
+    gram2 = (both_ref[:, 0 : 3 * n] + half_ref[...]) * scale
     eye = jnp.where(
         lax.broadcasted_iota(jnp.int32, (n, n), 0) == lax.broadcasted_iota(jnp.int32, (n, n), 1),
         SHIFT,
         0.0,
     )
-    g_ref[0:n, 0:n] = gram_ref[:, 0:n] * scale
-    g_ref[n : 2 * n, 0 : 2 * n] = gram_ref[:, n : 3 * n] * scale
-    g_ref[0:n, n : 2 * n] = jnp.transpose(gram_ref[:, n : 2 * n]) * scale
-    g_ref[2 * n :, :] = gram2_ref[...] * scale
-    g_ref[0:n, 2 * n :] = jnp.transpose(gram2_ref[:, 0:n]) * scale
-    g_ref[n : 2 * n, 2 * n :] = jnp.transpose(gram2_ref[:, n : 2 * n]) * scale
+    g_ref[0:n, 0:n] = both_ref[:, 3 * n : 4 * n] * scale
+    g_ref[n : 2 * n, 0 : 2 * n] = both_ref[:, 4 * n :] * scale
+    g_ref[0:n, n : 2 * n] = jnp.transpose(both_ref[:, 4 * n : 5 * n]) * scale
+    g_ref[2 * n :, :] = gram2
+    g_ref[0:n, 2 * n :] = jnp.transpose(gram2[:, 0:n])
+    g_ref[n : 2 * n, 2 * n :] = jnp.transpose(gram2[:, n : 2 * n])
     history_ref[0, 0] = history0_ref[0] + eye
     history_ref[0, 1] = history0_ref[1]
     w1 = image_ref[...]
@@ -183,14 +184,17 @@
     out_ref[...] = total
 
 
-def across_kernel(leads_ref, energies_ref, own_ref, high_ref, low_ref, out_ref):
+def across_kernel(lead_ref, energies_ref, own_ref, high_ref, low_ref, out_ref):
     slots, _, width = out_ref.shape
     left = parts_of(own_ref[...])
-    lead = (energies_ref[...] - SHIFT) * own_ref[...]
     for s in range(slots):
         rows = pl.ds(s * width, width)
         term = dot3(left, high_ref[rows, :], low_ref[rows, :], 1)
-        out_ref[s] = term + leads_ref[s] * lead
+        out_ref[s] = term
+
+    @pl.when(lead_ref[0] == 1)
+    def _():
+        out_ref[lead_ref[1]] += (energies_ref[...] - SHIFT) * own_ref[...]
 
 
 def gram_kernel(*refs):
@@ -234,8 +238,8 @@
     )(parts)
 
 
-def begin(gram, length):
-    vecs = gram.shape[0]
+def begin(both, length):
+    vecs = both.shape[0]
     return pl.pallas_call(
         functools.partial(first_step, 1.0 / length),
         in_specs=[IN_VMEM],
@@ -248,10 +252,10 @@
         compiler_params=LIMIT,
         cost_estimate=pl.CostEstimate(flops=6 * 10**9, bytes_accessed=10**5, transcendentals=0),
         name="first_step",
-    )(gram)
-
-
-def close(gram, gram2, history0, image, second, x, y, z, length):
+    )(both)
+
+
+def close(both, half, history0, image, second, x, y, z, length):
     vecs = x.shape[0]
     return pl.pallas_call(
         functools.partial(last_step, 1.0 / length),
@@ -266,19 +270,15 @@
         ],
         compiler_params=LIMIT,
         name="last_step",
-    )(gram, gram2, history0, image, second, x, y, z)
-
-
-EXCHANGES = (
-    ("y", [(0, 1), (1, 0), (2, 3), (3, 2)]),
-    ("y", [(0, 3), (3, 0), (1, 2), (2, 1)]),
-    (("zh", "z"), [(h * 4 + z, (1 - h) * 4 + (z + 2) % 4) for h in range(2) for z in range(4)]),
-)
-
-
-def exchanged(value, step):
-    axis, pairs = EXCHANGES[step]
-    return value + lax.ppermute(value, axis, pairs)
+    )(both, half, history0, image, second, x, y, z)
+
+
+PAIRS = ([(0, 1), (1, 0), (2, 3), (3, 2)], [(0, 3), (3, 0), (1, 2), (2, 1)])
+
+
+def across_half(value):
+    pairs = [(h * 4 + z, (1 - h) * 4 + (z + 2) % 4) for h in range(2) for z in range(4)]
+    return lax.ppermute(value, ("zh", "z"), pairs)
 
 
 def on_device(start_block, energies, hamiltonian):
@@ -296,7 +296,7 @@
     weight = jnp.where(block_rows < col, 1.0, jnp.where(block_rows == col, 0.5, 0.0)).astype(
         jnp.float32
     )
-    leads = ((jnp.arange(slots) == z) & (place == row)).astype(jnp.float32)
+    lead = jnp.stack([(place == row).astype(jnp.int32), z])
     bits = jnp.int32(0)
     for r in range(8):
         bits = jnp.where(row == r, jnp.int32(far_bits(r)), bits)
@@ -304,8 +304,8 @@
     slot = jnp.where(far, (z + 2) % 4, z)
     odd = lax.rem(z, 2) == 1
     upper = (z >= 2) != far
-    weight, leads, slot, odd, upper, first = lax.optimization_barrier(
-        (weight, leads, slot, odd, upper, core == 0)
+    weight, lead, slot, odd, upper, first = lax.optimization_barrier(
+        (weight, lead, slot, odd, upper, core == 0)
     )
     in_slot = (jnp.arange(slots) == slot)[:, None, None]
     every = NAMES
@@ -341,7 +341,7 @@
             out_shape=pltpu.VMEM((slots, vecs, width), jnp.float32),
             compiler_params=LIMIT,
             name="across",
-        )(leads, energies.reshape(1, width), own, high, low)
+        )(lead, energies.reshape(1, width), own, high, low)
 
     def total(acrosses, downs, gram=None):
         arrived = lax.ppermute(downs, every, to_row_group())
@@ -351,14 +351,14 @@
         low, high = part[..., :half], part[..., half:]
         mine = jnp.where(first, low, high)
         other = jnp.where(first, high, low)
+        if gram is not None:
+            other_half = across_half(gram)
         mine = mine + lax.ppermute(other, "co", [(0, 1), (1, 0)])
-        if gram is not None:
-            mine, gram = lax.optimization_barrier((mine, exchanged(gram, 0)))
         pieces = lax.all_to_all(mine, ("z", "x"), 0, 0, tiled=True)
         whole = lax.all_to_all(sum_spread(pieces), ("z", "x"), 0, 0, tiled=True)
         if gram is not None:
-            whole, gram = lax.optimization_barrier((whole, gram))
-            gram = exchanged(gram, 1)
+            whole, other_half = lax.optimization_barrier((whole, other_half))
+            gram = gram + other_half
         facing = lax.ppermute(whole, "co", [(0, 1), (1, 0)])
         low = jnp.where(first, whole, facing)
         high = jnp.where(first, facing, whole)
@@ -382,13 +382,13 @@
     acrosses = across(y)
     gram = jnp.concatenate([grams_of(x4_late), grams_of(x4_late, y4_late)], axis=1)
     z4, gram = total(acrosses, downs, gram)
-    gram2, gram = lax.optimization_barrier((grams_of(x4, y4, z4), gram))
-    gram = exchanged(gram, 2)
+    both = jnp.concatenate([grams_of(x4, y4, z4), gram], axis=1)
     zz = lax.ppermute(slot_of(z4), every, from_row_group())
-    for step in range(len(EXCHANGES)):
-        gram2 = exchanged(gram2, step)
+    for pairs in PAIRS:
+        both = both + lax.ppermute(both, "y", pairs)
+    other_half = across_half(both[:, : 3 * vecs])
     length = col_count * width
-    return close(gram, gram2, *begin(gram, length), x, y, zz, length)
+    return close(both, other_half, *begin(both, length), x, y, zz, length)
 
 
 def solution(mesh):

time: 133 us -> 132 us (level)
  blocking collectives: 59.4 us -> 50.6 us
  starting transfers between devices: 17.6 us -> 23.2 us
    all_to_all x2 -> x1, blocking collectives: 23.7 us -> 11.8 us  [total(): whole = lax.all_to_all(sum_spread(pieces), ('z', 'x'), 0, 0, tiled=True)]
    all_to_all x0 -> x1, starting transfers between devices: none -> 4.76 us  [total(): whole = lax.all_to_all(sum_spread(pieces), ('z', 'x'), 0, 0, tiled=True)]
    all_to_all x2, blocking collectives: 35.7 us -> 38.7 us  [total(): pieces = lax.all_to_all(mine, ('z', 'x'), 0, 0, tiled=True)]
    ppermute x6 -> x4, waiting for transfers between devices: 14.5 us -> 11.7 us  [the longest x2 5.87 us: on_device(): both = both + lax.ppermute(both, 'y', pairs)]
    ppermute x2, waiting for transfers between devices: 1.34 us -> 2.67 us  [total(): mine = mine + lax.ppermute(other, 'co', [(0, 1), (1, 0)])]
  transfers between devices with their start and end apart: 17 -> 16, of which waited for: 11 -> 13; matrix products, arithmetic and copies ran while one was open for 1% -> 1% of each run, Pallas kernels for 11% -> 11%
where the time goes in v6:
time: 132 us
  blocking collectives  50.6 us (38%)
  waiting for transfers between devices  34.7 us (26%)
  starting transfers between devices  23.2 us (18%)
  Pallas kernels  20.8 us (16%)
  other arithmetic  1.59 us (1%)
    all_to_all x2, blocking collectives, total(): pieces = lax.all_to_all(mine, ('z', 'x'), 0, 0, tiled=True)  38.7 us
    all_to_all x1, blocking collectives, total(): whole = lax.all_to_all(sum_spread(pieces), ('z', 'x'), 0, 0, tiled=True)  11.8 us
    ppermute x1, waiting for transfers between devices, on_device(): over = lax.ppermute(two, 'z', [(0, 2), (2, 0), (1, 3), (3, 1)])  6.59 us
    ppermute x2, waiting for transfers between devices, on_device(): both = both + lax.ppermute(both, 'y', pairs)  5.87 us
    ppermute x2, waiting for transfers between devices, across_half(): return lax.ppermute(value, ('zh', 'z'), pairs)  5.86 us
    pallas_call x1, Pallas kernels, begin(): pl.pallas_call(functools.partial(first_step, 1.0 / length), in_specs=[IN_...  5.83 us
    ppermute x2, waiting for transfers between devices, total(): arrived = lax.ppermute(downs, every, to_row_group())  4.79 us
    all_to_all x1, starting transfers between devices, total(): whole = lax.all_to_all(sum_spread(pieces), ('z', 'x'), 0, 0, tiled=True)  4.76 us
  transfers between devices with their start and end apart: 16, of which 13 were waited for; matrix products, arithmetic and copies ran while one was open for 1% of the time, Pallas kernels for 11%

profile of v6, /device:TPU:2, one launch (start us, length us, event | category | flops | bytes accessed | tf_op | source)
XLA Modules:
  0.0 131.8 jit_solution(12994318447689595031)
XLA Ops:
  0.6 3.3 %collective-permute-start = (f32[32,512]{1,0:T(8,128)}, f32[32,512]{1,0:T(8,128)S(1)}, u32[]{:S(2)}, u32[]{:S(2)}) collective-permute-start(f32[32,512]{1,0:T(8,128)} %x_ref.1), channel_id=1, source_target_pairs={{0,5},{1,34},{2,64},{3,103},{4,147},{5,180},{6,214},{7,241},{8,13}... | collective-permute-start | bytes 196616 | tf_op jit(solution)/shard_map/ppermute | solution.py:371
  4.5 3.1 %split_blocks.1 = (bf16[2048,512]{1,0:T(8,128)(2,1)S(1)}, bf16[2048,512]{1,0:T(8,128)(2,1)S(1)}) custom-call(f32[4]{0:T(128)} %compare_select_fusion.1.weight_ref, f32[4,512,512]{2,1,0:T(8,128)} %bitcast.24), custom_call_target="tpu_custom_call" | custom-call | tf_op jit(solution)/shard_map/split_blocks/pallas_call | solution.py:313
  7.9 1.9 %collective-permute-start.1 = (f32[32,512]{1,0:T(8,128)S(1)}, f32[32,512]{1,0:T(8,128)S(1)}, u32[]{:S(2)}, u32[]{:S(2)}) collective-permute-start(f32[32,512]{1,0:T(8,128)S(1)} %collective-permute-done), channel_id=1, source_target_pairs={{0,8},{8,0},{16,24},{24,16},{1,9},{9,1},{17,25},{25,17},{2,10},{10... | collective-permute-start | bytes 196616 | tf_op jit(solution)/shard_map/ppermute | solution.py:373
  9.8 3.0 %collective-permute-done.1 = f32[32,512]{1,0:T(8,128)S(1)} collective-permute-done((f32[32,512]{1,0:T(8,128)S(1)}, f32[32,512]{1,0:T(8,128)S(1)}, u32[]{:S(2)}, u32[]{:S(2)}) %collective-permute-start.1) | collective-permute-done | bytes 65568 | tf_op jit(solution)/shard_map/ppermute | solution.py:373
  12.8 3.4 %collective-permute-start.2 = (f32[2,32,512]{2,1,0:T(8,128)S(1)}, f32[2,32,512]{2,1,0:T(8,128)S(1)}, u32[]{:S(2)}, u32[]{:S(2)}) collective-permute-start(f32[2,32,512]{2,1,0:T(8,128)S(1)} %pad_maximum_fusion.3), channel_id=1, source_target_pairs={{0,16},{16,0},{8,24},{24,8},{1,17},{17,1},{9,25},{25,9},{2,18},{18... | collective-permute-start | bytes 393224 | tf_op jit(solution)/shard_map/ppermute | solution.py:375
  16.2 6.6 %collective-permute-done.2 = f32[2,32,512]{2,1,0:T(8,128)S(1)} collective-permute-done((f32[2,32,512]{2,1,0:T(8,128)S(1)}, f32[2,32,512]{2,1,0:T(8,128)S(1)}, u32[]{:S(2)}, u32[]{:S(2)}) %collective-permute-start.2) | collective-permute-done | bytes 131104 | tf_op jit(solution)/shard_map/ppermute | solution.py:375
  23.7 1.9 %across.2 = f32[4,32,512]{2,1,0:T(8,128)S(1)} custom-call(s32[2]{0:T(128)S(1)} %pad_add_fusion.lead_ref, f32[1,512]{1,0:T(1,128)S(1)} %bitcast.22, f32[32,512]{1,0:T(8,128)S(1)} %copy-done, bf16[2048,512]{1,0:T(8,128)(2,1)S(1)} %get-tuple-element.29.high_ref, bf16[2048,512]{1,0:T(8,128)(2,1)S(1)} %get-tuple-element.30.low_ref), custom_call_target="tpu_custom_call" | custom-call | tf_op jit(solution)/shard_map/across/pallas_call | solution.py:337
  25.6 4.8 %collective-permute-done.3 = f32[32,512]{1,0:T(8,128)S(1)} collective-permute-done((f32[32,512]{1,0:T(8,128)S(1)}, f32[32,512]{1,0:T(8,128)S(1)}, u32[]{:S(2)}, u32[]{:S(2)}) %collective-permute-start.3) | collective-permute-done | bytes 65568 | tf_op jit(solution)/shard_map/ppermute | solution.py:347
  30.5 1.3 %collective-permute-done.4 = f32[16,8,256]{2,1,0:T(8,128)S(1)} collective-permute-done((f32[16,8,256]{2,1,0:T(8,128)S(1)}, f32[16,8,256]{2,1,0:T(8,128)S(1)}, u32[]{:S(2)}, u32[]{:S(2)}) %collective-permute-start.4) | collective-permute-done | bytes 131104 | tf_op jit(solution)/shard_map/ppermute | solution.py:356
  31.9 20.0 %all_to_all.20.parts_ref = f32[16,8,256]{2,1,0:T(8,128)S(1)} all-to-all(f32[16,8,256]{2,1,0:T(8,128)S(1)} %select_add_fusion.3), channel_id=1, replica_groups=mesh['zh'=2,'y'=4,'z'=4,'x'=4,'co'=2] {'z','x'}, dimensions={0} | all-to-all | bytes 262144 | tf_op jit(solution)/shard_map/all_to_all | solution.py:357
  52.0 11.8 %all_to_all.21 = f32[16,8,256]{2,1,0:T(8,128)S(1)} all-to-all(f32[16,8,256]{2,1,0:T(8,128)S(1)} %sum_spread.2), channel_id=1, replica_groups=mesh['zh'=2,'y'=4,'z'=4,'x'=4,'co'=2] {'z','x'}, dimensions={0} | all-to-all | bytes 262144 | tf_op jit(solution)/shard_map/all_to_all | solution.py:358
  63.8 1.3 %collective-permute-done.5 = f32[16,8,256]{2,1,0:T(8,128)S(1)} collective-permute-done((f32[16,8,256]{2,1,0:T(8,128)S(1)}, f32[16,8,256]{2,1,0:T(8,128)S(1)}, u32[]{:S(2)}, u32[]{:S(2)}) %collective-permute-start.5) | collective-permute-done | bytes 131104 | tf_op jit(solution)/shard_map/ppermute | solution.py:362
  66.5 4.2 %collective-permute-start.7 = (f32[32,512]{1,0:T(8,128)S(1)}, f32[32,512]{1,0:T(8,128)S(1)}, u32[]{:S(2)}, u32[]{:S(2)}) collective-permute-start(f32[32,512]{1,0:T(8,128)S(1)} %down.3), channel_id=1, source_target_pairs={{0,5},{1,34},{2,64},{3,103},{4,147},{5,180},{6,214},{7,241},{8,13}... | collective-permute-start | bytes 196616 | tf_op jit(solution)/shard_map/ppermute | solution.py:347
  70.7 2.3 %collective-permute-done.6.own_ref.y_ref = f32[32,512]{1,0:T(8,128)S(1)} collective-permute-done((f32[32,512]{1,0:T(8,128)S(1)}, f32[32,512]{1,0:T(8,128)S(1)}, u32[]{:S(2)}, u32[]{:S(2)}) %collective-permute-start.6) | collective-permute-done | bytes 65568 | tf_op jit(solution)/shard_map/ppermute | solution.py:379
  73.0 1.9 %across.3 = f32[4,32,512]{2,1,0:T(8,128)S(1)} custom-call(s32[2]{0:T(128)S(1)} %pad_add_fusion.lead_ref, f32[1,512]{1,0:T(1,128)S(1)} %bitcast.23, f32[32,512]{1,0:T(8,128)S(1)} %collective-permute-done.6.own_ref.y_ref, bf16[2048,512]{1,0:T(8,128)(2,1)S(1)} %get-tuple-element.29.high_ref, bf16[2048,512]{1,0:T(8,128)(2,1)S(1)} %get-tuple-element.30.low_ref), custom_call_target="tpu_custom_call" | custom-call | tf_op jit(solution)/shard_map/across/pallas_call | solution.py:337
  76.4 18.7 %all_to_all.22.parts_ref = f32[16,8,256]{2,1,0:T(8,128)S(1)} all-to-all(f32[16,8,256]{2,1,0:T(8,128)S(1)} %select_add_fusion.2), channel_id=1, replica_groups=mesh['zh'=2,'y'=4,'z'=4,'x'=4,'co'=2] {'z','x'}, dimensions={0} | all-to-all | bytes 262144 | tf_op jit(solution)/shard_map/all_to_all | solution.py:357
  95.8 4.8 %all-to-all-start.3 = ((f32[16,8,256]{2,1,0:T(8,128)}), f32[16,8,256]{2,1,0:T(8,128)S(1)}, u32[]{:S(2)}, u32[]{:S(2)}) async-start(f32[16,8,256]{2,1,0:T(8,128)} %sum_spread.3), calls=%async_computation.3 | async-start | bytes 262144 | tf_op jit(solution)/shard_map/all_to_all | solution.py:358
  101.6 5.8 %collective-permute-done.9 = f32[32,96]{1,0:T(8,128)S(1)} collective-permute-done((f32[32,96]{1,0:T(8,128)S(1)}, f32[32,96]{1,0:T(8,128)S(1)}, u32[]{:S(2)}, u32[]{:S(2)}) %collective-permute-start.9) | collective-permute-done | bytes 12320 | tf_op jit(solution)/shard_map/ppermute | solution.py:281
  110.5 3.9 %collective-permute-done.11 = f32[32,192]{1,0:T(8,128)S(1)} collective-permute-done((f32[32,192]{1,0:T(8,128)S(1)}, f32[32,192]{1,0:T(8,128)S(1)}, u32[]{:S(2)}, u32[]{:S(2)}) %collective-permute-start.11) | collective-permute-done | bytes 24608 | tf_op jit(solution)/shard_map/ppermute | solution.py:388
  114.6 3.0 %collective-permute-start.14 = (f32[32,512]{1,0:T(8,128)S(1)}, f32[32,512]{1,0:T(8,128)S(1)}, u32[]{:S(2)}, u32[]{:S(2)}) collective-permute-start(f32[32,512]{1,0:T(8,128)S(1)} %select_reduce_fusion), channel_id=1, source_target_pairs={{5,0},{34,1},{64,2},{103,3},{147,4},{180,5},{214,6},{241,7},{13,8}... | collective-permute-start | bytes 196616 | tf_op jit(solution)/shard_map/ppermute | solution.py:386
  117.6 2.0 %collective-permute-done.12 = f32[32,192]{1,0:T(8,128)S(1)} collective-permute-done((f32[32,192]{1,0:T(8,128)S(1)}, f32[32,192]{1,0:T(8,128)S(1)}, u32[]{:S(2)}, u32[]{:S(2)}) %collective-permute-start.12) | collective-permute-done | bytes 24608 | tf_op jit(solution)/shard_map/ppermute | solution.py:388
  119.6 2.1 %collective-permute-start.13 = (f32[32,96]{1,0:T(8,128)S(1)}, f32[32,96]{1,0:T(8,128)S(1)}, u32[]{:S(2)}, u32[]{:S(2)}) collective-permute-start(f32[32,96]{1,0:T(8,128)S(1)} %slice.24), channel_id=1, source_target_pairs={{0,144},{8,152},{16,128},{24,136},{128,16},{136,24},{144,0},{152,8... | collective-permute-start | bytes 36872 | tf_op jit(solution)/shard_map/ppermute | solution.py:281
  121.7 5.8 %first_step.1 = (f32[2,32,32]{2,1,0:T(8,128)S(1)}, f32[32,96]{1,0:T(8,128)S(1)}, f32[32,64]{1,0:T(8,128)S(1)}) custom-call(f32[32,192]{1,0:T(8,128)S(1)} %add.61.both_ref), custom_call_target="tpu_custom_call" | custom-call | flops 6000000000 | bytes 100000 | tf_op jit(solution)/shard_map/first_step/pallas_call | solution.py:243
  127.6 4.3 %last_step.1 = (f32[2,2,32,32]{3,2,1,0:T(8,128)}, f32[32,512]{1,0:T(8,128)}) custom-call(f32[32,192]{1,0:T(8,128)S(1)} %add.61.both_ref, f32[32,96]{1,0:T(8,128)S(1)} %collective-permute-done.13.half_ref, f32[2,32,32]{2,1,0:T(8,128)S(1)} %get-tuple-element.37.history0_ref, f32[32,96]{1,0:T(8,128)S(1)} %get-tuple-element.38.image_ref, ...), custom_call_target="tpu_custom_call" | custom-call | tf_op jit(solution)/shard_map/last_step/pallas_call | solution.py:260
  (52 shorter events, 9.9 us)
Async XLA Ops:
  0.6 7.2 %collective-permute-start = (f32[32,512]{1,0:T(8,128)}, f32[32,512]{1,0:T(8,128)S(1)}, u32[]{:S(2)}, u32[]{:S(2)}) collective-permute-start(f32[32,512]{1,0:T(8,128)} %x_ref.1), channel_id=1, source_target_pairs={{0,5},{1,34},{2,64},{3,103},{4,147},{5,180},{6,214},{7,241},{8,13}... | collective-permute-start | bytes 196616 | tf_op jit(solution)/shard_map/ppermute | solution.py:371
  7.9 4.9 %collective-permute-start.1 = (f32[32,512]{1,0:T(8,128)S(1)}, f32[32,512]{1,0:T(8,128)S(1)}, u32[]{:S(2)}, u32[]{:S(2)}) collective-permute-start(f32[32,512]{1,0:T(8,128)S(1)} %collective-permute-done), channel_id=1, source_target_pairs={{0,8},{8,0},{16,24},{24,16},{1,9},{9,1},{17,25},{25,17},{2,10},{10... | collective-permute-start | bytes 196616 | tf_op jit(solution)/shard_map/ppermute | solution.py:373
  12.8 9.9 %collective-permute-start.2 = (f32[2,32,512]{2,1,0:T(8,128)S(1)}, f32[2,32,512]{2,1,0:T(8,128)S(1)}, u32[]{:S(2)}, u32[]{:S(2)}) collective-permute-start(f32[2,32,512]{2,1,0:T(8,128)S(1)} %pad_maximum_fusion.3), channel_id=1, source_target_pairs={{0,16},{16,0},{8,24},{24,8},{1,17},{17,1},{9,25},{25,9},{2,18},{18... | collective-permute-start | bytes 393224 | tf_op jit(solution)/shard_map/ppermute | solution.py:375
  22.8 0.9 copy-start
  22.8 0.9 copy-start.1
  23.6 6.7 %collective-permute-start.3 = (f32[32,512]{1,0:T(8,128)S(1)}, f32[32,512]{1,0:T(8,128)S(1)}, u32[]{:S(2)}, u32[]{:S(2)}) collective-permute-start(f32[32,512]{1,0:T(8,128)S(1)} %down.2), channel_id=1, source_target_pairs={{0,5},{1,34},{2,64},{3,103},{4,147},{5,180},{6,214},{7,241},{8,13}... | collective-permute-start | bytes 196616 | tf_op jit(solution)/shard_map/ppermute | solution.py:347
  30.4 1.4 %collective-permute-start.4 = (f32[16,8,256]{2,1,0:T(8,128)S(1)}, f32[16,8,256]{2,1,0:T(8,128)S(1)}, u32[]{:S(2)}, u32[]{:S(2)}) collective-permute-start(f32[16,8,256]{2,1,0:T(8,128)S(1)} %slice_select_fusion.1), channel_id=1, source_target_pairs={{0,1},{1,0},{2,3},{3,2},{4,5},{5,4},{6,7},{7,6},{8,9},{9,8},{10,11... | collective-permute-start | bytes 393224 | tf_op jit(solution)/shard_map/ppermute | solution.py:356
  63.8 1.3 %collective-permute-start.5 = (f32[16,8,256]{2,1,0:T(8,128)S(1)}, f32[16,8,256]{2,1,0:T(8,128)S(1)}, u32[]{:S(2)}, u32[]{:S(2)}) collective-permute-start(f32[16,8,256]{2,1,0:T(8,128)S(1)} %all_to_all.21), channel_id=1, source_target_pairs={{0,1},{1,0},{2,3},{3,2},{4,5},{5,4},{6,7},{7,6},{8,9},{9,8},{10,11... | collective-permute-start | bytes 393224 | tf_op jit(solution)/shard_map/ppermute | solution.py:362
  65.3 7.6 %collective-permute-start.6 = (f32[32,512]{1,0:T(8,128)S(1)}, f32[32,512]{1,0:T(8,128)S(1)}, u32[]{:S(2)}, u32[]{:S(2)}) collective-permute-start(f32[32,512]{1,0:T(8,128)S(1)} %select_reduce_fusion.1), channel_id=1, source_target_pairs={{5,0},{34,1},{64,2},{103,3},{147,4},{180,5},{214,6},{241,7},{13,8}... | collective-permute-start | bytes 196616 | tf_op jit(solution)/shard_map/ppermute | solution.py:379
  66.5 8.3 %collective-permute-start.7 = (f32[32,512]{1,0:T(8,128)S(1)}, f32[32,512]{1,0:T(8,128)S(1)}, u32[]{:S(2)}, u32[]{:S(2)}) collective-permute-start(f32[32,512]{1,0:T(8,128)S(1)} %down.3), channel_id=1, source_target_pairs={{0,5},{1,34},{2,64},{3,103},{4,147},{5,180},{6,214},{7,241},{8,13}... | collective-permute-start | bytes 196616 | tf_op jit(solution)/shard_map/ppermute | solution.py:347
  75.0 1.4 %collective-permute-start.8 = (f32[16,8,256]{2,1,0:T(8,128)S(1)}, f32[16,8,256]{2,1,0:T(8,128)S(1)}, u32[]{:S(2)}, u32[]{:S(2)}) collective-permute-start(f32[16,8,256]{2,1,0:T(8,128)S(1)} %slice_select_fusion), channel_id=1, source_target_pairs={{0,1},{1,0},{2,3},{3,2},{4,5},{5,4},{6,7},{7,6},{8,9},{9,8},{10,11... | collective-permute-start | bytes 393224 | tf_op jit(solution)/shard_map/ppermute | solution.py:356
  95.8 12.4 %all-to-all-start.3 = ((f32[16,8,256]{2,1,0:T(8,128)}), f32[16,8,256]{2,1,0:T(8,128)S(1)}, u32[]{:S(2)}, u32[]{:S(2)}) async-start(f32[16,8,256]{2,1,0:T(8,128)} %sum_spread.3), calls=%async_computation.3 | async-start | bytes 262144 | tf_op jit(solution)/shard_map/all_to_all | solution.py:358
  101.5 5.9 %collective-permute-start.9 = (f32[32,96]{1,0:T(8,128)S(1)}, f32[32,96]{1,0:T(8,128)S(1)}, u32[]{:S(2)}, u32[]{:S(2)}) collective-permute-start(f32[32,96]{1,0:T(8,128)S(1)} %pad_maximum_fusion.5), channel_id=1, source_target_pairs={{0,144},{8,152},{16,128},{24,136},{128,16},{136,24},{144,0},{152,8... | collective-permute-start | bytes 36872 | tf_op jit(solution)/shard_map/ppermute | solution.py:281
  108.2 1.3 %collective-permute-start.10 = (f32[16,8,256]{2,1,0:T(8,128)S(1)}, f32[16,8,256]{2,1,0:T(8,128)S(1)}, u32[]{:S(2)}, u32[]{:S(2)}) collective-permute-start(f32[16,8,256]{2,1,0:T(8,128)S(1)} %all-to-all-done.3), channel_id=1, source_target_pairs={{0,1},{1,0},{2,3},{3,2},{4,5},{5,4},{6,7},{7,6},{8,9},{9,8},{10,11... | collective-permute-start | bytes 393224 | tf_op jit(solution)/shard_map/ppermute | solution.py:362
  110.4 3.9 %collective-permute-start.11 = (f32[32,192]{1,0:T(8,128)S(1)}, f32[32,192]{1,0:T(8,128)S(1)}, u32[]{:S(2)}, u32[]{:S(2)}) collective-permute-start(f32[32,192]{1,0:T(8,128)S(1)} %pad_maximum_fusion.4), channel_id=1, source_target_pairs={{0,32},{32,0},{64,96},{96,64},{1,33},{33,1},{65,97},{97,65},{2,34}... | collective-permute-start | bytes 73736 | tf_op jit(solution)/shard_map/ppermute | solution.py:388
  114.5 5.2 %collective-permute-start.12 = (f32[32,192]{1,0:T(8,128)S(1)}, f32[32,192]{1,0:T(8,128)S(1)}, u32[]{:S(2)}, u32[]{:S(2)}) collective-permute-start(f32[32,192]{1,0:T(8,128)S(1)} %fusion), channel_id=1, source_target_pairs={{0,96},{96,0},{32,64},{64,32},{1,97},{97,1},{33,65},{65,33},{2,98}... | collective-permute-start | bytes 73736 | tf_op jit(solution)/shard_map/ppermute | solution.py:388
  114.6 13.0 %collective-permute-start.14 = (f32[32,512]{1,0:T(8,128)S(1)}, f32[32,512]{1,0:T(8,128)S(1)}, u32[]{:S(2)}, u32[]{:S(2)}) collective-permute-start(f32[32,512]{1,0:T(8,128)S(1)} %select_reduce_fusion), channel_id=1, source_target_pairs={{5,0},{34,1},{64,2},{103,3},{147,4},{180,5},{214,6},{241,7},{13,8}... | collective-permute-start | bytes 196616 | tf_op jit(solution)/shard_map/ppermute | solution.py:386
  119.6 7.9 %collective-permute-start.13 = (f32[32,96]{1,0:T(8,128)S(1)}, f32[32,96]{1,0:T(8,128)S(1)}, u32[]{:S(2)}, u32[]{:S(2)}) collective-permute-start(f32[32,96]{1,0:T(8,128)S(1)} %slice.24), channel_id=1, source_target_pairs={{0,144},{8,152},{16,128},{24,136},{128,16},{136,24},{144,0},{152,8... | collective-permute-start | bytes 36872 | tf_op jit(solution)/shard_map/ppermute | solution.py:281

commit v7 on v6

--- a/solution.py
+++ b/solution.py
@@ -18,14 +18,14 @@
 COL = ("z", "x", "co")
 
 PLACE = (
-    (5, 3, 2, 4, 7, 1, 0, 6),
-    (2, 4, 5, 3, 0, 6, 7, 1),
-    (0, 1, 7, 6, 2, 3, 5, 4),
-    (7, 0, 4, 6, 2, 3, 1, 5),
-    (3, 5, 4, 2, 1, 0, 6, 7),
-    (4, 2, 3, 5, 1, 0, 6, 7),
-    (6, 0, 1, 7, 4, 2, 3, 5),
-    (1, 7, 6, 0, 3, 5, 4, 2),
+    (5, 3, 1, 7, 4, 2, 0, 6),
+    (2, 4, 6, 0, 3, 5, 7, 1),
+    (3, 1, 7, 5, 2, 0, 6, 4),
+    (0, 2, 4, 6, 1, 3, 5, 7),
+    (0, 2, 4, 6, 1, 3, 5, 7),
+    (3, 1, 7, 5, 2, 0, 6, 4),
+    (6, 0, 2, 4, 7, 1, 3, 5),
+    (1, 7, 5, 3, 0, 6, 4, 2),
 )
 
 
@@ -118,7 +118,7 @@
     history_ref, out_ref, g_ref, p_ref, v_ref,
 ):
     n = both_ref.shape[0]
-    gram2 = (both_ref[:, 0 : 3 * n] + half_ref[...]) * scale
+    gram2 = (both_ref[:, 0 : 3 * n] + half_ref[:, 0 : 3 * n]) * scale
     eye = jnp.where(
         lax.broadcasted_iota(jnp.int32, (n, n), 0) == lax.broadcasted_iota(jnp.int32, (n, n), 1),
         SHIFT,
@@ -372,7 +372,7 @@
     moved, high, low = lax.optimization_barrier((moved, high, low))
     near = lax.ppermute(moved, "z", [(0, 1), (1, 0), (2, 3), (3, 2)])
     two = jnp.stack([jnp.where(odd, near, moved), jnp.where(odd, moved, near)])
-    over = lax.ppermute(two, "z", [(0, 2), (2, 0), (1, 3), (3, 1)])
+    over = lax.ppermute(two, "co", [(0, 1), (1, 0)])
     x4 = jnp.concatenate([jnp.where(upper, over, two), jnp.where(upper, two, over)])
     x = start_block
     y4, _ = total(across(x), down(x4))
@@ -383,10 +383,11 @@
     gram = jnp.concatenate([grams_of(x4_late), grams_of(x4_late, y4_late)], axis=1)
     z4, gram = total(acrosses, downs, gram)
     both = jnp.concatenate([grams_of(x4, y4, z4), gram], axis=1)
-    zz = lax.ppermute(slot_of(z4), every, from_row_group())
     for pairs in PAIRS:
         both = both + lax.ppermute(both, "y", pairs)
-    other_half = across_half(both[:, : 3 * vecs])
+    other_half = across_half(both)
+    mine, both = lax.optimization_barrier((slot_of(z4), both))
+    zz = lax.ppermute(mine, every, from_row_group())
     length = col_count * width
     return close(both, other_half, *begin(both, length), x, y, zz, length)
 

time: 132 us -> 128 us (0.970); the launches traced: 132 us -> 126 us
  blocking collectives: 50.6 us -> 47.8 us
  starting transfers between devices: 23.2 us -> 20.4 us
    ppermute x2, waiting for transfers between devices: 6.6 us -> 1.35 us  [the longest x1 1.33 us: on_device(): over = lax.ppermute(two, 'co', [(0, 1), (1, 0)])]
    ppermute x1, waiting for transfers between devices: 0.23 us -> 3.37 us  [on_device(): moved = lax.ppermute(start_block, every, to_row_group())]
    all_to_all x2, blocking collectives: 38.7 us -> 36 us  [total(): pieces = lax.all_to_all(mine, ('z', 'x'), 0, 0, tiled=True)]
    ppermute x2, starting transfers between devices: 6.4 us -> 3.71 us  [the longest x1 3.61 us: on_device(): zz = lax.ppermute(mine, every, from_row_group())]
    ppermute x2, waiting for transfers between devices: 5.87 us -> 8.57 us  [on_device(): both = both + lax.ppermute(both, 'y', pairs)]
    ppermute x2, waiting for transfers between devices: 4.79 us -> 7.05 us  [total(): arrived = lax.ppermute(downs, every, to_row_group())]
    ppermute x2, starting transfers between devices: 2.1 us -> 0.78 us  [across_half(): return lax.ppermute(value, ('zh', 'z'), pairs)]
  transfers between devices with their start and end apart: 16 -> 16, of which waited for: 13 -> 14; matrix products, arithmetic and copies ran while one was open for 1% -> 1% of each run, Pallas kernels for 11% -> 11%
where the time goes in v7:
time: 128 us; the launch traced here: 126 us
  blocking collectives  47.8 us (37%)
  waiting for transfers between devices  34.9 us (27%)
  Pallas kernels  20.8 us (16%)
  starting transfers between devices  20.4 us (16%)
  other arithmetic  1.58 us (1%)
    all_to_all x2, blocking collectives, total(): pieces = lax.all_to_all(mine, ('z', 'x'), 0, 0, tiled=True)  36 us
    all_to_all x1, blocking collectives, total(): whole = lax.all_to_all(sum_spread(pieces), ('z', 'x'), 0, 0, tiled=True)  11.8 us
    ppermute x2, waiting for transfers between devices, on_device(): both = both + lax.ppermute(both, 'y', pairs)  8.57 us
    ppermute x2, waiting for transfers between devices, total(): arrived = lax.ppermute(downs, every, to_row_group())  7.05 us
    pallas_call x1, Pallas kernels, begin(): pl.pallas_call(functools.partial(first_step, 1.0 / length), in_specs=[IN_...  5.83 us
    ppermute x2, waiting for transfers between devices, across_half(): return lax.ppermute(value, ('zh', 'z'), pairs)  5.13 us
    ppermute x2, starting transfers between devices, total(): arrived = lax.ppermute(downs, every, to_row_group())  4.95 us
    all_to_all x1, starting transfers between devices, total(): whole = lax.all_to_all(sum_spread(pieces), ('z', 'x'), 0, 0, tiled=True)  4.76 us
  transfers between devices with their start and end apart: 16, of which 14 were waited for; matrix products, arithmetic and copies ran while one was open for 1% of the time, Pallas kernels for 11%

profile of v7, /device:TPU:2, one launch (start us, length us, event | category | flops | bytes accessed | tf_op | source)
XLA Modules:
  0.0 126.4 jit_solution(8023203262606499018)
XLA Ops:
  0.6 2.7 %collective-permute-start = (f32[32,512]{1,0:T(8,128)}, f32[32,512]{1,0:T(8,128)S(1)}, u32[]{:S(2)}, u32[]{:S(2)}) collective-permute-start(f32[32,512]{1,0:T(8,128)} %x_ref.1), channel_id=1, source_target_pairs={{0,5},{1,34},{2,67},{3,96},{4,144},{5,179},{6,214},{7,241},{8,13},... | collective-permute-start | bytes 196616 | tf_op jit(solution)/shard_map/ppermute | solution.py:371
  4.0 3.1 %split_blocks.1 = (bf16[2048,512]{1,0:T(8,128)(2,1)S(1)}, bf16[2048,512]{1,0:T(8,128)(2,1)S(1)}) custom-call(f32[4]{0:T(128)} %compare_select_fusion.1.weight_ref, f32[4,512,512]{2,1,0:T(8,128)} %bitcast.24), custom_call_target="tpu_custom_call" | custom-call | tf_op jit(solution)/shard_map/split_blocks/pallas_call | solution.py:313
  7.1 3.4 %collective-permute-done = f32[32,512]{1,0:T(8,128)S(1)} collective-permute-done((f32[32,512]{1,0:T(8,128)}, f32[32,512]{1,0:T(8,128)S(1)}, u32[]{:S(2)}, u32[]{:S(2)}) %collective-permute-start) | collective-permute-done | bytes 65568 | tf_op jit(solution)/shard_map/ppermute | solution.py:371
  10.5 2.8 %collective-permute-start.1 = (f32[32,512]{1,0:T(8,128)S(1)}, f32[32,512]{1,0:T(8,128)S(1)}, u32[]{:S(2)}, u32[]{:S(2)}) collective-permute-start(f32[32,512]{1,0:T(8,128)S(1)} %collective-permute-done), channel_id=1, source_target_pairs={{0,8},{8,0},{16,24},{24,16},{1,9},{9,1},{17,25},{25,17},{2,10},{10... | collective-permute-start | bytes 196616 | tf_op jit(solution)/shard_map/ppermute | solution.py:373
  13.2 2.2 %collective-permute-done.1 = f32[32,512]{1,0:T(8,128)S(1)} collective-permute-done((f32[32,512]{1,0:T(8,128)S(1)}, f32[32,512]{1,0:T(8,128)S(1)}, u32[]{:S(2)}, u32[]{:S(2)}) %collective-permute-start.1) | collective-permute-done | bytes 65568 | tf_op jit(solution)/shard_map/ppermute | solution.py:373
  17.8 1.7 %collective-permute-start.3 = (f32[32,512]{1,0:T(8,128)S(1)}, f32[32,512]{1,0:T(8,128)S(1)}, u32[]{:S(2)}, u32[]{:S(2)}) collective-permute-start(f32[32,512]{1,0:T(8,128)S(1)} %down.2), channel_id=1, source_target_pairs={{0,5},{1,34},{2,67},{3,96},{4,144},{5,179},{6,214},{7,241},{8,13},... | collective-permute-start | bytes 196616 | tf_op jit(solution)/shard_map/ppermute | solution.py:347
  19.5 1.9 %across.2 = f32[4,32,512]{2,1,0:T(8,128)S(1)} custom-call(s32[2]{0:T(128)S(1)} %pad_add_fusion.lead_ref, f32[1,512]{1,0:T(1,128)S(1)} %bitcast.22, f32[32,512]{1,0:T(8,128)S(1)} %copy-done, bf16[2048,512]{1,0:T(8,128)(2,1)S(1)} %get-tuple-element.29.high_ref, bf16[2048,512]{1,0:T(8,128)(2,1)S(1)} %get-tuple-element.30.low_ref), custom_call_target="tpu_custom_call" | custom-call | tf_op jit(solution)/shard_map/across/pallas_call | solution.py:337
  21.4 5.1 %collective-permute-done.3 = f32[32,512]{1,0:T(8,128)S(1)} collective-permute-done((f32[32,512]{1,0:T(8,128)S(1)}, f32[32,512]{1,0:T(8,128)S(1)}, u32[]{:S(2)}, u32[]{:S(2)}) %collective-permute-start.3) | collective-permute-done | bytes 65568 | tf_op jit(solution)/shard_map/ppermute | solution.py:347
  26.7 1.3 %collective-permute-done.4 = f32[16,8,256]{2,1,0:T(8,128)S(1)} collective-permute-done((f32[16,8,256]{2,1,0:T(8,128)S(1)}, f32[16,8,256]{2,1,0:T(8,128)S(1)}, u32[]{:S(2)}, u32[]{:S(2)}) %collective-permute-start.4) | collective-permute-done | bytes 131104 | tf_op jit(solution)/shard_map/ppermute | solution.py:356
  28.1 18.5 %all_to_all.20.parts_ref = f32[16,8,256]{2,1,0:T(8,128)S(1)} all-to-all(f32[16,8,256]{2,1,0:T(8,128)S(1)} %select_add_fusion.3), channel_id=1, replica_groups=mesh['zh'=2,'y'=4,'z'=4,'x'=4,'co'=2] {'z','x'}, dimensions={0} | all-to-all | bytes 262144 | tf_op jit(solution)/shard_map/all_to_all | solution.py:357
  46.6 11.8 %all_to_all.21 = f32[16,8,256]{2,1,0:T(8,128)S(1)} all-to-all(f32[16,8,256]{2,1,0:T(8,128)S(1)} %sum_spread.2), channel_id=1, replica_groups=mesh['zh'=2,'y'=4,'z'=4,'x'=4,'co'=2] {'z','x'}, dimensions={0} | all-to-all | bytes 262144 | tf_op jit(solution)/shard_map/all_to_all | solution.py:358
  58.5 1.3 %collective-permute-done.5 = f32[16,8,256]{2,1,0:T(8,128)S(1)} collective-permute-done((f32[16,8,256]{2,1,0:T(8,128)S(1)}, f32[16,8,256]{2,1,0:T(8,128)S(1)}, u32[]{:S(2)}, u32[]{:S(2)}) %collective-permute-start.5) | collective-permute-done | bytes 131104 | tf_op jit(solution)/shard_map/ppermute | solution.py:362
  60.9 3.3 %collective-permute-start.7 = (f32[32,512]{1,0:T(8,128)S(1)}, f32[32,512]{1,0:T(8,128)S(1)}, u32[]{:S(2)}, u32[]{:S(2)}) collective-permute-start(f32[32,512]{1,0:T(8,128)S(1)} %down.3), channel_id=1, source_target_pairs={{0,5},{1,34},{2,67},{3,96},{4,144},{5,179},{6,214},{7,241},{8,13},... | collective-permute-start | bytes 196616 | tf_op jit(solution)/shard_map/ppermute | solution.py:347
  65.2 1.9 %across.3 = f32[4,32,512]{2,1,0:T(8,128)S(1)} custom-call(s32[2]{0:T(128)S(1)} %pad_add_fusion.lead_ref, f32[1,512]{1,0:T(1,128)S(1)} %bitcast.23, f32[32,512]{1,0:T(8,128)S(1)} %collective-permute-done.6.own_ref.y_ref, bf16[2048,512]{1,0:T(8,128)(2,1)S(1)} %get-tuple-element.29.high_ref, bf16[2048,512]{1,0:T(8,128)(2,1)S(1)} %get-tuple-element.30.low_ref), custom_call_target="tpu_custom_call" | custom-call | tf_op jit(solution)/shard_map/across/pallas_call | solution.py:337
  67.1 2.0 %collective-permute-done.7 = f32[32,512]{1,0:T(8,128)S(1)} collective-permute-done((f32[32,512]{1,0:T(8,128)S(1)}, f32[32,512]{1,0:T(8,128)S(1)}, u32[]{:S(2)}, u32[]{:S(2)}) %collective-permute-start.7) | collective-permute-done | bytes 65568 | tf_op jit(solution)/shard_map/ppermute | solution.py:347
  69.3 1.3 %collective-permute-done.8 = f32[16,8,256]{2,1,0:T(8,128)S(1)} collective-permute-done((f32[16,8,256]{2,1,0:T(8,128)S(1)}, f32[16,8,256]{2,1,0:T(8,128)S(1)}, u32[]{:S(2)}, u32[]{:S(2)}) %collective-permute-start.8) | collective-permute-done | bytes 131104 | tf_op jit(solution)/shard_map/ppermute | solution.py:356
  70.6 17.5 %all_to_all.22.parts_ref = f32[16,8,256]{2,1,0:T(8,128)S(1)} all-to-all(f32[16,8,256]{2,1,0:T(8,128)S(1)} %select_add_fusion.2), channel_id=1, replica_groups=mesh['zh'=2,'y'=4,'z'=4,'x'=4,'co'=2] {'z','x'}, dimensions={0} | all-to-all | bytes 262144 | tf_op jit(solution)/shard_map/all_to_all | solution.py:357
  88.8 4.8 %all-to-all-start.3 = ((f32[16,8,256]{2,1,0:T(8,128)}), f32[16,8,256]{2,1,0:T(8,128)S(1)}, u32[]{:S(2)}, u32[]{:S(2)}) async-start(f32[16,8,256]{2,1,0:T(8,128)} %sum_spread.3), calls=%async_computation.3 | async-start | bytes 262144 | tf_op jit(solution)/shard_map/all_to_all | solution.py:358
  95.3 5.1 %collective-permute-done.9 = f32[32,96]{1,0:T(8,128)S(1)} collective-permute-done((f32[32,96]{1,0:T(8,128)S(1)}, f32[32,96]{1,0:T(8,128)S(1)}, u32[]{:S(2)}, u32[]{:S(2)}) %collective-permute-start.9) | collective-permute-done | bytes 12320 | tf_op jit(solution)/shard_map/ppermute | solution.py:281
  103.8 3.5 %collective-permute-done.11 = f32[32,192]{1,0:T(8,128)S(1)} collective-permute-done((f32[32,192]{1,0:T(8,128)S(1)}, f32[32,192]{1,0:T(8,128)S(1)}, u32[]{:S(2)}, u32[]{:S(2)}) %collective-permute-start.11) | collective-permute-done | bytes 24608 | tf_op jit(solution)/shard_map/ppermute | solution.py:387
  107.6 5.0 %collective-permute-done.12 = f32[32,192]{1,0:T(8,128)S(1)} collective-permute-done((f32[32,192]{1,0:T(8,128)S(1)}, f32[32,192]{1,0:T(8,128)S(1)}, u32[]{:S(2)}, u32[]{:S(2)}) %collective-permute-start.12) | collective-permute-done | bytes 24608 | tf_op jit(solution)/shard_map/ppermute | solution.py:387
  112.6 3.6 %collective-permute-start.14 = (f32[32,512]{1,0:T(8,128)S(1)}, f32[32,512]{1,0:T(8,128)S(1)}, u32[]{:S(2)}, u32[]{:S(2)}) collective-permute-start(f32[32,512]{1,0:T(8,128)S(1)} %select_reduce_fusion), channel_id=1, source_target_pairs={{5,0},{34,1},{67,2},{96,3},{144,4},{179,5},{214,6},{241,7},{13,8},... | collective-permute-start | bytes 196616 | tf_op jit(solution)/shard_map/ppermute | solution.py:390
  116.2 5.8 %first_step.1 = (f32[2,32,32]{2,1,0:T(8,128)S(1)}, f32[32,96]{1,0:T(8,128)S(1)}, f32[32,64]{1,0:T(8,128)S(1)}) custom-call(f32[32,192]{1,0:T(8,128)S(1)} %add.61.both_ref), custom_call_target="tpu_custom_call" | custom-call | flops 6000000000 | bytes 100000 | tf_op jit(solution)/shard_map/first_step/pallas_call | solution.py:243
  122.1 4.3 %last_step.1 = (f32[2,2,32,32]{3,2,1,0:T(8,128)}, f32[32,512]{1,0:T(8,128)}) custom-call(f32[32,192]{1,0:T(8,128)S(1)} %add.61.both_ref, f32[32,192]{1,0:T(8,128)S(1)} %collective-permute-done.13.half_ref, f32[2,32,32]{2,1,0:T(8,128)S(1)} %get-tuple-element.40.history0_ref, f32[32,96]{1,0:T(8,128)S(1)} %get-tuple-element.41.image_ref, ...), custom_call_target="tpu_custom_call" | custom-call | tf_op jit(solution)/shard_map/last_step/pallas_call | solution.py:260
  (51 shorter events, 11.7 us)
Async XLA Ops:
  0.6 9.8 %collective-permute-start = (f32[32,512]{1,0:T(8,128)}, f32[32,512]{1,0:T(8,128)S(1)}, u32[]{:S(2)}, u32[]{:S(2)}) collective-permute-start(f32[32,512]{1,0:T(8,128)} %x_ref.1), channel_id=1, source_target_pairs={{0,5},{1,34},{2,67},{3,96},{4,144},{5,179},{6,214},{7,241},{8,13},... | collective-permute-start | bytes 196616 | tf_op jit(solution)/shard_map/ppermute | solution.py:371
  10.5 5.0 %collective-permute-start.1 = (f32[32,512]{1,0:T(8,128)S(1)}, f32[32,512]{1,0:T(8,128)S(1)}, u32[]{:S(2)}, u32[]{:S(2)}) collective-permute-start(f32[32,512]{1,0:T(8,128)S(1)} %collective-permute-done), channel_id=1, source_target_pairs={{0,8},{8,0},{16,24},{24,16},{1,9},{9,1},{17,25},{25,17},{2,10},{10... | collective-permute-start | bytes 196616 | tf_op jit(solution)/shard_map/ppermute | solution.py:373
  15.5 1.4 %collective-permute-start.2 = (f32[2,32,512]{2,1,0:T(8,128)S(1)}, f32[2,32,512]{2,1,0:T(8,128)S(1)}, u32[]{:S(2)}, u32[]{:S(2)}) collective-permute-start(f32[2,32,512]{2,1,0:T(8,128)S(1)} %pad_maximum_fusion.3), channel_id=1, source_target_pairs={{0,1},{1,0},{2,3},{3,2},{4,5},{5,4},{6,7},{7,6},{8,9},{9,8},{10,11... | collective-permute-start | bytes 393224 | tf_op jit(solution)/shard_map/ppermute | solution.py:375
  17.0 2.5 %copy-start = (f32[32,512]{1,0:T(8,128)S(1)}, f32[32,512]{1,0:T(8,128)}, u32[]{:S(2)}) copy-start(f32[32,512]{1,0:T(8,128)} %x_ref.1) | copy-start | bytes 196612
  17.0 2.5 %copy-start.1 = (f32[512]{0:T(512)S(1)}, f32[512]{0:T(512)}, u32[]{:S(2)}) copy-start(f32[512]{0:T(512)} %param.4) | copy-start | bytes 6148
  17.8 8.7 %collective-permute-start.3 = (f32[32,512]{1,0:T(8,128)S(1)}, f32[32,512]{1,0:T(8,128)S(1)}, u32[]{:S(2)}, u32[]{:S(2)}) collective-permute-start(f32[32,512]{1,0:T(8,128)S(1)} %down.2), channel_id=1, source_target_pairs={{0,5},{1,34},{2,67},{3,96},{4,144},{5,179},{6,214},{7,241},{8,13},... | collective-permute-start | bytes 196616 | tf_op jit(solution)/shard_map/ppermute | solution.py:347
  26.6 1.4 %collective-permute-start.4 = (f32[16,8,256]{2,1,0:T(8,128)S(1)}, f32[16,8,256]{2,1,0:T(8,128)S(1)}, u32[]{:S(2)}, u32[]{:S(2)}) collective-permute-start(f32[16,8,256]{2,1,0:T(8,128)S(1)} %slice_select_fusion.1), channel_id=1, source_target_pairs={{0,1},{1,0},{2,3},{3,2},{4,5},{5,4},{6,7},{7,6},{8,9},{9,8},{10,11... | collective-permute-start | bytes 393224 | tf_op jit(solution)/shard_map/ppermute | solution.py:356
  58.5 1.3 %collective-permute-start.5 = (f32[16,8,256]{2,1,0:T(8,128)S(1)}, f32[16,8,256]{2,1,0:T(8,128)S(1)}, u32[]{:S(2)}, u32[]{:S(2)}) collective-permute-start(f32[16,8,256]{2,1,0:T(8,128)S(1)} %all_to_all.21), channel_id=1, source_target_pairs={{0,1},{1,0},{2,3},{3,2},{4,5},{5,4},{6,7},{7,6},{8,9},{9,8},{10,11... | collective-permute-start | bytes 393224 | tf_op jit(solution)/shard_map/ppermute | solution.py:362
  60.0 5.3 %collective-permute-start.6 = (f32[32,512]{1,0:T(8,128)S(1)}, f32[32,512]{1,0:T(8,128)S(1)}, u32[]{:S(2)}, u32[]{:S(2)}) collective-permute-start(f32[32,512]{1,0:T(8,128)S(1)} %select_reduce_fusion.1), channel_id=1, source_target_pairs={{5,0},{34,1},{67,2},{96,3},{144,4},{179,5},{214,6},{241,7},{13,8},... | collective-permute-start | bytes 196616 | tf_op jit(solution)/shard_map/ppermute | solution.py:379
  60.9 8.2 %collective-permute-start.7 = (f32[32,512]{1,0:T(8,128)S(1)}, f32[32,512]{1,0:T(8,128)S(1)}, u32[]{:S(2)}, u32[]{:S(2)}) collective-permute-start(f32[32,512]{1,0:T(8,128)S(1)} %down.3), channel_id=1, source_target_pairs={{0,5},{1,34},{2,67},{3,96},{4,144},{5,179},{6,214},{7,241},{8,13},... | collective-permute-start | bytes 196616 | tf_op jit(solution)/shard_map/ppermute | solution.py:347
  69.2 1.4 %collective-permute-start.8 = (f32[16,8,256]{2,1,0:T(8,128)S(1)}, f32[16,8,256]{2,1,0:T(8,128)S(1)}, u32[]{:S(2)}, u32[]{:S(2)}) collective-permute-start(f32[16,8,256]{2,1,0:T(8,128)S(1)} %slice_select_fusion), channel_id=1, source_target_pairs={{0,1},{1,0},{2,3},{3,2},{4,5},{5,4},{6,7},{7,6},{8,9},{9,8},{10,11... | collective-permute-start | bytes 393224 | tf_op jit(solution)/shard_map/ppermute | solution.py:356
  88.8 12.4 %all-to-all-start.3 = ((f32[16,8,256]{2,1,0:T(8,128)}), f32[16,8,256]{2,1,0:T(8,128)S(1)}, u32[]{:S(2)}, u32[]{:S(2)}) async-start(f32[16,8,256]{2,1,0:T(8,128)} %sum_spread.3), calls=%async_computation.3 | async-start | bytes 262144 | tf_op jit(solution)/shard_map/all_to_all | solution.py:358
  94.5 5.9 %collective-permute-start.9 = (f32[32,96]{1,0:T(8,128)S(1)}, f32[32,96]{1,0:T(8,128)S(1)}, u32[]{:S(2)}, u32[]{:S(2)}) collective-permute-start(f32[32,96]{1,0:T(8,128)S(1)} %pad_maximum_fusion.5), channel_id=1, source_target_pairs={{0,144},{8,152},{16,128},{24,136},{128,16},{136,24},{144,0},{152,8... | collective-permute-start | bytes 36872 | tf_op jit(solution)/shard_map/ppermute | solution.py:281
  101.2 1.3 %collective-permute-start.10 = (f32[16,8,256]{2,1,0:T(8,128)S(1)}, f32[16,8,256]{2,1,0:T(8,128)S(1)}, u32[]{:S(2)}, u32[]{:S(2)}) collective-permute-start(f32[16,8,256]{2,1,0:T(8,128)S(1)} %all-to-all-done.3), channel_id=1, source_target_pairs={{0,1},{1,0},{2,3},{3,2},{4,5},{5,4},{6,7},{7,6},{8,9},{9,8},{10,11... | collective-permute-start | bytes 393224 | tf_op jit(solution)/shard_map/ppermute | solution.py:362
  103.4 3.9 %collective-permute-start.11 = (f32[32,192]{1,0:T(8,128)S(1)}, f32[32,192]{1,0:T(8,128)S(1)}, u32[]{:S(2)}, u32[]{:S(2)}) collective-permute-start(f32[32,192]{1,0:T(8,128)S(1)} %pad_maximum_fusion.4), channel_id=1, source_target_pairs={{0,32},{32,0},{64,96},{96,64},{1,33},{33,1},{65,97},{97,65},{2,34}... | collective-permute-start | bytes 73736 | tf_op jit(solution)/shard_map/ppermute | solution.py:387
  107.4 5.2 %collective-permute-start.12 = (f32[32,192]{1,0:T(8,128)S(1)}, f32[32,192]{1,0:T(8,128)S(1)}, u32[]{:S(2)}, u32[]{:S(2)}) collective-permute-start(f32[32,192]{1,0:T(8,128)S(1)} %fusion), channel_id=1, source_target_pairs={{0,96},{96,0},{32,64},{64,32},{1,97},{97,1},{33,65},{65,33},{2,98}... | collective-permute-start | bytes 73736 | tf_op jit(solution)/shard_map/ppermute | solution.py:387
  112.6 9.5 %collective-permute-start.13 = (f32[32,192]{1,0:T(8,128)S(1)}, f32[32,192]{1,0:T(8,128)S(1)}, u32[]{:S(2)}, u32[]{:S(2)}) collective-permute-start(f32[32,192]{1,0:T(8,128)S(1)} %add.61.both_ref), channel_id=1, source_target_pairs={{0,144},{8,152},{16,128},{24,136},{128,16},{136,24},{144,0},{152,8... | collective-permute-start | bytes 73736 | tf_op jit(solution)/shard_map/ppermute | solution.py:281
  112.6 9.5 %collective-permute-start.14 = (f32[32,512]{1,0:T(8,128)S(1)}, f32[32,512]{1,0:T(8,128)S(1)}, u32[]{:S(2)}, u32[]{:S(2)}) collective-permute-start(f32[32,512]{1,0:T(8,128)S(1)} %select_reduce_fusion), channel_id=1, source_target_pairs={{5,0},{34,1},{67,2},{96,3},{144,4},{179,5},{214,6},{241,7},{13,8},... | collective-permute-start | bytes 196616 | tf_op jit(solution)/shard_map/ppermute | solution.py:390

commit v8 on v7

--- a/solution.py
+++ b/solution.py
@@ -56,33 +56,56 @@
 
 def factor_and_inverse(g):
     n = g.shape[0]
-    down = lax.broadcasted_iota(jnp.int32, (n, 2 * n), 0)
-    along = lax.broadcasted_iota(jnp.int32, (n, 2 * n), 1)
-    same = (down == along)[:, :n]
+    same = lax.broadcasted_iota(jnp.int32, (n, n), 0) == lax.broadcasted_iota(jnp.int32, (n, n), 1)
     diagonal = jnp.where(same, g, 0.0)
     root = jnp.sqrt(jnp.sum(diagonal, axis=0, keepdims=True))
     root_down = jnp.sqrt(jnp.sum(diagonal, axis=1, keepdims=True))
     wide = jnp.concatenate([g / root, jnp.where(same, 1.0, 0.0)], axis=1) / root_down
-    for k in range(0, n - 2, 2):
-        r0 = jnp.broadcast_to(wide[k : k + 1, :], (8, 2 * n))
-        r1 = jnp.broadcast_to(wide[k + 1 : k + 2, :], (8, 2 * n))
-        a = jnp.broadcast_to(r0[:, k : k + 1], r0.shape)
-        b = jnp.broadcast_to(r0[:, k + 1 : k + 2], r0.shape)
-        c = jnp.broadcast_to(r1[:, k + 1 : k + 2], r0.shape)
-        c0 = jnp.broadcast_to(wide[:, k : k + 1], wide.shape)
-        c1 = jnp.broadcast_to(wide[:, k + 1 : k + 2], wide.shape)
-        det = 1.0 / (a * c - b * b)
-        s0 = jnp.concatenate([(r0 * c - r1 * b) * det] * (n // 8), axis=0)
-        s1 = jnp.concatenate([(r1 * a - r0 * b) * det] * (n // 8), axis=0)
-        wide = jnp.where(down > k + 1, wide - (c0 * s0 + c1 * s1), wide)
-    above = jnp.roll(wide, 1, axis=0)
-    left = down - 1 == along
-    b = jnp.sum(jnp.where(left, wide, 0.0), axis=1, keepdims=True)
-    a = jnp.sum(jnp.where(left, above, 0.0), axis=1, keepdims=True)
-    wide = jnp.where(lax.rem(down, 2) == 1, wide - (b / a) * above, wide)
-    pivot = jnp.sum(jnp.where(down == along, wide, 0.0), axis=1, keepdims=True)
-    wide = wide * (1.0 / jnp.sqrt(pivot))
-    upper = jnp.where(down <= along, wide, 0.0)[:, :n] * root
+    tiles = [wide[8 * b : 8 * b + 8, :] for b in range(n // 8)]
+    solved = [jnp.zeros_like(tile) for tile in tiles]
+    shape = tiles[0].shape
+    down = lax.broadcasted_iota(jnp.int32, shape, 0)
+
+    def lane(tile, k):
+        return jnp.broadcast_to(tile[:, k : k + 1], shape)
+
+    for k in range(0, n, 4):
+        at, first = k // 8, k % 8
+        r0, r1, r2, r3 = (
+            jnp.broadcast_to(tiles[at][first + i : first + i + 1, :], shape) for i in range(4)
+        )
+        a10, a11 = lane(r1, k), lane(r1, k + 1)
+        a20, a21, a22 = lane(r2, k), lane(r2, k + 1), lane(r2, k + 2)
+        a30, a31, a32, a33 = lane(r3, k), lane(r3, k + 1), lane(r3, k + 2), lane(r3, k + 3)
+        d0 = lane(r0, k)
+        i0 = 1.0 / d0
+        m10, m20, m30 = a10 * i0, a20 * i0, a30 * i0
+        d1 = a11 - m10 * a10
+        t21, t31 = a21 - m20 * a10, a31 - m30 * a10
+        i1 = 1.0 / d1
+        m21, m31 = t21 * i1, t31 * i1
+        d2 = a22 - m20 * a20 - m21 * t21
+        t32 = a32 - m30 * a20 - m31 * t21
+        i2 = 1.0 / d2
+        m32 = t32 * i2
+        d3 = a33 - m30 * a30 - m31 * t31 - m32 * t32
+        i3 = 1.0 / d3
+        r1 = r1 - m10 * r0
+        r2 = r2 - m20 * r0 - m21 * r1
+        r3 = r3 - m30 * r0 - m31 * r1 - m32 * r2
+        for i, (row, pivot) in enumerate(((r0, d0), (r1, d1), (r2, d2), (r3, d3))):
+            solved[at] = jnp.where(down == first + i, row * (1.0 / jnp.sqrt(pivot)), solved[at])
+        s0, s1, s2, s3 = r0 * i0, r1 * i1, r2 * i2, r3 * i3
+        for b in range((k + 4) // 8, n // 8):
+            c0, c1, c2, c3 = (lane(tiles[b], k + i) for i in range(4))
+            c1 = c1 - m10 * c0
+            c2 = c2 - m20 * c0 - m21 * c1
+            c3 = c3 - m30 * c0 - m31 * c1 - m32 * c2
+            less = tiles[b] - (c0 * s0 + c1 * s1) - (c2 * s2 + c3 * s3)
+            tiles[b] = jnp.where(down >= 4, less, tiles[b]) if b == at else less
+    wide = jnp.concatenate(solved, axis=0)
+    keep = lax.broadcasted_iota(jnp.int32, (n, n), 0) <= lax.broadcasted_iota(jnp.int32, (n, n), 1)
+    upper = jnp.where(keep, wide[:, :n], 0.0) * root
     return jnp.transpose(upper), wide[:, n:]
 
 
@@ -151,17 +174,22 @@
     return high, (v - high.astype(jnp.float32)).astype(jnp.bfloat16)
 
 
-def split_blocks(weight_ref, blocks_ref, high_ref, low_ref, held, arrived):
+def split_blocks(energies_ref, blocks_ref, high_ref, low_ref, lead_ref, held, arrived):
     slots, width = blocks_ref.shape[0], blocks_ref.shape[1]
     copies = [
         pltpu.make_async_copy(blocks_ref.at[s], held.at[s], arrived.at[s]) for s in range(slots)
     ]
     for copy in copies:
         copy.start()
+    row, col = lax.axis_index(ROW), lax.axis_index(COL)
     for s in range(slots):
+        block_row = row + 8 * s
+        shifted = energies_ref[...] - SHIFT
+        lead_ref[s : s + 1, :] = shifted * jnp.where(block_row == col, 1.0, 0.0)
+        weight = jnp.where(block_row < col, 1.0, jnp.where(block_row == col, 0.5, 0.0))
         copies[s].wait()
         rows = pl.ds(s * width, width)
-        high_ref[rows, :], low_ref[rows, :] = parts_of(held[s] * weight_ref[s])
+        high_ref[rows, :], low_ref[rows, :] = parts_of(held[s] * weight)
 
 
 def dot3(left, high, low, contract):
@@ -184,17 +212,13 @@
     out_ref[...] = total
 
 
-def across_kernel(lead_ref, energies_ref, own_ref, high_ref, low_ref, out_ref):
+def across_kernel(lead_ref, own_ref, high_ref, low_ref, out_ref):
     slots, _, width = out_ref.shape
     left = parts_of(own_ref[...])
     for s in range(slots):
         rows = pl.ds(s * width, width)
         term = dot3(left, high_ref[rows, :], low_ref[rows, :], 1)
-        out_ref[s] = term
-
-    @pl.when(lead_ref[0] == 1)
-    def _():
-        out_ref[lead_ref[1]] += (energies_ref[...] - SHIFT) * own_ref[...]
+        out_ref[s] = term + lead_ref[s : s + 1, :] * own_ref[...]
 
 
 def gram_kernel(*refs):
@@ -292,11 +316,6 @@
     place = lax.axis_index(("x", "co"))
     blocks = hamiltonian[:, 0]
     slots = blocks.shape[0]
-    block_rows = row + 8 * jnp.arange(slots, dtype=jnp.int32)
-    weight = jnp.where(block_rows < col, 1.0, jnp.where(block_rows == col, 0.5, 0.0)).astype(
-        jnp.float32
-    )
-    lead = jnp.stack([(place == row).astype(jnp.int32), z])
     bits = jnp.int32(0)
     for r in range(8):
         bits = jnp.where(row == r, jnp.int32(far_bits(r)), bits)
@@ -304,24 +323,28 @@
     slot = jnp.where(far, (z + 2) % 4, z)
     odd = lax.rem(z, 2) == 1
     upper = (z >= 2) != far
-    weight, lead, slot, odd, upper, first = lax.optimization_barrier(
-        (weight, lead, slot, odd, upper, core == 0)
+    energies, slot, odd, upper, first = lax.optimization_barrier(
+        (energies, slot, odd, upper, core == 0)
     )
     in_slot = (jnp.arange(slots) == slot)[:, None, None]
     every = NAMES
 
-    high, low = pl.pallas_call(
+    high, low, lead = pl.pallas_call(
         split_blocks,
-        in_specs=[pl.BlockSpec(memory_space=pltpu.SMEM), pl.BlockSpec(memory_space=pltpu.HBM)],
-        out_specs=(IN_VMEM, IN_VMEM),
-        out_shape=(pltpu.VMEM((slots * width, width), jnp.bfloat16),) * 2,
+        in_specs=[IN_VMEM, pl.BlockSpec(memory_space=pltpu.HBM)],
+        out_specs=(IN_VMEM, IN_VMEM, IN_VMEM),
+        out_shape=(
+            pltpu.VMEM((slots * width, width), jnp.bfloat16),
+            pltpu.VMEM((slots * width, width), jnp.bfloat16),
+            pltpu.VMEM((slots, width), jnp.float32),
+        ),
         scratch_shapes=[
             pltpu.VMEM(blocks.shape, jnp.float32),
             pltpu.SemaphoreType.DMA((slots,)),
         ],
         compiler_params=pltpu.CompilerParams(vmem_limit_bytes=58 * 2**20),
         name="split_blocks",
-    )(weight, blocks)
+    )(energies.reshape(1, width), blocks)
 
     def down(four):
         return pl.pallas_call(
@@ -336,12 +359,12 @@
     def across(own):
         return pl.pallas_call(
             across_kernel,
-            in_specs=[pl.BlockSpec(memory_space=pltpu.SMEM)] + [IN_VMEM] * 4,
+            in_specs=[IN_VMEM] * 4,
             out_specs=IN_VMEM,
             out_shape=pltpu.VMEM((slots, vecs, width), jnp.float32),
             compiler_params=LIMIT,
             name="across",
-        )(lead, energies.reshape(1, width), own, high, low)
+        )(lead, own, high, low)
 
     def total(acrosses, downs, gram=None):
         arrived = lax.ppermute(downs, every, to_row_group())
@@ -383,11 +406,10 @@
     gram = jnp.concatenate([grams_of(x4_late), grams_of(x4_late, y4_late)], axis=1)
     z4, gram = total(acrosses, downs, gram)
     both = jnp.concatenate([grams_of(x4, y4, z4), gram], axis=1)
+    zz = lax.ppermute(slot_of(z4), every, from_row_group())
     for pairs in PAIRS:
         both = both + lax.ppermute(both, "y", pairs)
     other_half = across_half(both)
-    mine, both = lax.optimization_barrier((slot_of(z4), both))
-    zz = lax.ppermute(mine, every, from_row_group())
     length = col_count * width
     return close(both, other_half, *begin(both, length), x, y, zz, length)
 

time: 128 us -> 123 us (0.961); the launches traced: 126 us -> 123 us
  Pallas kernels: 20.8 us -> 17.3 us
    ppermute x2, waiting for transfers between devices: 8.57 us -> 6.22 us  [on_device(): both = both + lax.ppermute(both, 'y', pairs)]
    ppermute x2, waiting for transfers between devices: 5.13 us -> 6.93 us  [across_half(): return lax.ppermute(value, ('zh', 'z'), pairs)]
    pallas_call x1, Pallas kernels: 5.83 us -> 4.16 us  [begin(): pl.pallas_call(functools.partial(first_step, 1.0 / length), in_specs=[IN_...]
  transfers between devices with their start and end apart: 16 -> 16, of which waited for: 14 -> 15; matrix products, arithmetic and copies ran while one was open for 1% -> 0% of each run, Pallas kernels for 11% -> 9%
where the time goes in v8:
time: 123 us
  blocking collectives  47.8 us (39%)
  waiting for transfers between devices  36.1 us (29%)
  starting transfers between devices  19.8 us (16%)
  Pallas kernels  17.3 us (14%)
    all_to_all x2, blocking collectives, total(): pieces = lax.all_to_all(mine, ('z', 'x'), 0, 0, tiled=True)  35.9 us
    all_to_all x1, blocking collectives, total(): whole = lax.all_to_all(sum_spread(pieces), ('z', 'x'), 0, 0, tiled=True)  11.8 us
    ppermute x2, waiting for transfers between devices, total(): arrived = lax.ppermute(downs, every, to_row_group())  8.07 us
    ppermute x2, waiting for transfers between devices, across_half(): return lax.ppermute(value, ('zh', 'z'), pairs)  6.93 us
    ppermute x2, waiting for transfers between devices, on_device(): both = both + lax.ppermute(both, 'y', pairs)  6.22 us
    ppermute x2, starting transfers between devices, total(): arrived = lax.ppermute(downs, every, to_row_group())  5.01 us
    all_to_all x1, starting transfers between devices, total(): whole = lax.all_to_all(sum_spread(pieces), ('z', 'x'), 0, 0, tiled=True)  4.76 us
    pallas_call x1, Pallas kernels, begin(): pl.pallas_call(functools.partial(first_step, 1.0 / length), in_specs=[IN_...  4.16 us
  transfers between devices with their start and end apart: 16, of which 15 were waited for; matrix products, arithmetic and copies ran while one was open for 0% of the time, Pallas kernels for 9%

profile of v8, /device:TPU:2, one launch (start us, length us, event | category | flops | bytes accessed | tf_op | source)
XLA Modules:
  0.0 122.7 jit_solution(16243651489267281780)
XLA Ops:
  0.6 2.7 %collective-permute-start = (f32[32,512]{1,0:T(8,128)}, f32[32,512]{1,0:T(8,128)S(1)}, u32[]{:S(2)}, u32[]{:S(2)}) collective-permute-start(f32[32,512]{1,0:T(8,128)} %x_ref.1), channel_id=1, source_target_pairs={{0,5},{1,34},{2,67},{3,96},{4,144},{5,179},{6,214},{7,241},{8,13},... | collective-permute-start | bytes 196616 | tf_op jit(solution)/shard_map/ppermute | solution.py:394
  3.3 3.1 %split_blocks.1 = (bf16[2048,512]{1,0:T(8,128)(2,1)S(1)}, bf16[2048,512]{1,0:T(8,128)(2,1)S(1)}, f32[4,512]{1,0:T(4,128)S(1)}) custom-call(f32[1,512]{1,0:T(1,128)} %bitcast.25, f32[4,512,512]{2,1,0:T(8,128)} %bitcast.20), custom_call_target="tpu_custom_call" | custom-call | tf_op jit(solution)/shard_map/split_blocks/pallas_call | solution.py:332
  6.4 4.0 %collective-permute-done = f32[32,512]{1,0:T(8,128)S(1)} collective-permute-done((f32[32,512]{1,0:T(8,128)}, f32[32,512]{1,0:T(8,128)S(1)}, u32[]{:S(2)}, u32[]{:S(2)}) %collective-permute-start) | collective-permute-done | bytes 65568 | tf_op jit(solution)/shard_map/ppermute | solution.py:394
  10.5 2.8 %collective-permute-start.1 = (f32[32,512]{1,0:T(8,128)S(1)}, f32[32,512]{1,0:T(8,128)S(1)}, u32[]{:S(2)}, u32[]{:S(2)}) collective-permute-start(f32[32,512]{1,0:T(8,128)S(1)} %collective-permute-done), channel_id=1, source_target_pairs={{0,8},{8,0},{16,24},{24,16},{1,9},{9,1},{17,25},{25,17},{2,10},{10... | collective-permute-start | bytes 196616 | tf_op jit(solution)/shard_map/ppermute | solution.py:396
  13.2 2.2 %collective-permute-done.1 = f32[32,512]{1,0:T(8,128)S(1)} collective-permute-done((f32[32,512]{1,0:T(8,128)S(1)}, f32[32,512]{1,0:T(8,128)S(1)}, u32[]{:S(2)}, u32[]{:S(2)}) %collective-permute-start.1) | collective-permute-done | bytes 65568 | tf_op jit(solution)/shard_map/ppermute | solution.py:396
  15.6 1.3 %collective-permute-done.2 = f32[2,32,512]{2,1,0:T(8,128)S(1)} collective-permute-done((f32[2,32,512]{2,1,0:T(8,128)S(1)}, f32[2,32,512]{2,1,0:T(8,128)S(1)}, u32[]{:S(2)}, u32[]{:S(2)}) %collective-permute-start.2) | collective-permute-done | bytes 131104 | tf_op jit(solution)/shard_map/ppermute | solution.py:398
  17.8 1.8 %collective-permute-start.3 = (f32[32,512]{1,0:T(8,128)S(1)}, f32[32,512]{1,0:T(8,128)S(1)}, u32[]{:S(2)}, u32[]{:S(2)}) collective-permute-start(f32[32,512]{1,0:T(8,128)S(1)} %down.2), channel_id=1, source_target_pairs={{0,5},{1,34},{2,67},{3,96},{4,144},{5,179},{6,214},{7,241},{8,13},... | collective-permute-start | bytes 196616 | tf_op jit(solution)/shard_map/ppermute | solution.py:370
  20.9 5.6 %collective-permute-done.3 = f32[32,512]{1,0:T(8,128)S(1)} collective-permute-done((f32[32,512]{1,0:T(8,128)S(1)}, f32[32,512]{1,0:T(8,128)S(1)}, u32[]{:S(2)}, u32[]{:S(2)}) %collective-permute-start.3) | collective-permute-done | bytes 65568 | tf_op jit(solution)/shard_map/ppermute | solution.py:370
  26.7 1.3 %collective-permute-done.4 = f32[16,8,256]{2,1,0:T(8,128)S(1)} collective-permute-done((f32[16,8,256]{2,1,0:T(8,128)S(1)}, f32[16,8,256]{2,1,0:T(8,128)S(1)}, u32[]{:S(2)}, u32[]{:S(2)}) %collective-permute-start.4) | collective-permute-done | bytes 131104 | tf_op jit(solution)/shard_map/ppermute | solution.py:379
  28.1 18.5 %all_to_all.20.parts_ref = f32[16,8,256]{2,1,0:T(8,128)S(1)} all-to-all(f32[16,8,256]{2,1,0:T(8,128)S(1)} %select_add_fusion.3), channel_id=1, replica_groups=mesh['zh'=2,'y'=4,'z'=4,'x'=4,'co'=2] {'z','x'}, dimensions={0} | all-to-all | bytes 262144 | tf_op jit(solution)/shard_map/all_to_all | solution.py:380
  46.6 11.8 %all_to_all.21 = f32[16,8,256]{2,1,0:T(8,128)S(1)} all-to-all(f32[16,8,256]{2,1,0:T(8,128)S(1)} %sum_spread.2), channel_id=1, replica_groups=mesh['zh'=2,'y'=4,'z'=4,'x'=4,'co'=2] {'z','x'}, dimensions={0} | all-to-all | bytes 262144 | tf_op jit(solution)/shard_map/all_to_all | solution.py:381
  58.5 1.3 %collective-permute-done.5 = f32[16,8,256]{2,1,0:T(8,128)S(1)} collective-permute-done((f32[16,8,256]{2,1,0:T(8,128)S(1)}, f32[16,8,256]{2,1,0:T(8,128)S(1)}, u32[]{:S(2)}, u32[]{:S(2)}) %collective-permute-start.5) | collective-permute-done | bytes 131104 | tf_op jit(solution)/shard_map/ppermute | solution.py:385
  60.9 3.3 %collective-permute-start.7 = (f32[32,512]{1,0:T(8,128)S(1)}, f32[32,512]{1,0:T(8,128)S(1)}, u32[]{:S(2)}, u32[]{:S(2)}) collective-permute-start(f32[32,512]{1,0:T(8,128)S(1)} %down.3), channel_id=1, source_target_pairs={{0,5},{1,34},{2,67},{3,96},{4,144},{5,179},{6,214},{7,241},{8,13},... | collective-permute-start | bytes 196616 | tf_op jit(solution)/shard_map/ppermute | solution.py:370
  66.6 2.5 %collective-permute-done.7 = f32[32,512]{1,0:T(8,128)S(1)} collective-permute-done((f32[32,512]{1,0:T(8,128)S(1)}, f32[32,512]{1,0:T(8,128)S(1)}, u32[]{:S(2)}, u32[]{:S(2)}) %collective-permute-start.7) | collective-permute-done | bytes 65568 | tf_op jit(solution)/shard_map/ppermute | solution.py:370
  69.3 1.3 %collective-permute-done.8 = f32[16,8,256]{2,1,0:T(8,128)S(1)} collective-permute-done((f32[16,8,256]{2,1,0:T(8,128)S(1)}, f32[16,8,256]{2,1,0:T(8,128)S(1)}, u32[]{:S(2)}, u32[]{:S(2)}) %collective-permute-start.8) | collective-permute-done | bytes 131104 | tf_op jit(solution)/shard_map/ppermute | solution.py:379
  70.6 17.4 %all_to_all.22.parts_ref = f32[16,8,256]{2,1,0:T(8,128)S(1)} all-to-all(f32[16,8,256]{2,1,0:T(8,128)S(1)} %select_add_fusion.2), channel_id=1, replica_groups=mesh['zh'=2,'y'=4,'z'=4,'x'=4,'co'=2] {'z','x'}, dimensions={0} | all-to-all | bytes 262144 | tf_op jit(solution)/shard_map/all_to_all | solution.py:380
  88.8 4.8 %all-to-all-start.3 = ((f32[16,8,256]{2,1,0:T(8,128)}), f32[16,8,256]{2,1,0:T(8,128)S(1)}, u32[]{:S(2)}, u32[]{:S(2)}) async-start(f32[16,8,256]{2,1,0:T(8,128)} %sum_spread.3), calls=%async_computation.3 | async-start | bytes 262144 | tf_op jit(solution)/shard_map/all_to_all | solution.py:381
  95.3 5.1 %collective-permute-done.9 = f32[32,96]{1,0:T(8,128)S(1)} collective-permute-done((f32[32,96]{1,0:T(8,128)S(1)}, f32[32,96]{1,0:T(8,128)S(1)}, u32[]{:S(2)}, u32[]{:S(2)}) %collective-permute-start.9) | collective-permute-done | bytes 12320 | tf_op jit(solution)/shard_map/ppermute | solution.py:305
  103.8 3.6 %collective-permute-done.11 = f32[32,192]{1,0:T(8,128)S(1)} collective-permute-done((f32[32,192]{1,0:T(8,128)S(1)}, f32[32,192]{1,0:T(8,128)S(1)}, u32[]{:S(2)}, u32[]{:S(2)}) %collective-permute-start.11) | collective-permute-done | bytes 24608 | tf_op jit(solution)/shard_map/ppermute | solution.py:411
  107.6 3.0 %collective-permute-start.14 = (f32[32,512]{1,0:T(8,128)S(1)}, f32[32,512]{1,0:T(8,128)S(1)}, u32[]{:S(2)}, u32[]{:S(2)}) collective-permute-start(f32[32,512]{1,0:T(8,128)S(1)} %select_reduce_fusion), channel_id=1, source_target_pairs={{5,0},{34,1},{67,2},{96,3},{144,4},{179,5},{214,6},{241,7},{13,8},... | collective-permute-start | bytes 196616 | tf_op jit(solution)/shard_map/ppermute | solution.py:409
  110.5 2.7 %collective-permute-done.12 = f32[32,192]{1,0:T(8,128)S(1)} collective-permute-done((f32[32,192]{1,0:T(8,128)S(1)}, f32[32,192]{1,0:T(8,128)S(1)}, u32[]{:S(2)}, u32[]{:S(2)}) %collective-permute-start.12) | collective-permute-done | bytes 24608 | tf_op jit(solution)/shard_map/ppermute | solution.py:411
  113.2 4.2 %first_step.1 = (f32[2,32,32]{2,1,0:T(8,128)S(1)}, f32[32,96]{1,0:T(8,128)S(1)}, f32[32,64]{1,0:T(8,128)S(1)}) custom-call(f32[32,192]{1,0:T(8,128)S(1)} %add.48.both_ref), custom_call_target="tpu_custom_call" | custom-call | flops 6000000000 | bytes 100000 | tf_op jit(solution)/shard_map/first_step/pallas_call | solution.py:267
  117.4 1.8 %collective-permute-done.13.half_ref = f32[32,192]{1,0:T(8,128)S(1)} collective-permute-done((f32[32,192]{1,0:T(8,128)S(1)}, f32[32,192]{1,0:T(8,128)S(1)}, u32[]{:S(2)}, u32[]{:S(2)}) %collective-permute-start.13) | collective-permute-done | bytes 24608 | tf_op jit(solution)/shard_map/ppermute | solution.py:305
  119.3 3.4 %last_step.1 = (f32[2,2,32,32]{3,2,1,0:T(8,128)}, f32[32,512]{1,0:T(8,128)}) custom-call(f32[32,192]{1,0:T(8,128)S(1)} %add.48.both_ref, f32[32,192]{1,0:T(8,128)S(1)} %collective-permute-done.13.half_ref, f32[2,32,32]{2,1,0:T(8,128)S(1)} %get-tuple-element.37.history0_ref, f32[32,96]{1,0:T(8,128)S(1)} %get-tuple-element.38.image_ref, ...), custom_call_target="tpu_custom_call" | custom-call | tf_op jit(solution)/shard_map/last_step/pallas_call | solution.py:284
  (47 shorter events, 12.3 us)
Async XLA Ops:
  0.6 9.8 %collective-permute-start = (f32[32,512]{1,0:T(8,128)}, f32[32,512]{1,0:T(8,128)S(1)}, u32[]{:S(2)}, u32[]{:S(2)}) collective-permute-start(f32[32,512]{1,0:T(8,128)} %x_ref.1), channel_id=1, source_target_pairs={{0,5},{1,34},{2,67},{3,96},{4,144},{5,179},{6,214},{7,241},{8,13},... | collective-permute-start | bytes 196616 | tf_op jit(solution)/shard_map/ppermute | solution.py:394
  10.5 5.0 %collective-permute-start.1 = (f32[32,512]{1,0:T(8,128)S(1)}, f32[32,512]{1,0:T(8,128)S(1)}, u32[]{:S(2)}, u32[]{:S(2)}) collective-permute-start(f32[32,512]{1,0:T(8,128)S(1)} %collective-permute-done), channel_id=1, source_target_pairs={{0,8},{8,0},{16,24},{24,16},{1,9},{9,1},{17,25},{25,17},{2,10},{10... | collective-permute-start | bytes 196616 | tf_op jit(solution)/shard_map/ppermute | solution.py:396
  15.5 1.4 %collective-permute-start.2 = (f32[2,32,512]{2,1,0:T(8,128)S(1)}, f32[2,32,512]{2,1,0:T(8,128)S(1)}, u32[]{:S(2)}, u32[]{:S(2)}) collective-permute-start(f32[2,32,512]{2,1,0:T(8,128)S(1)} %pad_maximum_fusion.3), channel_id=1, source_target_pairs={{0,1},{1,0},{2,3},{3,2},{4,5},{5,4},{6,7},{7,6},{8,9},{9,8},{10,11... | collective-permute-start | bytes 393224 | tf_op jit(solution)/shard_map/ppermute | solution.py:398
  17.0 2.6 %copy-start = (f32[32,512]{1,0:T(8,128)S(1)}, f32[32,512]{1,0:T(8,128)}, u32[]{:S(2)}) copy-start(f32[32,512]{1,0:T(8,128)} %x_ref.1) | copy-start | bytes 196612
  17.8 8.7 %collective-permute-start.3 = (f32[32,512]{1,0:T(8,128)S(1)}, f32[32,512]{1,0:T(8,128)S(1)}, u32[]{:S(2)}, u32[]{:S(2)}) collective-permute-start(f32[32,512]{1,0:T(8,128)S(1)} %down.2), channel_id=1, source_target_pairs={{0,5},{1,34},{2,67},{3,96},{4,144},{5,179},{6,214},{7,241},{8,13},... | collective-permute-start | bytes 196616 | tf_op jit(solution)/shard_map/ppermute | solution.py:370
  26.6 1.4 %collective-permute-start.4 = (f32[16,8,256]{2,1,0:T(8,128)S(1)}, f32[16,8,256]{2,1,0:T(8,128)S(1)}, u32[]{:S(2)}, u32[]{:S(2)}) collective-permute-start(f32[16,8,256]{2,1,0:T(8,128)S(1)} %slice_select_fusion.1), channel_id=1, source_target_pairs={{0,1},{1,0},{2,3},{3,2},{4,5},{5,4},{6,7},{7,6},{8,9},{9,8},{10,11... | collective-permute-start | bytes 393224 | tf_op jit(solution)/shard_map/ppermute | solution.py:379
  58.5 1.3 %collective-permute-start.5 = (f32[16,8,256]{2,1,0:T(8,128)S(1)}, f32[16,8,256]{2,1,0:T(8,128)S(1)}, u32[]{:S(2)}, u32[]{:S(2)}) collective-permute-start(f32[16,8,256]{2,1,0:T(8,128)S(1)} %all_to_all.21), channel_id=1, source_target_pairs={{0,1},{1,0},{2,3},{3,2},{4,5},{5,4},{6,7},{7,6},{8,9},{9,8},{10,11... | collective-permute-start | bytes 393224 | tf_op jit(solution)/shard_map/ppermute | solution.py:385
  59.9 5.3 %collective-permute-start.6 = (f32[32,512]{1,0:T(8,128)S(1)}, f32[32,512]{1,0:T(8,128)S(1)}, u32[]{:S(2)}, u32[]{:S(2)}) collective-permute-start(f32[32,512]{1,0:T(8,128)S(1)} %select_reduce_fusion.1), channel_id=1, source_target_pairs={{5,0},{34,1},{67,2},{96,3},{144,4},{179,5},{214,6},{241,7},{13,8},... | collective-permute-start | bytes 196616 | tf_op jit(solution)/shard_map/ppermute | solution.py:402
  60.9 8.2 %collective-permute-start.7 = (f32[32,512]{1,0:T(8,128)S(1)}, f32[32,512]{1,0:T(8,128)S(1)}, u32[]{:S(2)}, u32[]{:S(2)}) collective-permute-start(f32[32,512]{1,0:T(8,128)S(1)} %down.3), channel_id=1, source_target_pairs={{0,5},{1,34},{2,67},{3,96},{4,144},{5,179},{6,214},{7,241},{8,13},... | collective-permute-start | bytes 196616 | tf_op jit(solution)/shard_map/ppermute | solution.py:370
  69.2 1.4 %collective-permute-start.8 = (f32[16,8,256]{2,1,0:T(8,128)S(1)}, f32[16,8,256]{2,1,0:T(8,128)S(1)}, u32[]{:S(2)}, u32[]{:S(2)}) collective-permute-start(f32[16,8,256]{2,1,0:T(8,128)S(1)} %slice_select_fusion), channel_id=1, source_target_pairs={{0,1},{1,0},{2,3},{3,2},{4,5},{5,4},{6,7},{7,6},{8,9},{9,8},{10,11... | collective-permute-start | bytes 393224 | tf_op jit(solution)/shard_map/ppermute | solution.py:379
  88.8 12.4 %all-to-all-start.3 = ((f32[16,8,256]{2,1,0:T(8,128)}), f32[16,8,256]{2,1,0:T(8,128)S(1)}, u32[]{:S(2)}, u32[]{:S(2)}) async-start(f32[16,8,256]{2,1,0:T(8,128)} %sum_spread.3), calls=%async_computation.3 | async-start | bytes 262144 | tf_op jit(solution)/shard_map/all_to_all | solution.py:381
  94.5 5.9 %collective-permute-start.9 = (f32[32,96]{1,0:T(8,128)S(1)}, f32[32,96]{1,0:T(8,128)S(1)}, u32[]{:S(2)}, u32[]{:S(2)}) collective-permute-start(f32[32,96]{1,0:T(8,128)S(1)} %pad_maximum_fusion.5), channel_id=1, source_target_pairs={{0,144},{8,152},{16,128},{24,136},{128,16},{136,24},{144,0},{152,8... | collective-permute-start | bytes 36872 | tf_op jit(solution)/shard_map/ppermute | solution.py:305
  101.2 1.3 %collective-permute-start.10 = (f32[16,8,256]{2,1,0:T(8,128)S(1)}, f32[16,8,256]{2,1,0:T(8,128)S(1)}, u32[]{:S(2)}, u32[]{:S(2)}) collective-permute-start(f32[16,8,256]{2,1,0:T(8,128)S(1)} %all-to-all-done.3), channel_id=1, source_target_pairs={{0,1},{1,0},{2,3},{3,2},{4,5},{5,4},{6,7},{7,6},{8,9},{9,8},{10,11... | collective-permute-start | bytes 393224 | tf_op jit(solution)/shard_map/ppermute | solution.py:385
  103.4 3.9 %collective-permute-start.11 = (f32[32,192]{1,0:T(8,128)S(1)}, f32[32,192]{1,0:T(8,128)S(1)}, u32[]{:S(2)}, u32[]{:S(2)}) collective-permute-start(f32[32,192]{1,0:T(8,128)S(1)} %pad_maximum_fusion.4), channel_id=1, source_target_pairs={{0,32},{32,0},{64,96},{96,64},{1,33},{33,1},{65,97},{97,65},{2,34}... | collective-permute-start | bytes 73736 | tf_op jit(solution)/shard_map/ppermute | solution.py:411
  107.4 5.8 %collective-permute-start.12 = (f32[32,192]{1,0:T(8,128)S(1)}, f32[32,192]{1,0:T(8,128)S(1)}, u32[]{:S(2)}, u32[]{:S(2)}) collective-permute-start(f32[32,192]{1,0:T(8,128)S(1)} %fusion), channel_id=1, source_target_pairs={{0,96},{96,0},{32,64},{64,32},{1,97},{97,1},{33,65},{65,33},{2,98}... | collective-permute-start | bytes 73736 | tf_op jit(solution)/shard_map/ppermute | solution.py:411
  107.6 9.9 %collective-permute-start.14 = (f32[32,512]{1,0:T(8,128)S(1)}, f32[32,512]{1,0:T(8,128)S(1)}, u32[]{:S(2)}, u32[]{:S(2)}) collective-permute-start(f32[32,512]{1,0:T(8,128)S(1)} %select_reduce_fusion), channel_id=1, source_target_pairs={{5,0},{34,1},{67,2},{96,3},{144,4},{179,5},{214,6},{241,7},{13,8},... | collective-permute-start | bytes 196616 | tf_op jit(solution)/shard_map/ppermute | solution.py:409
  113.2 6.1 %collective-permute-start.13 = (f32[32,192]{1,0:T(8,128)S(1)}, f32[32,192]{1,0:T(8,128)S(1)}, u32[]{:S(2)}, u32[]{:S(2)}) collective-permute-start(f32[32,192]{1,0:T(8,128)S(1)} %add.48.both_ref), channel_id=1, source_target_pairs={{0,144},{8,152},{16,128},{24,136},{128,16},{136,24},{144,0},{152,8... | collective-permute-start | bytes 73736 | tf_op jit(solution)/shard_map/ppermute | solution.py:305

commit v9 on v8

--- a/solution.py
+++ b/solution.py
@@ -109,7 +109,7 @@
     return jnp.transpose(upper), wide[:, n:]
 
 
-def first_step(scale, both_ref, history_ref, first_ref, second_ref):
+def first_step(scale, both_ref, history_ref, first_ref, second_ref, own_ref):
     n = both_ref.shape[0]
     g00 = both_ref[:, 3 * n : 4 * n] * scale
     g10 = both_ref[:, 4 * n : 5 * n] * scale
@@ -130,6 +130,7 @@
     history_ref[1] = low1
     q1 = mm(t1, p1)
     second_ref[...] = q1
+    own_ref[...] = mmt(mm(q1, whole), q1)
     first_ref[:, 0:n] = -lax.dot_general(
         low1, t0, (((0,), (0,)), ((), ())), precision=FULL, preferred_element_type=jnp.float32
     )
@@ -137,8 +138,8 @@
 
 
 def last_step(
-    scale, both_ref, half_ref, history0_ref, image_ref, second_ref, x_ref, y_ref, z_ref,
-    history_ref, out_ref, g_ref, p_ref, v_ref,
+    scale, both_ref, half_ref, history0_ref, image_ref, second_ref, own_ref, x_ref, y_ref, z_ref,
+    history_ref, out_ref, g_ref, p_ref, v_ref, s_ref,
 ):
     n = both_ref.shape[0]
     gram2 = (both_ref[:, 0 : 3 * n] + half_ref[:, 0 : 3 * n]) * scale
@@ -157,12 +158,16 @@
     history_ref[0, 1] = history0_ref[1]
     w1 = image_ref[...]
     q1 = second_ref[...]
-    a1 = mmt(mm(w1, g_ref[:, 0 : 2 * n]), q1)
+    against = mm(w1, g_ref[...])
+    a1 = mmt(against[:, 0 : 2 * n], q1)
     history_ref[1, 0] = a1 + eye
+    s_ref[0:n] = mmt(against, w1)
+    s_ref[n : 2 * n] = mm(a1, own_ref[...])
+    s_ref[2 * n :] = mmt(a1 + a1 - s_ref[n : 2 * n], a1)
+    low2, t2 = factor_and_inverse(s_ref[0:n] - s_ref[2 * n :])
+    history_ref[1, 1] = low2
     p_ref[...] = mm(a1, q1)
     w1 = jnp.concatenate([w1[:, 0 : 2 * n] - p_ref[...], w1[:, 2 * n :]], axis=1)
-    low2, t2 = factor_and_inverse(mmt(mm(w1, g_ref[...]), w1))
-    history_ref[1, 1] = low2
     v_ref[0:n] = x_ref[...]
     v_ref[n : 2 * n] = y_ref[...]
     v_ref[2 * n :] = z_ref[...]
@@ -262,16 +267,32 @@
     )(parts)
 
 
+def plus_kernel(left_ref, right_ref, out_ref):
+    out_ref[...] = left_ref[...] + right_ref[...]
+
+
+def plus(left, right):
+    return pl.pallas_call(
+        plus_kernel,
+        in_specs=[IN_VMEM] * 2,
+        out_specs=IN_VMEM,
+        out_shape=pltpu.VMEM(left.shape, jnp.float32),
+        compiler_params=LIMIT,
+        name="plus",
+    )(left, right)
+
+
 def begin(both, length):
     vecs = both.shape[0]
     return pl.pallas_call(
         functools.partial(first_step, 1.0 / length),
         in_specs=[IN_VMEM],
-        out_specs=(IN_VMEM,) * 3,
+        out_specs=(IN_VMEM,) * 4,
         out_shape=(
             pltpu.VMEM((2, vecs, vecs), jnp.float32),
             pltpu.VMEM((vecs, 3 * vecs), jnp.float32),
             pltpu.VMEM((vecs, 2 * vecs), jnp.float32),
+            pltpu.VMEM((vecs, vecs), jnp.float32),
         ),
         compiler_params=LIMIT,
         cost_estimate=pl.CostEstimate(flops=6 * 10**9, bytes_accessed=10**5, transcendentals=0),
@@ -279,7 +300,7 @@
     )(both)
 
 
-def close(both, half, history0, image, second, x, y, z, length):
+def close(both, half, history0, image, second, own, x, y, z, length):
     vecs = x.shape[0]
     return pl.pallas_call(
         functools.partial(last_step, 1.0 / length),
@@ -291,10 +312,11 @@
             pltpu.VMEM((3 * vecs, 3 * vecs), jnp.float32),
             pltpu.VMEM((vecs, 2 * vecs), jnp.float32),
             pltpu.VMEM((3 * vecs, x.shape[1]), jnp.float32),
+            pltpu.VMEM((3 * vecs, vecs), jnp.float32),
         ],
         compiler_params=LIMIT,
         name="last_step",
-    )(both, half, history0, image, second, x, y, z)
+    )(both, half, history0, image, second, own, x, y, z)
 
 
 PAIRS = ([(0, 1), (1, 0), (2, 3), (3, 2)], [(0, 3), (3, 0), (1, 2), (2, 1)])
@@ -408,7 +430,7 @@
     both = jnp.concatenate([grams_of(x4, y4, z4), gram], axis=1)
     zz = lax.ppermute(slot_of(z4), every, from_row_group())
     for pairs in PAIRS:
-        both = both + lax.ppermute(both, "y", pairs)
+        both = plus(both, lax.ppermute(both, "y", pairs))
     other_half = across_half(both)
     length = col_count * width
     return close(both, other_half, *begin(both, length), x, y, zz, length)

time: 123 us -> 123 us (level)
  transfers between devices with their start and end apart: 16 -> 16, of which waited for: 15 -> 15; matrix products, arithmetic and copies ran while one was open for 0% -> 0% of each run, Pallas kernels for 9% -> 10%
where the time goes in v9:
time: 123 us; the launch traced here: 122 us
  blocking collectives  47.8 us (39%)
  waiting for transfers between devices  35.8 us (29%)
  starting transfers between devices  19.8 us (16%)
  Pallas kernels  17.4 us (14%)
    all_to_all x2, blocking collectives, total(): pieces = lax.all_to_all(mine, ('z', 'x'), 0, 0, tiled=True)  35.9 us
    all_to_all x1, blocking collectives, total(): whole = lax.all_to_all(sum_spread(pieces), ('z', 'x'), 0, 0, tiled=True)  11.8 us
    ppermute x2, waiting for transfers between devices, total(): arrived = lax.ppermute(downs, every, to_row_group())  8.07 us
    ppermute x2, waiting for transfers between devices, across_half(): return lax.ppermute(value, ('zh', 'z'), pairs)  6.69 us
    ppermute x2, waiting for transfers between devices, on_device(): both = plus(both, lax.ppermute(both, 'y', pairs))  6.22 us
    ppermute x2, starting transfers between devices, total(): arrived = lax.ppermute(downs, every, to_row_group())  5.01 us
    all_to_all x1, starting transfers between devices, total(): whole = lax.all_to_all(sum_spread(pieces), ('z', 'x'), 0, 0, tiled=True)  4.76 us
    pallas_call x1, Pallas kernels, begin(): pl.pallas_call(functools.partial(first_step, 1.0 / length), in_specs=[IN_...  4.45 us
  transfers between devices with their start and end apart: 16, of which 15 were waited for; matrix products, arithmetic and copies ran while one was open for 0% of the time, Pallas kernels for 10%

profile of v9, /device:TPU:2, one launch (start us, length us, event | category | flops | bytes accessed | tf_op | source)
XLA Modules:
  0.0 122.4 jit_solution(3449476367382663073)
XLA Ops:
  0.6 2.7 %collective-permute-start = (f32[32,512]{1,0:T(8,128)}, f32[32,512]{1,0:T(8,128)S(1)}, u32[]{:S(2)}, u32[]{:S(2)}) collective-permute-start(f32[32,512]{1,0:T(8,128)} %x_ref.1), channel_id=1, source_target_pairs={{0,5},{1,34},{2,67},{3,96},{4,144},{5,179},{6,214},{7,241},{8,13},... | collective-permute-start | bytes 196616 | tf_op jit(solution)/shard_map/ppermute | solution.py:416
  3.3 3.1 %split_blocks.1 = (bf16[2048,512]{1,0:T(8,128)(2,1)S(1)}, bf16[2048,512]{1,0:T(8,128)(2,1)S(1)}, f32[4,512]{1,0:T(4,128)S(1)}) custom-call(f32[1,512]{1,0:T(1,128)} %bitcast.25, f32[4,512,512]{2,1,0:T(8,128)} %bitcast.20), custom_call_target="tpu_custom_call" | custom-call | tf_op jit(solution)/shard_map/split_blocks/pallas_call | solution.py:354
  6.4 4.0 %collective-permute-done = f32[32,512]{1,0:T(8,128)S(1)} collective-permute-done((f32[32,512]{1,0:T(8,128)}, f32[32,512]{1,0:T(8,128)S(1)}, u32[]{:S(2)}, u32[]{:S(2)}) %collective-permute-start) | collective-permute-done | bytes 65568 | tf_op jit(solution)/shard_map/ppermute | solution.py:416
  10.5 2.8 %collective-permute-start.1 = (f32[32,512]{1,0:T(8,128)S(1)}, f32[32,512]{1,0:T(8,128)S(1)}, u32[]{:S(2)}, u32[]{:S(2)}) collective-permute-start(f32[32,512]{1,0:T(8,128)S(1)} %collective-permute-done), channel_id=1, source_target_pairs={{0,8},{8,0},{16,24},{24,16},{1,9},{9,1},{17,25},{25,17},{2,10},{10... | collective-permute-start | bytes 196616 | tf_op jit(solution)/shard_map/ppermute | solution.py:418
  13.2 2.2 %collective-permute-done.1 = f32[32,512]{1,0:T(8,128)S(1)} collective-permute-done((f32[32,512]{1,0:T(8,128)S(1)}, f32[32,512]{1,0:T(8,128)S(1)}, u32[]{:S(2)}, u32[]{:S(2)}) %collective-permute-start.1) | collective-permute-done | bytes 65568 | tf_op jit(solution)/shard_map/ppermute | solution.py:418
  15.6 1.3 %collective-permute-done.2 = f32[2,32,512]{2,1,0:T(8,128)S(1)} collective-permute-done((f32[2,32,512]{2,1,0:T(8,128)S(1)}, f32[2,32,512]{2,1,0:T(8,128)S(1)}, u32[]{:S(2)}, u32[]{:S(2)}) %collective-permute-start.2) | collective-permute-done | bytes 131104 | tf_op jit(solution)/shard_map/ppermute | solution.py:420
  17.8 1.8 %collective-permute-start.3 = (f32[32,512]{1,0:T(8,128)S(1)}, f32[32,512]{1,0:T(8,128)S(1)}, u32[]{:S(2)}, u32[]{:S(2)}) collective-permute-start(f32[32,512]{1,0:T(8,128)S(1)} %down.2), channel_id=1, source_target_pairs={{0,5},{1,34},{2,67},{3,96},{4,144},{5,179},{6,214},{7,241},{8,13},... | collective-permute-start | bytes 196616 | tf_op jit(solution)/shard_map/ppermute | solution.py:392
  20.9 5.6 %collective-permute-done.3 = f32[32,512]{1,0:T(8,128)S(1)} collective-permute-done((f32[32,512]{1,0:T(8,128)S(1)}, f32[32,512]{1,0:T(8,128)S(1)}, u32[]{:S(2)}, u32[]{:S(2)}) %collective-permute-start.3) | collective-permute-done | bytes 65568 | tf_op jit(solution)/shard_map/ppermute | solution.py:392
  26.7 1.3 %collective-permute-done.4 = f32[16,8,256]{2,1,0:T(8,128)S(1)} collective-permute-done((f32[16,8,256]{2,1,0:T(8,128)S(1)}, f32[16,8,256]{2,1,0:T(8,128)S(1)}, u32[]{:S(2)}, u32[]{:S(2)}) %collective-permute-start.4) | collective-permute-done | bytes 131104 | tf_op jit(solution)/shard_map/ppermute | solution.py:401
  28.1 18.5 %all_to_all.20.parts_ref = f32[16,8,256]{2,1,0:T(8,128)S(1)} all-to-all(f32[16,8,256]{2,1,0:T(8,128)S(1)} %select_add_fusion.3), channel_id=1, replica_groups=mesh['zh'=2,'y'=4,'z'=4,'x'=4,'co'=2] {'z','x'}, dimensions={0} | all-to-all | bytes 262144 | tf_op jit(solution)/shard_map/all_to_all | solution.py:402
  46.6 11.8 %all_to_all.21 = f32[16,8,256]{2,1,0:T(8,128)S(1)} all-to-all(f32[16,8,256]{2,1,0:T(8,128)S(1)} %sum_spread.2), channel_id=1, replica_groups=mesh['zh'=2,'y'=4,'z'=4,'x'=4,'co'=2] {'z','x'}, dimensions={0} | all-to-all | bytes 262144 | tf_op jit(solution)/shard_map/all_to_all | solution.py:403
  58.5 1.3 %collective-permute-done.5 = f32[16,8,256]{2,1,0:T(8,128)S(1)} collective-permute-done((f32[16,8,256]{2,1,0:T(8,128)S(1)}, f32[16,8,256]{2,1,0:T(8,128)S(1)}, u32[]{:S(2)}, u32[]{:S(2)}) %collective-permute-start.5) | collective-permute-done | bytes 131104 | tf_op jit(solution)/shard_map/ppermute | solution.py:407
  60.9 3.3 %collective-permute-start.7 = (f32[32,512]{1,0:T(8,128)S(1)}, f32[32,512]{1,0:T(8,128)S(1)}, u32[]{:S(2)}, u32[]{:S(2)}) collective-permute-start(f32[32,512]{1,0:T(8,128)S(1)} %down.3), channel_id=1, source_target_pairs={{0,5},{1,34},{2,67},{3,96},{4,144},{5,179},{6,214},{7,241},{8,13},... | collective-permute-start | bytes 196616 | tf_op jit(solution)/shard_map/ppermute | solution.py:392
  66.6 2.5 %collective-permute-done.7 = f32[32,512]{1,0:T(8,128)S(1)} collective-permute-done((f32[32,512]{1,0:T(8,128)S(1)}, f32[32,512]{1,0:T(8,128)S(1)}, u32[]{:S(2)}, u32[]{:S(2)}) %collective-permute-start.7) | collective-permute-done | bytes 65568 | tf_op jit(solution)/shard_map/ppermute | solution.py:392
  69.3 1.3 %collective-permute-done.8 = f32[16,8,256]{2,1,0:T(8,128)S(1)} collective-permute-done((f32[16,8,256]{2,1,0:T(8,128)S(1)}, f32[16,8,256]{2,1,0:T(8,128)S(1)}, u32[]{:S(2)}, u32[]{:S(2)}) %collective-permute-start.8) | collective-permute-done | bytes 131104 | tf_op jit(solution)/shard_map/ppermute | solution.py:401
  70.6 17.4 %all_to_all.22.parts_ref = f32[16,8,256]{2,1,0:T(8,128)S(1)} all-to-all(f32[16,8,256]{2,1,0:T(8,128)S(1)} %select_add_fusion.2), channel_id=1, replica_groups=mesh['zh'=2,'y'=4,'z'=4,'x'=4,'co'=2] {'z','x'}, dimensions={0} | all-to-all | bytes 262144 | tf_op jit(solution)/shard_map/all_to_all | solution.py:402
  88.8 4.8 %all-to-all-start.3 = ((f32[16,8,256]{2,1,0:T(8,128)}), f32[16,8,256]{2,1,0:T(8,128)S(1)}, u32[]{:S(2)}, u32[]{:S(2)}) async-start(f32[16,8,256]{2,1,0:T(8,128)} %sum_spread.3), calls=%async_computation.3 | async-start | bytes 262144 | tf_op jit(solution)/shard_map/all_to_all | solution.py:403
  95.3 5.1 %collective-permute-done.9 = f32[32,96]{1,0:T(8,128)S(1)} collective-permute-done((f32[32,96]{1,0:T(8,128)S(1)}, f32[32,96]{1,0:T(8,128)S(1)}, u32[]{:S(2)}, u32[]{:S(2)}) %collective-permute-start.9) | collective-permute-done | bytes 12320 | tf_op jit(solution)/shard_map/ppermute | solution.py:327
  103.8 3.6 %collective-permute-done.11.right_ref = f32[32,192]{1,0:T(8,128)S(1)} collective-permute-done((f32[32,192]{1,0:T(8,128)S(1)}, f32[32,192]{1,0:T(8,128)S(1)}, u32[]{:S(2)}, u32[]{:S(2)}) %collective-permute-start.11) | collective-permute-done | bytes 24608 | tf_op jit(solution)/shard_map/ppermute | solution.py:433
  107.5 3.0 %collective-permute-start.14 = (f32[32,512]{1,0:T(8,128)S(1)}, f32[32,512]{1,0:T(8,128)S(1)}, u32[]{:S(2)}, u32[]{:S(2)}) collective-permute-start(f32[32,512]{1,0:T(8,128)S(1)} %select_reduce_fusion), channel_id=1, source_target_pairs={{5,0},{34,1},{67,2},{96,3},{144,4},{179,5},{214,6},{241,7},{13,8},... | collective-permute-start | bytes 196616 | tf_op jit(solution)/shard_map/ppermute | solution.py:431
  110.4 2.7 %collective-permute-done.12.right_ref = f32[32,192]{1,0:T(8,128)S(1)} collective-permute-done((f32[32,192]{1,0:T(8,128)S(1)}, f32[32,192]{1,0:T(8,128)S(1)}, u32[]{:S(2)}, u32[]{:S(2)}) %collective-permute-start.12) | collective-permute-done | bytes 24608 | tf_op jit(solution)/shard_map/ppermute | solution.py:433
  113.1 4.5 %first_step.1 = (f32[2,32,32]{2,1,0:T(8,128)S(1)}, f32[32,96]{1,0:T(8,128)S(1)}, f32[32,64]{1,0:T(8,128)S(1)}, f32[32,32]{1,0:T(8,128)S(1)}) custom-call(f32[32,192]{1,0:T(8,128)S(1)} %plus.3.both_ref), custom_call_target="tpu_custom_call" | custom-call | flops 6000000000 | bytes 100000 | tf_op jit(solution)/shard_map/first_step/pallas_call | solution.py:287
  117.6 1.6 %collective-permute-done.13.half_ref = f32[32,192]{1,0:T(8,128)S(1)} collective-permute-done((f32[32,192]{1,0:T(8,128)S(1)}, f32[32,192]{1,0:T(8,128)S(1)}, u32[]{:S(2)}, u32[]{:S(2)}) %collective-permute-start.13) | collective-permute-done | bytes 24608 | tf_op jit(solution)/shard_map/ppermute | solution.py:327
  119.2 3.3 %last_step.1 = (f32[2,2,32,32]{3,2,1,0:T(8,128)}, f32[32,512]{1,0:T(8,128)}) custom-call(f32[32,192]{1,0:T(8,128)S(1)} %plus.3.both_ref, f32[32,192]{1,0:T(8,128)S(1)} %collective-permute-done.13.half_ref, f32[2,32,32]{2,1,0:T(8,128)S(1)} %get-tuple-element.38.history0_ref, f32[32,96]{1,0:T(8,128)S(1)} %get-tuple-element.39.image_ref, ...), custom_call_target="tpu_custom_call" | custom-call | tf_op jit(solution)/shard_map/last_step/pallas_call | solution.py:305
  (47 shorter events, 12.2 us)
Async XLA Ops:
  0.6 9.8 %collective-permute-start = (f32[32,512]{1,0:T(8,128)}, f32[32,512]{1,0:T(8,128)S(1)}, u32[]{:S(2)}, u32[]{:S(2)}) collective-permute-start(f32[32,512]{1,0:T(8,128)} %x_ref.1), channel_id=1, source_target_pairs={{0,5},{1,34},{2,67},{3,96},{4,144},{5,179},{6,214},{7,241},{8,13},... | collective-permute-start | bytes 196616 | tf_op jit(solution)/shard_map/ppermute | solution.py:416
  10.5 5.0 %collective-permute-start.1 = (f32[32,512]{1,0:T(8,128)S(1)}, f32[32,512]{1,0:T(8,128)S(1)}, u32[]{:S(2)}, u32[]{:S(2)}) collective-permute-start(f32[32,512]{1,0:T(8,128)S(1)} %collective-permute-done), channel_id=1, source_target_pairs={{0,8},{8,0},{16,24},{24,16},{1,9},{9,1},{17,25},{25,17},{2,10},{10... | collective-permute-start | bytes 196616 | tf_op jit(solution)/shard_map/ppermute | solution.py:418
  15.5 1.4 %collective-permute-start.2 = (f32[2,32,512]{2,1,0:T(8,128)S(1)}, f32[2,32,512]{2,1,0:T(8,128)S(1)}, u32[]{:S(2)}, u32[]{:S(2)}) collective-permute-start(f32[2,32,512]{2,1,0:T(8,128)S(1)} %pad_maximum_fusion.3), channel_id=1, source_target_pairs={{0,1},{1,0},{2,3},{3,2},{4,5},{5,4},{6,7},{7,6},{8,9},{9,8},{10,11... | collective-permute-start | bytes 393224 | tf_op jit(solution)/shard_map/ppermute | solution.py:420
  17.0 2.6 %copy-start = (f32[32,512]{1,0:T(8,128)S(1)}, f32[32,512]{1,0:T(8,128)}, u32[]{:S(2)}) copy-start(f32[32,512]{1,0:T(8,128)} %x_ref.1) | copy-start | bytes 196612
  17.8 8.7 %collective-permute-start.3 = (f32[32,512]{1,0:T(8,128)S(1)}, f32[32,512]{1,0:T(8,128)S(1)}, u32[]{:S(2)}, u32[]{:S(2)}) collective-permute-start(f32[32,512]{1,0:T(8,128)S(1)} %down.2), channel_id=1, source_target_pairs={{0,5},{1,34},{2,67},{3,96},{4,144},{5,179},{6,214},{7,241},{8,13},... | collective-permute-start | bytes 196616 | tf_op jit(solution)/shard_map/ppermute | solution.py:392
  26.6 1.4 %collective-permute-start.4 = (f32[16,8,256]{2,1,0:T(8,128)S(1)}, f32[16,8,256]{2,1,0:T(8,128)S(1)}, u32[]{:S(2)}, u32[]{:S(2)}) collective-permute-start(f32[16,8,256]{2,1,0:T(8,128)S(1)} %slice_select_fusion.1), channel_id=1, source_target_pairs={{0,1},{1,0},{2,3},{3,2},{4,5},{5,4},{6,7},{7,6},{8,9},{9,8},{10,11... | collective-permute-start | bytes 393224 | tf_op jit(solution)/shard_map/ppermute | solution.py:401
  58.5 1.3 %collective-permute-start.5 = (f32[16,8,256]{2,1,0:T(8,128)S(1)}, f32[16,8,256]{2,1,0:T(8,128)S(1)}, u32[]{:S(2)}, u32[]{:S(2)}) collective-permute-start(f32[16,8,256]{2,1,0:T(8,128)S(1)} %all_to_all.21), channel_id=1, source_target_pairs={{0,1},{1,0},{2,3},{3,2},{4,5},{5,4},{6,7},{7,6},{8,9},{9,8},{10,11... | collective-permute-start | bytes 393224 | tf_op jit(solution)/shard_map/ppermute | solution.py:407
  59.9 5.3 %collective-permute-start.6 = (f32[32,512]{1,0:T(8,128)S(1)}, f32[32,512]{1,0:T(8,128)S(1)}, u32[]{:S(2)}, u32[]{:S(2)}) collective-permute-start(f32[32,512]{1,0:T(8,128)S(1)} %select_reduce_fusion.1), channel_id=1, source_target_pairs={{5,0},{34,1},{67,2},{96,3},{144,4},{179,5},{214,6},{241,7},{13,8},... | collective-permute-start | bytes 196616 | tf_op jit(solution)/shard_map/ppermute | solution.py:424
  60.9 8.2 %collective-permute-start.7 = (f32[32,512]{1,0:T(8,128)S(1)}, f32[32,512]{1,0:T(8,128)S(1)}, u32[]{:S(2)}, u32[]{:S(2)}) collective-permute-start(f32[32,512]{1,0:T(8,128)S(1)} %down.3), channel_id=1, source_target_pairs={{0,5},{1,34},{2,67},{3,96},{4,144},{5,179},{6,214},{7,241},{8,13},... | collective-permute-start | bytes 196616 | tf_op jit(solution)/shard_map/ppermute | solution.py:392
  69.2 1.4 %collective-permute-start.8 = (f32[16,8,256]{2,1,0:T(8,128)S(1)}, f32[16,8,256]{2,1,0:T(8,128)S(1)}, u32[]{:S(2)}, u32[]{:S(2)}) collective-permute-start(f32[16,8,256]{2,1,0:T(8,128)S(1)} %slice_select_fusion), channel_id=1, source_target_pairs={{0,1},{1,0},{2,3},{3,2},{4,5},{5,4},{6,7},{7,6},{8,9},{9,8},{10,11... | collective-permute-start | bytes 393224 | tf_op jit(solution)/shard_map/ppermute | solution.py:401
  88.8 12.4 %all-to-all-start.3 = ((f32[16,8,256]{2,1,0:T(8,128)}), f32[16,8,256]{2,1,0:T(8,128)S(1)}, u32[]{:S(2)}, u32[]{:S(2)}) async-start(f32[16,8,256]{2,1,0:T(8,128)} %sum_spread.3), calls=%async_computation.3 | async-start | bytes 262144 | tf_op jit(solution)/shard_map/all_to_all | solution.py:403
  94.5 5.9 %collective-permute-start.9 = (f32[32,96]{1,0:T(8,128)S(1)}, f32[32,96]{1,0:T(8,128)S(1)}, u32[]{:S(2)}, u32[]{:S(2)}) collective-permute-start(f32[32,96]{1,0:T(8,128)S(1)} %pad_maximum_fusion.5), channel_id=1, source_target_pairs={{0,144},{8,152},{16,128},{24,136},{128,16},{136,24},{144,0},{152,8... | collective-permute-start | bytes 36872 | tf_op jit(solution)/shard_map/ppermute | solution.py:327
  101.2 1.3 %collective-permute-start.10 = (f32[16,8,256]{2,1,0:T(8,128)S(1)}, f32[16,8,256]{2,1,0:T(8,128)S(1)}, u32[]{:S(2)}, u32[]{:S(2)}) collective-permute-start(f32[16,8,256]{2,1,0:T(8,128)S(1)} %all-to-all-done.3), channel_id=1, source_target_pairs={{0,1},{1,0},{2,3},{3,2},{4,5},{5,4},{6,7},{7,6},{8,9},{9,8},{10,11... | collective-permute-start | bytes 393224 | tf_op jit(solution)/shard_map/ppermute | solution.py:407
  103.4 3.9 %collective-permute-start.11 = (f32[32,192]{1,0:T(8,128)S(1)}, f32[32,192]{1,0:T(8,128)S(1)}, u32[]{:S(2)}, u32[]{:S(2)}) collective-permute-start(f32[32,192]{1,0:T(8,128)S(1)} %pad_maximum_fusion.4.left_ref), channel_id=1, source_target_pairs={{0,32},{32,0},{64,96},{96,64},{1,33},{33,1},{65,97},{97,65},{2,34}... | collective-permute-start | bytes 73736 | tf_op jit(solution)/shard_map/ppermute | solution.py:433
  107.4 5.7 %collective-permute-start.12 = (f32[32,192]{1,0:T(8,128)S(1)}, f32[32,192]{1,0:T(8,128)S(1)}, u32[]{:S(2)}, u32[]{:S(2)}) collective-permute-start(f32[32,192]{1,0:T(8,128)S(1)} %plus.2.left_ref), channel_id=1, source_target_pairs={{0,96},{96,0},{32,64},{64,32},{1,97},{97,1},{33,65},{65,33},{2,98}... | collective-permute-start | bytes 73736 | tf_op jit(solution)/shard_map/ppermute | solution.py:433
  107.5 10.1 %collective-permute-start.14 = (f32[32,512]{1,0:T(8,128)S(1)}, f32[32,512]{1,0:T(8,128)S(1)}, u32[]{:S(2)}, u32[]{:S(2)}) collective-permute-start(f32[32,512]{1,0:T(8,128)S(1)} %select_reduce_fusion), channel_id=1, source_target_pairs={{5,0},{34,1},{67,2},{96,3},{144,4},{179,5},{214,6},{241,7},{13,8},... | collective-permute-start | bytes 196616 | tf_op jit(solution)/shard_map/ppermute | solution.py:431
  113.1 6.1 %collective-permute-start.13 = (f32[32,192]{1,0:T(8,128)S(1)}, f32[32,192]{1,0:T(8,128)S(1)}, u32[]{:S(2)}, u32[]{:S(2)}) collective-permute-start(f32[32,192]{1,0:T(8,128)S(1)} %plus.3.both_ref), channel_id=1, source_target_pairs={{0,144},{8,152},{16,128},{24,136},{128,16},{136,24},{144,0},{152,8... | collective-permute-start | bytes 73736 | tf_op jit(solution)/shard_map/ppermute | solution.py:327

commit v10 on v9

--- a/solution.py
+++ b/solution.py
@@ -390,7 +390,7 @@
 
     def total(acrosses, downs, gram=None):
         arrived = lax.ppermute(downs, every, to_row_group())
-        acrosses = lax.optimization_barrier(acrosses)
+        acrosses, gram = lax.optimization_barrier((acrosses, gram))
         part = acrosses + jnp.where(in_slot, arrived[None], 0.0)
         part = part.reshape(slots * vecs // 8, 8, width)
         low, high = part[..., :half], part[..., half:]

time: 123 us -> 123 us (level)
  no operation moved by 1% of the time
where the time goes in v10:
time: 123 us
  blocking collectives  47.8 us (39%)
  waiting for transfers between devices  36.6 us (30%)
  starting transfers between devices  19.2 us (16%)
  Pallas kernels  17.4 us (14%)
    all_to_all x2, blocking collectives, total(): pieces = lax.all_to_all(mine, ('z', 'x'), 0, 0, tiled=True)  36 us
    all_to_all x1, blocking collectives, total(): whole = lax.all_to_all(sum_spread(pieces), ('z', 'x'), 0, 0, tiled=True)  11.8 us
    ppermute x2, waiting for transfers between devices, total(): arrived = lax.ppermute(downs, every, to_row_group())  7.09 us
    ppermute x2, waiting for transfers between devices, on_device(): both = plus(both, lax.ppermute(both, 'y', pairs))  6.8 us
    ppermute x2, waiting for transfers between devices, across_half(): return lax.ppermute(value, ('zh', 'z'), pairs)  6.66 us
    ppermute x2, starting transfers between devices, total(): arrived = lax.ppermute(downs, every, to_row_group())  5.01 us
    all_to_all x1, starting transfers between devices, total(): whole = lax.all_to_all(sum_spread(pieces), ('z', 'x'), 0, 0, tiled=True)  4.76 us
    pallas_call x1, Pallas kernels, begin(): pl.pallas_call(functools.partial(first_step, 1.0 / length), in_specs=[IN_...  4.45 us
  transfers between devices with their start and end apart: 16, of which 15 were waited for; matrix products, arithmetic and copies ran while one was open for 0% of the time, Pallas kernels for 10%

profile of v10, /device:TPU:2, one launch (start us, length us, event | category | flops | bytes accessed | tf_op | source)
XLA Modules:
  0.0 122.6 jit_solution(5565410416637124665)
XLA Ops:
  0.6 2.7 %collective-permute-start = (f32[32,512]{1,0:T(8,128)}, f32[32,512]{1,0:T(8,128)S(1)}, u32[]{:S(2)}, u32[]{:S(2)}) collective-permute-start(f32[32,512]{1,0:T(8,128)} %x_ref.1), channel_id=1, source_target_pairs={{0,5},{1,34},{2,67},{3,96},{4,144},{5,179},{6,214},{7,241},{8,13},... | collective-permute-start | bytes 196616 | tf_op jit(solution)/shard_map/ppermute | solution.py:416
  3.3 3.1 %split_blocks.1 = (bf16[2048,512]{1,0:T(8,128)(2,1)S(1)}, bf16[2048,512]{1,0:T(8,128)(2,1)S(1)}, f32[4,512]{1,0:T(4,128)S(1)}) custom-call(f32[1,512]{1,0:T(1,128)} %bitcast.25, f32[4,512,512]{2,1,0:T(8,128)} %bitcast.20), custom_call_target="tpu_custom_call" | custom-call | tf_op jit(solution)/shard_map/split_blocks/pallas_call | solution.py:354
  6.4 4.0 %collective-permute-done = f32[32,512]{1,0:T(8,128)S(1)} collective-permute-done((f32[32,512]{1,0:T(8,128)}, f32[32,512]{1,0:T(8,128)S(1)}, u32[]{:S(2)}, u32[]{:S(2)}) %collective-permute-start) | collective-permute-done | bytes 65568 | tf_op jit(solution)/shard_map/ppermute | solution.py:416
  10.5 2.8 %collective-permute-start.1 = (f32[32,512]{1,0:T(8,128)S(1)}, f32[32,512]{1,0:T(8,128)S(1)}, u32[]{:S(2)}, u32[]{:S(2)}) collective-permute-start(f32[32,512]{1,0:T(8,128)S(1)} %collective-permute-done), channel_id=1, source_target_pairs={{0,8},{8,0},{16,24},{24,16},{1,9},{9,1},{17,25},{25,17},{2,10},{10... | collective-permute-start | bytes 196616 | tf_op jit(solution)/shard_map/ppermute | solution.py:418
  13.2 2.2 %collective-permute-done.1 = f32[32,512]{1,0:T(8,128)S(1)} collective-permute-done((f32[32,512]{1,0:T(8,128)S(1)}, f32[32,512]{1,0:T(8,128)S(1)}, u32[]{:S(2)}, u32[]{:S(2)}) %collective-permute-start.1) | collective-permute-done | bytes 65568 | tf_op jit(solution)/shard_map/ppermute | solution.py:418
  17.8 1.8 %collective-permute-start.3 = (f32[32,512]{1,0:T(8,128)S(1)}, f32[32,512]{1,0:T(8,128)S(1)}, u32[]{:S(2)}, u32[]{:S(2)}) collective-permute-start(f32[32,512]{1,0:T(8,128)S(1)} %down.2), channel_id=1, source_target_pairs={{0,5},{1,34},{2,67},{3,96},{4,144},{5,179},{6,214},{7,241},{8,13},... | collective-permute-start | bytes 196616 | tf_op jit(solution)/shard_map/ppermute | solution.py:392
  20.9 5.6 %collective-permute-done.3 = f32[32,512]{1,0:T(8,128)S(1)} collective-permute-done((f32[32,512]{1,0:T(8,128)S(1)}, f32[32,512]{1,0:T(8,128)S(1)}, u32[]{:S(2)}, u32[]{:S(2)}) %collective-permute-start.3) | collective-permute-done | bytes 65568 | tf_op jit(solution)/shard_map/ppermute | solution.py:392
  26.7 1.3 %collective-permute-done.4 = f32[16,8,256]{2,1,0:T(8,128)S(1)} collective-permute-done((f32[16,8,256]{2,1,0:T(8,128)S(1)}, f32[16,8,256]{2,1,0:T(8,128)S(1)}, u32[]{:S(2)}, u32[]{:S(2)}) %collective-permute-start.4) | collective-permute-done | bytes 131104 | tf_op jit(solution)/shard_map/ppermute | solution.py:401
  28.1 18.5 %all_to_all.20.parts_ref = f32[16,8,256]{2,1,0:T(8,128)S(1)} all-to-all(f32[16,8,256]{2,1,0:T(8,128)S(1)} %select_add_fusion.3), channel_id=1, replica_groups=mesh['zh'=2,'y'=4,'z'=4,'x'=4,'co'=2] {'z','x'}, dimensions={0} | all-to-all | bytes 262144 | tf_op jit(solution)/shard_map/all_to_all | solution.py:402
  46.6 11.8 %all_to_all.21 = f32[16,8,256]{2,1,0:T(8,128)S(1)} all-to-all(f32[16,8,256]{2,1,0:T(8,128)S(1)} %sum_spread.2), channel_id=1, replica_groups=mesh['zh'=2,'y'=4,'z'=4,'x'=4,'co'=2] {'z','x'}, dimensions={0} | all-to-all | bytes 262144 | tf_op jit(solution)/shard_map/all_to_all | solution.py:403
  58.5 1.3 %collective-permute-done.5 = f32[16,8,256]{2,1,0:T(8,128)S(1)} collective-permute-done((f32[16,8,256]{2,1,0:T(8,128)S(1)}, f32[16,8,256]{2,1,0:T(8,128)S(1)}, u32[]{:S(2)}, u32[]{:S(2)}) %collective-permute-start.5) | collective-permute-done | bytes 131104 | tf_op jit(solution)/shard_map/ppermute | solution.py:407
  60.9 3.3 %collective-permute-start.7 = (f32[32,512]{1,0:T(8,128)S(1)}, f32[32,512]{1,0:T(8,128)S(1)}, u32[]{:S(2)}, u32[]{:S(2)}) collective-permute-start(f32[32,512]{1,0:T(8,128)S(1)} %down.3), channel_id=1, source_target_pairs={{0,5},{1,34},{2,67},{3,96},{4,144},{5,179},{6,214},{7,241},{8,13},... | collective-permute-start | bytes 196616 | tf_op jit(solution)/shard_map/ppermute | solution.py:392
  67.5 1.5 %collective-permute-done.7 = f32[32,512]{1,0:T(8,128)S(1)} collective-permute-done((f32[32,512]{1,0:T(8,128)S(1)}, f32[32,512]{1,0:T(8,128)S(1)}, u32[]{:S(2)}, u32[]{:S(2)}) %collective-permute-start.7) | collective-permute-done | bytes 65568 | tf_op jit(solution)/shard_map/ppermute | solution.py:392
  70.6 17.4 %all_to_all.22.parts_ref = f32[16,8,256]{2,1,0:T(8,128)S(1)} all-to-all(f32[16,8,256]{2,1,0:T(8,128)S(1)} %select_add_fusion.2), channel_id=1, replica_groups=mesh['zh'=2,'y'=4,'z'=4,'x'=4,'co'=2] {'z','x'}, dimensions={0} | all-to-all | bytes 262144 | tf_op jit(solution)/shard_map/all_to_all | solution.py:402
  88.8 4.8 %all-to-all-start.3 = ((f32[16,8,256]{2,1,0:T(8,128)}), f32[16,8,256]{2,1,0:T(8,128)S(1)}, u32[]{:S(2)}, u32[]{:S(2)}) async-start(f32[16,8,256]{2,1,0:T(8,128)} %sum_spread.3), calls=%async_computation.3 | async-start | bytes 262144 | tf_op jit(solution)/shard_map/all_to_all | solution.py:403
  94.3 5.1 %collective-permute-done.9 = f32[32,96]{1,0:T(8,128)S(1)} collective-permute-done((f32[32,96]{1,0:T(8,128)S(1)}, f32[32,96]{1,0:T(8,128)S(1)}, u32[]{:S(2)}, u32[]{:S(2)}) %collective-permute-start.9) | collective-permute-done | bytes 12320 | tf_op jit(solution)/shard_map/ppermute | solution.py:327
  99.4 2.0 %all-to-all-done.3 = f32[16,8,256]{2,1,0:T(8,128)S(1)} async-done(((f32[16,8,256]{2,1,0:T(8,128)}), f32[16,8,256]{2,1,0:T(8,128)S(1)}, u32[]{:S(2)}, u32[]{:S(2)}) %all-to-all-start.3) | async-done | bytes 131104 | tf_op jit(solution)/shard_map/all_to_all | solution.py:403
  101.4 1.3 %collective-permute-done.10 = f32[16,8,256]{2,1,0:T(8,128)S(1)} collective-permute-done((f32[16,8,256]{2,1,0:T(8,128)S(1)}, f32[16,8,256]{2,1,0:T(8,128)S(1)}, u32[]{:S(2)}, u32[]{:S(2)}) %collective-permute-start.10) | collective-permute-done | bytes 131104 | tf_op jit(solution)/shard_map/ppermute | solution.py:407
  104.0 3.5 %collective-permute-done.11.right_ref = f32[32,192]{1,0:T(8,128)S(1)} collective-permute-done((f32[32,192]{1,0:T(8,128)S(1)}, f32[32,192]{1,0:T(8,128)S(1)}, u32[]{:S(2)}, u32[]{:S(2)}) %collective-permute-start.11) | collective-permute-done | bytes 24608 | tf_op jit(solution)/shard_map/ppermute | solution.py:433
  107.6 2.4 %collective-permute-start.14 = (f32[32,512]{1,0:T(8,128)S(1)}, f32[32,512]{1,0:T(8,128)S(1)}, u32[]{:S(2)}, u32[]{:S(2)}) collective-permute-start(f32[32,512]{1,0:T(8,128)S(1)} %select_reduce_fusion), channel_id=1, source_target_pairs={{5,0},{34,1},{67,2},{96,3},{144,4},{179,5},{214,6},{241,7},{13,8},... | collective-permute-start | bytes 196616 | tf_op jit(solution)/shard_map/ppermute | solution.py:431
  110.0 3.3 %collective-permute-done.12.right_ref = f32[32,192]{1,0:T(8,128)S(1)} collective-permute-done((f32[32,192]{1,0:T(8,128)S(1)}, f32[32,192]{1,0:T(8,128)S(1)}, u32[]{:S(2)}, u32[]{:S(2)}) %collective-permute-start.12) | collective-permute-done | bytes 24608 | tf_op jit(solution)/shard_map/ppermute | solution.py:433
  113.3 4.5 %first_step.1 = (f32[2,32,32]{2,1,0:T(8,128)S(1)}, f32[32,96]{1,0:T(8,128)S(1)}, f32[32,64]{1,0:T(8,128)S(1)}, f32[32,32]{1,0:T(8,128)S(1)}) custom-call(f32[32,192]{1,0:T(8,128)S(1)} %plus.3.both_ref), custom_call_target="tpu_custom_call" | custom-call | flops 6000000000 | bytes 100000 | tf_op jit(solution)/shard_map/first_step/pallas_call | solution.py:287
  117.7 1.6 %collective-permute-done.13.half_ref = f32[32,192]{1,0:T(8,128)S(1)} collective-permute-done((f32[32,192]{1,0:T(8,128)S(1)}, f32[32,192]{1,0:T(8,128)S(1)}, u32[]{:S(2)}, u32[]{:S(2)}) %collective-permute-start.13) | collective-permute-done | bytes 24608 | tf_op jit(solution)/shard_map/ppermute | solution.py:327
  119.3 3.3 %last_step.1 = (f32[2,2,32,32]{3,2,1,0:T(8,128)}, f32[32,512]{1,0:T(8,128)}) custom-call(f32[32,192]{1,0:T(8,128)S(1)} %plus.3.both_ref, f32[32,192]{1,0:T(8,128)S(1)} %collective-permute-done.13.half_ref, f32[2,32,32]{2,1,0:T(8,128)S(1)} %get-tuple-element.42.history0_ref, f32[32,96]{1,0:T(8,128)S(1)} %get-tuple-element.43.image_ref, ...), custom_call_target="tpu_custom_call" | custom-call | tf_op jit(solution)/shard_map/last_step/pallas_call | solution.py:305
  (47 shorter events, 12.7 us)
Async XLA Ops:
  0.6 9.8 %collective-permute-start = (f32[32,512]{1,0:T(8,128)}, f32[32,512]{1,0:T(8,128)S(1)}, u32[]{:S(2)}, u32[]{:S(2)}) collective-permute-start(f32[32,512]{1,0:T(8,128)} %x_ref.1), channel_id=1, source_target_pairs={{0,5},{1,34},{2,67},{3,96},{4,144},{5,179},{6,214},{7,241},{8,13},... | collective-permute-start | bytes 196616 | tf_op jit(solution)/shard_map/ppermute | solution.py:416
  10.5 5.0 %collective-permute-start.1 = (f32[32,512]{1,0:T(8,128)S(1)}, f32[32,512]{1,0:T(8,128)S(1)}, u32[]{:S(2)}, u32[]{:S(2)}) collective-permute-start(f32[32,512]{1,0:T(8,128)S(1)} %collective-permute-done), channel_id=1, source_target_pairs={{0,8},{8,0},{16,24},{24,16},{1,9},{9,1},{17,25},{25,17},{2,10},{10... | collective-permute-start | bytes 196616 | tf_op jit(solution)/shard_map/ppermute | solution.py:418
  15.5 1.4 %collective-permute-start.2 = (f32[2,32,512]{2,1,0:T(8,128)S(1)}, f32[2,32,512]{2,1,0:T(8,128)S(1)}, u32[]{:S(2)}, u32[]{:S(2)}) collective-permute-start(f32[2,32,512]{2,1,0:T(8,128)S(1)} %pad_maximum_fusion.3), channel_id=1, source_target_pairs={{0,1},{1,0},{2,3},{3,2},{4,5},{5,4},{6,7},{7,6},{8,9},{9,8},{10,11... | collective-permute-start | bytes 393224 | tf_op jit(solution)/shard_map/ppermute | solution.py:420
  17.0 2.6 %copy-start = (f32[32,512]{1,0:T(8,128)S(1)}, f32[32,512]{1,0:T(8,128)}, u32[]{:S(2)}) copy-start(f32[32,512]{1,0:T(8,128)} %x_ref.1) | copy-start | bytes 196612
  17.8 8.7 %collective-permute-start.3 = (f32[32,512]{1,0:T(8,128)S(1)}, f32[32,512]{1,0:T(8,128)S(1)}, u32[]{:S(2)}, u32[]{:S(2)}) collective-permute-start(f32[32,512]{1,0:T(8,128)S(1)} %down.2), channel_id=1, source_target_pairs={{0,5},{1,34},{2,67},{3,96},{4,144},{5,179},{6,214},{7,241},{8,13},... | collective-permute-start | bytes 196616 | tf_op jit(solution)/shard_map/ppermute | solution.py:392
  26.6 1.4 %collective-permute-start.4 = (f32[16,8,256]{2,1,0:T(8,128)S(1)}, f32[16,8,256]{2,1,0:T(8,128)S(1)}, u32[]{:S(2)}, u32[]{:S(2)}) collective-permute-start(f32[16,8,256]{2,1,0:T(8,128)S(1)} %slice_select_fusion.1), channel_id=1, source_target_pairs={{0,1},{1,0},{2,3},{3,2},{4,5},{5,4},{6,7},{7,6},{8,9},{9,8},{10,11... | collective-permute-start | bytes 393224 | tf_op jit(solution)/shard_map/ppermute | solution.py:401
  58.5 1.3 %collective-permute-start.5 = (f32[16,8,256]{2,1,0:T(8,128)S(1)}, f32[16,8,256]{2,1,0:T(8,128)S(1)}, u32[]{:S(2)}, u32[]{:S(2)}) collective-permute-start(f32[16,8,256]{2,1,0:T(8,128)S(1)} %all_to_all.21), channel_id=1, source_target_pairs={{0,1},{1,0},{2,3},{3,2},{4,5},{5,4},{6,7},{7,6},{8,9},{9,8},{10,11... | collective-permute-start | bytes 393224 | tf_op jit(solution)/shard_map/ppermute | solution.py:407
  59.9 5.3 %collective-permute-start.6 = (f32[32,512]{1,0:T(8,128)S(1)}, f32[32,512]{1,0:T(8,128)S(1)}, u32[]{:S(2)}, u32[]{:S(2)}) collective-permute-start(f32[32,512]{1,0:T(8,128)S(1)} %select_reduce_fusion.1), channel_id=1, source_target_pairs={{5,0},{34,1},{67,2},{96,3},{144,4},{179,5},{214,6},{241,7},{13,8},... | collective-permute-start | bytes 196616 | tf_op jit(solution)/shard_map/ppermute | solution.py:424
  60.9 8.2 %collective-permute-start.7 = (f32[32,512]{1,0:T(8,128)S(1)}, f32[32,512]{1,0:T(8,128)S(1)}, u32[]{:S(2)}, u32[]{:S(2)}) collective-permute-start(f32[32,512]{1,0:T(8,128)S(1)} %down.3), channel_id=1, source_target_pairs={{0,5},{1,34},{2,67},{3,96},{4,144},{5,179},{6,214},{7,241},{8,13},... | collective-permute-start | bytes 196616 | tf_op jit(solution)/shard_map/ppermute | solution.py:392
  69.2 1.4 %collective-permute-start.8 = (f32[16,8,256]{2,1,0:T(8,128)S(1)}, f32[16,8,256]{2,1,0:T(8,128)S(1)}, u32[]{:S(2)}, u32[]{:S(2)}) collective-permute-start(f32[16,8,256]{2,1,0:T(8,128)S(1)} %slice_select_fusion), channel_id=1, source_target_pairs={{0,1},{1,0},{2,3},{3,2},{4,5},{5,4},{6,7},{7,6},{8,9},{9,8},{10,11... | collective-permute-start | bytes 393224 | tf_op jit(solution)/shard_map/ppermute | solution.py:401
  88.8 12.6 %all-to-all-start.3 = ((f32[16,8,256]{2,1,0:T(8,128)}), f32[16,8,256]{2,1,0:T(8,128)S(1)}, u32[]{:S(2)}, u32[]{:S(2)}) async-start(f32[16,8,256]{2,1,0:T(8,128)} %sum_spread.3), calls=%async_computation.3 | async-start | bytes 262144 | tf_op jit(solution)/shard_map/all_to_all | solution.py:403
  93.5 5.9 %collective-permute-start.9 = (f32[32,96]{1,0:T(8,128)S(1)}, f32[32,96]{1,0:T(8,128)S(1)}, u32[]{:S(2)}, u32[]{:S(2)}) collective-permute-start(f32[32,96]{1,0:T(8,128)S(1)} %pad_maximum_fusion.5), channel_id=1, source_target_pairs={{0,144},{8,152},{16,128},{24,136},{128,16},{136,24},{144,0},{152,8... | collective-permute-start | bytes 36872 | tf_op jit(solution)/shard_map/ppermute | solution.py:327
  101.4 1.3 %collective-permute-start.10 = (f32[16,8,256]{2,1,0:T(8,128)S(1)}, f32[16,8,256]{2,1,0:T(8,128)S(1)}, u32[]{:S(2)}, u32[]{:S(2)}) collective-permute-start(f32[16,8,256]{2,1,0:T(8,128)S(1)} %all-to-all-done.3), channel_id=1, source_target_pairs={{0,1},{1,0},{2,3},{3,2},{4,5},{5,4},{6,7},{7,6},{8,9},{9,8},{10,11... | collective-permute-start | bytes 393224 | tf_op jit(solution)/shard_map/ppermute | solution.py:407
  103.6 3.9 %collective-permute-start.11 = (f32[32,192]{1,0:T(8,128)S(1)}, f32[32,192]{1,0:T(8,128)S(1)}, u32[]{:S(2)}, u32[]{:S(2)}) collective-permute-start(f32[32,192]{1,0:T(8,128)S(1)} %pad_maximum_fusion.4.left_ref), channel_id=1, source_target_pairs={{0,32},{32,0},{64,96},{96,64},{1,33},{33,1},{65,97},{97,65},{2,34}... | collective-permute-start | bytes 73736 | tf_op jit(solution)/shard_map/ppermute | solution.py:433
  107.5 5.7 %collective-permute-start.12 = (f32[32,192]{1,0:T(8,128)S(1)}, f32[32,192]{1,0:T(8,128)S(1)}, u32[]{:S(2)}, u32[]{:S(2)}) collective-permute-start(f32[32,192]{1,0:T(8,128)S(1)} %plus.2.left_ref), channel_id=1, source_target_pairs={{0,96},{96,0},{32,64},{64,32},{1,97},{97,1},{33,65},{65,33},{2,98}... | collective-permute-start | bytes 73736 | tf_op jit(solution)/shard_map/ppermute | solution.py:433
  107.6 10.1 %collective-permute-start.14 = (f32[32,512]{1,0:T(8,128)S(1)}, f32[32,512]{1,0:T(8,128)S(1)}, u32[]{:S(2)}, u32[]{:S(2)}) collective-permute-start(f32[32,512]{1,0:T(8,128)S(1)} %select_reduce_fusion), channel_id=1, source_target_pairs={{5,0},{34,1},{67,2},{96,3},{144,4},{179,5},{214,6},{241,7},{13,8},... | collective-permute-start | bytes 196616 | tf_op jit(solution)/shard_map/ppermute | solution.py:431
  113.3 6.0 %collective-permute-start.13 = (f32[32,192]{1,0:T(8,128)S(1)}, f32[32,192]{1,0:T(8,128)S(1)}, u32[]{:S(2)}, u32[]{:S(2)}) collective-permute-start(f32[32,192]{1,0:T(8,128)S(1)} %plus.3.both_ref), channel_id=1, source_target_pairs={{0,144},{8,152},{16,128},{24,136},{128,16},{136,24},{144,0},{152,8... | collective-permute-start | bytes 73736 | tf_op jit(solution)/shard_map/ppermute | solution.py:327

commit v11 on v10

--- a/solution.py
+++ b/solution.py
@@ -138,14 +138,14 @@
 
 
 def last_step(
-    scale, both_ref, half_ref, history0_ref, image_ref, second_ref, own_ref, x_ref, y_ref, z_ref,
+    scale, mean_ref, both_ref, half_ref, history0_ref, image_ref, second_ref, own_ref, x_ref, y_ref, z_ref,
     history_ref, out_ref, g_ref, p_ref, v_ref, s_ref,
 ):
     n = both_ref.shape[0]
     gram2 = (both_ref[:, 0 : 3 * n] + half_ref[:, 0 : 3 * n]) * scale
     eye = jnp.where(
         lax.broadcasted_iota(jnp.int32, (n, n), 0) == lax.broadcasted_iota(jnp.int32, (n, n), 1),
-        SHIFT,
+        jnp.broadcast_to(mean_ref[0:1, 0:1], (n, n)),
         0.0,
     )
     g_ref[0:n, 0:n] = both_ref[:, 3 * n : 4 * n] * scale
@@ -179,13 +179,17 @@
     return high, (v - high.astype(jnp.float32)).astype(jnp.bfloat16)
 
 
-def split_blocks(energies_ref, blocks_ref, high_ref, low_ref, lead_ref, held, arrived):
+def split_blocks(
+    length, energies_ref, blocks_ref, high_ref, low_ref, lead_ref, mean_ref, held, arrived
+):
     slots, width = blocks_ref.shape[0], blocks_ref.shape[1]
     copies = [
         pltpu.make_async_copy(blocks_ref.at[s], held.at[s], arrived.at[s]) for s in range(slots)
     ]
     for copy in copies:
         copy.start()
+    mean = jnp.sum(energies_ref[...], axis=1, keepdims=True) * (1.0 / length)
+    mean_ref[...] = jnp.broadcast_to(mean, mean_ref.shape)
     row, col = lax.axis_index(ROW), lax.axis_index(COL)
     for s in range(slots):
         block_row = row + 8 * s
@@ -300,7 +304,7 @@
     )(both)
 
 
-def close(both, half, history0, image, second, own, x, y, z, length):
+def close(mean, both, half, history0, image, second, own, x, y, z, length):
     vecs = x.shape[0]
     return pl.pallas_call(
         functools.partial(last_step, 1.0 / length),
@@ -316,7 +320,7 @@
         ],
         compiler_params=LIMIT,
         name="last_step",
-    )(both, half, history0, image, second, own, x, y, z)
+    )(mean, both, half, history0, image, second, own, x, y, z)
 
 
 PAIRS = ([(0, 1), (1, 0), (2, 3), (3, 2)], [(0, 3), (3, 0), (1, 2), (2, 1)])
@@ -351,14 +355,15 @@
     in_slot = (jnp.arange(slots) == slot)[:, None, None]
     every = NAMES
 
-    high, low, lead = pl.pallas_call(
-        split_blocks,
+    high, low, lead, mean = pl.pallas_call(
+        functools.partial(split_blocks, col_count * width),
         in_specs=[IN_VMEM, pl.BlockSpec(memory_space=pltpu.HBM)],
-        out_specs=(IN_VMEM, IN_VMEM, IN_VMEM),
+        out_specs=(IN_VMEM,) * 4,
         out_shape=(
             pltpu.VMEM((slots * width, width), jnp.bfloat16),
             pltpu.VMEM((slots * width, width), jnp.bfloat16),
             pltpu.VMEM((slots, width), jnp.float32),
+            pltpu.VMEM((8, 128), jnp.float32),
         ),
         scratch_shapes=[
             pltpu.VMEM(blocks.shape, jnp.float32),
@@ -388,8 +393,11 @@
             name="across",
         )(lead, own, high, low)
 
-    def total(acrosses, downs, gram=None):
+    def total(acrosses, downs, before, mean, far_mean, gram=None):
         arrived = lax.ppermute(downs, every, to_row_group())
+        if far_mean is not None:
+            arrived, far_mean = lax.optimization_barrier((arrived, far_mean))
+            mean = mean + far_mean
         acrosses, gram = lax.optimization_barrier((acrosses, gram))
         part = acrosses + jnp.where(in_slot, arrived[None], 0.0)
         part = part.reshape(slots * vecs // 8, 8, width)
@@ -408,32 +416,40 @@
         low = jnp.where(first, whole, facing)
         high = jnp.where(first, facing, whole)
         four = jnp.concatenate([low, high], axis=-1).reshape(slots, vecs, width)
-        return four, gram
+        four = four - (mean[:1, :1] - SHIFT)[None] * before
+        return four, gram, mean
 
     def slot_of(four):
         return jnp.sum(jnp.where(in_slot, four, 0.0), axis=0)
 
     moved = lax.ppermute(start_block, every, to_row_group())
-    moved, high, low = lax.optimization_barrier((moved, high, low))
+    mean = mean + lax.ppermute(mean, "co", [(0, 1), (1, 0)])
+    mean = mean + lax.ppermute(mean, "x", PAIRS[0])
+    moved, high, low, mean = lax.optimization_barrier((moved, high, low, mean))
     near = lax.ppermute(moved, "z", [(0, 1), (1, 0), (2, 3), (3, 2)])
+    near, near_mean = lax.optimization_barrier((near, lax.ppermute(mean, "x", PAIRS[1])))
+    mean = mean + near_mean
     two = jnp.stack([jnp.where(odd, near, moved), jnp.where(odd, moved, near)])
     over = lax.ppermute(two, "co", [(0, 1), (1, 0)])
     x4 = jnp.concatenate([jnp.where(upper, over, two), jnp.where(upper, two, over)])
     x = start_block
-    y4, _ = total(across(x), down(x4))
+    downs, mean = lax.optimization_barrier((down(x4), mean))
+    mean = mean + lax.ppermute(mean, "z", PAIRS[0])
+    far_mean = lax.ppermute(mean, "z", [(0, 2), (2, 0), (1, 3), (3, 1)])
+    y4, _, mean = total(across(x), downs, x4, mean, far_mean)
     y = lax.ppermute(slot_of(y4), every, from_row_group())
     downs = down(y4)
     y, x4_late, y4_late = lax.optimization_barrier((y, x4, y4))
     acrosses = across(y)
     gram = jnp.concatenate([grams_of(x4_late), grams_of(x4_late, y4_late)], axis=1)
-    z4, gram = total(acrosses, downs, gram)
+    z4, gram, mean = total(acrosses, downs, y4, mean, None, gram)
     both = jnp.concatenate([grams_of(x4, y4, z4), gram], axis=1)
     zz = lax.ppermute(slot_of(z4), every, from_row_group())
     for pairs in PAIRS:
         both = plus(both, lax.ppermute(both, "y", pairs))
     other_half = across_half(both)
     length = col_count * width
-    return close(both, other_half, *begin(both, length), x, y, zz, length)
+    return close(mean, both, other_half, *begin(both, length), x, y, zz, length)
 
 
 def solution(mesh):

time: 123 us -> 129 us (1.049)
  starting transfers between devices: 19.2 us -> 29 us
  waiting for transfers between devices: 36.6 us -> 32.7 us
  blocking collectives: 47.8 us -> 46.2 us
    ppermute x0 -> x5, waiting for transfers between devices: none -> 9.22 us  [the longest x1 3.37 us: on_device(): mean = mean + lax.ppermute(mean, 'x', PAIRS[0])]
    ppermute x0 -> x5, starting transfers between devices: none -> 9.21 us  [the longest x1 5.94 us: on_device(): lax.ppermute(mean, 'x', PAIRS[1])]
    ppermute x2, waiting for transfers between devices: 7.09 us -> 2.92 us  [total(): arrived = lax.ppermute(downs, every, to_row_group())]
    ppermute x1, waiting for transfers between devices: 4.02 us -> 0.01 us  [on_device(): moved = lax.ppermute(start_block, every, to_row_group())]
    ppermute x1, waiting for transfers between devices: 2.24 us -> 0.01 us  [on_device(): near = lax.ppermute(moved, 'z', [(0, 1), (1, 0), (2, 3), (3, 2)])]
    all_to_all x2, blocking collectives: 36 us -> 34.4 us  [total(): pieces = lax.all_to_all(mine, ('z', 'x'), 0, 0, tiled=True)]
    ppermute x2, waiting for transfers between devices: 6.66 us -> 5.35 us  [across_half(): return lax.ppermute(value, ('zh', 'z'), pairs)]
    ppermute x2, starting transfers between devices: 0.76 us -> 2.07 us  [across_half(): return lax.ppermute(value, ('zh', 'z'), pairs)]
  transfers between devices with their start and end apart: 16 -> 21, of which waited for: 15 -> 18; matrix products, arithmetic and copies ran while one was open for 0% -> 0% of each run, Pallas kernels for 10% -> 9%
where the time goes in v11:
time: 129 us; the launch traced here: 128 us
  blocking collectives  46.2 us (36%)
  waiting for transfers between devices  32.7 us (25%)
  starting transfers between devices  29 us (22%)
  Pallas kernels  17.4 us (13%)
  between operations  1.47 us (1%)
    all_to_all x2, blocking collectives, total(): pieces = lax.all_to_all(mine, ('z', 'x'), 0, 0, tiled=True)  34.4 us
    all_to_all x1, blocking collectives, total(): whole = lax.all_to_all(sum_spread(pieces), ('z', 'x'), 0, 0, tiled=True)  11.8 us
    ppermute x2, waiting for transfers between devices, on_device(): both = plus(both, lax.ppermute(both, 'y', pairs))  6.75 us
    ppermute x1, starting transfers between devices, on_device(): lax.ppermute(mean, 'x', PAIRS[1])  5.94 us
    ppermute x2, waiting for transfers between devices, across_half(): return lax.ppermute(value, ('zh', 'z'), pairs)  5.35 us
    all_to_all x1, starting transfers between devices, total(): whole = lax.all_to_all(sum_spread(pieces), ('z', 'x'), 0, 0, tiled=True)  4.76 us
    pallas_call x1, Pallas kernels, begin(): pl.pallas_call(functools.partial(first_step, 1.0 / length), in_specs=[IN_...  4.46 us
    ppermute x2, starting transfers between devices, total(): arrived = lax.ppermute(downs, every, to_row_group())  4.28 us
  transfers between devices with their start and end apart: 21, of which 18 were waited for; matrix products, arithmetic and copies ran while one was open for 0% of the time, Pallas kernels for 9%

profile of v11, /device:TPU:2, one launch (start us, length us, event | category | flops | bytes accessed | tf_op | source)
XLA Modules:
  0.0 128.2 jit_solution(982559989142312877)
XLA Ops:
  0.6 2.7 %collective-permute-start = (f32[32,512]{1,0:T(8,128)}, f32[32,512]{1,0:T(8,128)S(1)}, u32[]{:S(2)}, u32[]{:S(2)}) collective-permute-start(f32[32,512]{1,0:T(8,128)} %x_ref.1), channel_id=1, source_target_pairs={{0,5},{1,34},{2,67},{3,96},{4,144},{5,179},{6,214},{7,241},{8,13},... | collective-permute-start | bytes 196616 | tf_op jit(solution)/shard_map/ppermute | solution.py:425
  3.3 3.1 %split_blocks.1 = (bf16[2048,512]{1,0:T(8,128)(2,1)S(1)}, bf16[2048,512]{1,0:T(8,128)(2,1)S(1)}, f32[4,512]{1,0:T(4,128)S(1)}, f32[8,128]{1,0:T(8,128)S(1)}) custom-call(f32[1,512]{1,0:T(1,128)} %bitcast.22, f32[4,512,512]{2,1,0:T(8,128)} %bitcast.15), custom_call_target="tpu_custom_call" | custom-call | tf_op jit(solution)/shard_map/split_blocks/pallas_call | solution.py:358
  8.1 3.4 %collective-permute-done.2 = f32[8,128]{1,0:T(8,128)S(1)} collective-permute-done((f32[8,128]{1,0:T(8,128)S(1)}, f32[8,128]{1,0:T(8,128)S(1)}, u32[]{:S(2)}, u32[]{:S(2)}) %collective-permute-start.2) | collective-permute-done | bytes 4128 | tf_op jit(solution)/shard_map/ppermute | solution.py:427
  11.4 1.9 %collective-permute-start.3 = (f32[32,512]{1,0:T(8,128)S(1)}, f32[32,512]{1,0:T(8,128)S(1)}, u32[]{:S(2)}, u32[]{:S(2)}) collective-permute-start(f32[32,512]{1,0:T(8,128)S(1)} %collective-permute-done), channel_id=1, source_target_pairs={{0,8},{8,0},{16,24},{24,16},{1,9},{9,1},{17,25},{25,17},{2,10},{10... | collective-permute-start | bytes 196616 | tf_op jit(solution)/shard_map/ppermute | solution.py:429
  13.4 5.9 %collective-permute-start.4 = (f32[8,128]{1,0:T(8,128)S(1)}, f32[8,128]{1,0:T(8,128)S(1)}, u32[]{:S(2)}, u32[]{:S(2)}) collective-permute-start(f32[8,128]{1,0:T(8,128)S(1)} %add.53), channel_id=1, source_target_pairs={{0,6},{6,0},{2,4},{4,2},{1,7},{7,1},{3,5},{5,3},{8,14},{14,8},{10,... | collective-permute-start | bytes 12296 | tf_op jit(solution)/shard_map/ppermute | solution.py:430
  19.3 1.6 %collective-permute-done.4 = f32[8,128]{1,0:T(8,128)S(1)} collective-permute-done((f32[8,128]{1,0:T(8,128)S(1)}, f32[8,128]{1,0:T(8,128)S(1)}, u32[]{:S(2)}, u32[]{:S(2)}) %collective-permute-start.4) | collective-permute-done | bytes 4128 | tf_op jit(solution)/shard_map/ppermute | solution.py:430
  25.1 1.7 %collective-permute-done.6 = f32[8,128]{1,0:T(8,128)S(1)} collective-permute-done((f32[8,128]{1,0:T(8,128)S(1)}, f32[8,128]{1,0:T(8,128)S(1)}, u32[]{:S(2)}, u32[]{:S(2)}) %collective-permute-start.6) | collective-permute-done | bytes 4128 | tf_op jit(solution)/shard_map/ppermute | solution.py:437
  26.9 1.5 %collective-permute-start.8 = (f32[8,128]{1,0:T(8,128)S(1)}, f32[8,128]{1,0:T(8,128)S(1)}, u32[]{:S(2)}, u32[]{:S(2)}) collective-permute-start(f32[8,128]{1,0:T(8,128)S(1)} %add.55), channel_id=1, source_target_pairs={{0,16},{16,0},{8,24},{24,8},{1,17},{17,1},{9,25},{25,9},{2,18},{18... | collective-permute-start | bytes 12296 | tf_op jit(solution)/shard_map/ppermute | solution.py:438
  29.6 1.7 %collective-permute-done.8 = f32[8,128]{1,0:T(8,128)S(1)} collective-permute-done((f32[8,128]{1,0:T(8,128)S(1)}, f32[8,128]{1,0:T(8,128)S(1)}, u32[]{:S(2)}, u32[]{:S(2)}) %collective-permute-start.8) | collective-permute-done | bytes 4128 | tf_op jit(solution)/shard_map/ppermute | solution.py:438
  34.2 18.3 %all_to_all.20.parts_ref = f32[16,8,256]{2,1,0:T(8,128)S(1)} all-to-all(f32[16,8,256]{2,1,0:T(8,128)S(1)} %select_add_fusion.3), channel_id=1, replica_groups=mesh['zh'=2,'y'=4,'z'=4,'x'=4,'co'=2] {'z','x'}, dimensions={0} | all-to-all | bytes 262144 | tf_op jit(solution)/shard_map/all_to_all | solution.py:410
  52.6 11.8 %all_to_all.21 = f32[16,8,256]{2,1,0:T(8,128)S(1)} all-to-all(f32[16,8,256]{2,1,0:T(8,128)S(1)} %sum_spread.2), channel_id=1, replica_groups=mesh['zh'=2,'y'=4,'z'=4,'x'=4,'co'=2] {'z','x'}, dimensions={0} | all-to-all | bytes 262144 | tf_op jit(solution)/shard_map/all_to_all | solution.py:411
  66.8 3.4 %collective-permute-start.12 = (f32[32,512]{1,0:T(8,128)S(1)}, f32[32,512]{1,0:T(8,128)S(1)}, u32[]{:S(2)}, u32[]{:S(2)}) collective-permute-start(f32[32,512]{1,0:T(8,128)S(1)} %down.3), channel_id=1, source_target_pairs={{0,5},{1,34},{2,67},{3,96},{4,144},{5,179},{6,214},{7,241},{8,13},... | collective-permute-start | bytes 196616 | tf_op jit(solution)/shard_map/ppermute | solution.py:397
  73.5 1.7 %collective-permute-done.12 = f32[32,512]{1,0:T(8,128)S(1)} collective-permute-done((f32[32,512]{1,0:T(8,128)S(1)}, f32[32,512]{1,0:T(8,128)S(1)}, u32[]{:S(2)}, u32[]{:S(2)}) %collective-permute-start.12) | collective-permute-done | bytes 65568 | tf_op jit(solution)/shard_map/ppermute | solution.py:397
  76.7 16.1 %all_to_all.22.parts_ref = f32[16,8,256]{2,1,0:T(8,128)S(1)} all-to-all(f32[16,8,256]{2,1,0:T(8,128)S(1)} %select_add_fusion.2), channel_id=1, replica_groups=mesh['zh'=2,'y'=4,'z'=4,'x'=4,'co'=2] {'z','x'}, dimensions={0} | all-to-all | bytes 262144 | tf_op jit(solution)/shard_map/all_to_all | solution.py:410
  93.5 4.8 %all-to-all-start.3 = ((f32[16,8,256]{2,1,0:T(8,128)}), f32[16,8,256]{2,1,0:T(8,128)S(1)}, u32[]{:S(2)}, u32[]{:S(2)}) async-start(f32[16,8,256]{2,1,0:T(8,128)} %sum_spread.3), calls=%async_computation.3 | async-start | bytes 262144 | tf_op jit(solution)/shard_map/all_to_all | solution.py:411
  98.2 2.1 %collective-permute-start.14 = (f32[32,96]{1,0:T(8,128)S(1)}, f32[32,96]{1,0:T(8,128)S(1)}, u32[]{:S(2)}, u32[]{:S(2)}) collective-permute-start(f32[32,96]{1,0:T(8,128)S(1)} %pad_maximum_fusion.5), channel_id=1, source_target_pairs={{0,144},{8,152},{16,128},{24,136},{128,16},{136,24},{144,0},{152,8... | collective-permute-start | bytes 36872 | tf_op jit(solution)/shard_map/ppermute | solution.py:331
  100.3 3.8 %collective-permute-done.14 = f32[32,96]{1,0:T(8,128)S(1)} collective-permute-done((f32[32,96]{1,0:T(8,128)S(1)}, f32[32,96]{1,0:T(8,128)S(1)}, u32[]{:S(2)}, u32[]{:S(2)}) %collective-permute-start.14) | collective-permute-done | bytes 12320 | tf_op jit(solution)/shard_map/ppermute | solution.py:331
  104.1 2.0 %all-to-all-done.3 = f32[16,8,256]{2,1,0:T(8,128)S(1)} async-done(((f32[16,8,256]{2,1,0:T(8,128)}), f32[16,8,256]{2,1,0:T(8,128)S(1)}, u32[]{:S(2)}, u32[]{:S(2)}) %all-to-all-start.3) | async-done | bytes 131104 | tf_op jit(solution)/shard_map/all_to_all | solution.py:411
  108.4 3.9 %collective-permute-done.16.right_ref = f32[32,192]{1,0:T(8,128)S(1)} collective-permute-done((f32[32,192]{1,0:T(8,128)S(1)}, f32[32,192]{1,0:T(8,128)S(1)}, u32[]{:S(2)}, u32[]{:S(2)}) %collective-permute-start.16) | collective-permute-done | bytes 24608 | tf_op jit(solution)/shard_map/ppermute | solution.py:449
  112.6 3.4 %collective-permute-start.19 = (f32[32,512]{1,0:T(8,128)S(1)}, f32[32,512]{1,0:T(8,128)S(1)}, u32[]{:S(2)}, u32[]{:S(2)}) collective-permute-start(f32[32,512]{1,0:T(8,128)S(1)} %get-tuple-element.62), channel_id=1, source_target_pairs={{5,0},{34,1},{67,2},{96,3},{144,4},{179,5},{214,6},{241,7},{13,8},... | collective-permute-start | bytes 196616 | tf_op jit(solution)/shard_map/ppermute | solution.py:447
  116.0 2.9 %collective-permute-done.17.right_ref = f32[32,192]{1,0:T(8,128)S(1)} collective-permute-done((f32[32,192]{1,0:T(8,128)S(1)}, f32[32,192]{1,0:T(8,128)S(1)}, u32[]{:S(2)}, u32[]{:S(2)}) %collective-permute-start.17) | collective-permute-done | bytes 24608 | tf_op jit(solution)/shard_map/ppermute | solution.py:449
  118.9 4.5 %first_step.1 = (f32[2,32,32]{2,1,0:T(8,128)S(1)}, f32[32,96]{1,0:T(8,128)S(1)}, f32[32,64]{1,0:T(8,128)S(1)}, f32[32,32]{1,0:T(8,128)S(1)}) custom-call(f32[32,192]{1,0:T(8,128)S(1)} %plus.3.both_ref), custom_call_target="tpu_custom_call" | custom-call | flops 6000000000 | bytes 100000 | tf_op jit(solution)/shard_map/first_step/pallas_call | solution.py:291
  123.3 1.6 %collective-permute-done.18.half_ref = f32[32,192]{1,0:T(8,128)S(1)} collective-permute-done((f32[32,192]{1,0:T(8,128)S(1)}, f32[32,192]{1,0:T(8,128)S(1)}, u32[]{:S(2)}, u32[]{:S(2)}) %collective-permute-start.18) | collective-permute-done | bytes 24608 | tf_op jit(solution)/shard_map/ppermute | solution.py:331
  124.9 3.3 %last_step.1 = (f32[2,2,32,32]{3,2,1,0:T(8,128)}, f32[32,512]{1,0:T(8,128)}) custom-call(f32[8,128]{1,0:T(8,128)S(1)} %add.56.mean_ref, f32[32,192]{1,0:T(8,128)S(1)} %plus.3.both_ref, f32[32,192]{1,0:T(8,128)S(1)} %collective-permute-done.18.half_ref, f32[2,32,32]{2,1,0:T(8,128)S(1)} %get-tuple-element.58.history0_ref, ...), custom_call_target="tpu_custom_call" | custom-call | tf_op jit(solution)/shard_map/last_step/pallas_call | solution.py:309
  (63 shorter events, 19.8 us)
Async XLA Ops:
  0.6 10.8 %collective-permute-start = (f32[32,512]{1,0:T(8,128)}, f32[32,512]{1,0:T(8,128)S(1)}, u32[]{:S(2)}, u32[]{:S(2)}) collective-permute-start(f32[32,512]{1,0:T(8,128)} %x_ref.1), channel_id=1, source_target_pairs={{0,5},{1,34},{2,67},{3,96},{4,144},{5,179},{6,214},{7,241},{8,13},... | collective-permute-start | bytes 196616 | tf_op jit(solution)/shard_map/ppermute | solution.py:425
  6.4 1.4 %collective-permute-start.1 = (f32[8,128]{1,0:T(8,128)S(1)}, f32[8,128]{1,0:T(8,128)S(1)}, u32[]{:S(2)}, u32[]{:S(2)}) collective-permute-start(f32[8,128]{1,0:T(8,128)S(1)} %get-tuple-element.37), channel_id=1, source_target_pairs={{0,1},{1,0},{2,3},{3,2},{4,5},{5,4},{6,7},{7,6},{8,9},{9,8},{10,11... | collective-permute-start | bytes 12296 | tf_op jit(solution)/shard_map/ppermute | solution.py:426
  7.8 3.6 %collective-permute-start.2 = (f32[8,128]{1,0:T(8,128)S(1)}, f32[8,128]{1,0:T(8,128)S(1)}, u32[]{:S(2)}, u32[]{:S(2)}) collective-permute-start(f32[8,128]{1,0:T(8,128)S(1)} %add.52), channel_id=1, source_target_pairs={{0,2},{2,0},{4,6},{6,4},{1,3},{3,1},{5,7},{7,5},{8,10},{10,8},{12,... | collective-permute-start | bytes 12296 | tf_op jit(solution)/shard_map/ppermute | solution.py:427
  11.4 9.4 %collective-permute-start.3 = (f32[32,512]{1,0:T(8,128)S(1)}, f32[32,512]{1,0:T(8,128)S(1)}, u32[]{:S(2)}, u32[]{:S(2)}) collective-permute-start(f32[32,512]{1,0:T(8,128)S(1)} %collective-permute-done), channel_id=1, source_target_pairs={{0,8},{8,0},{16,24},{24,16},{1,9},{9,1},{17,25},{25,17},{2,10},{10... | collective-permute-start | bytes 196616 | tf_op jit(solution)/shard_map/ppermute | solution.py:429
  13.4 7.5 %collective-permute-start.4 = (f32[8,128]{1,0:T(8,128)S(1)}, f32[8,128]{1,0:T(8,128)S(1)}, u32[]{:S(2)}, u32[]{:S(2)}) collective-permute-start(f32[8,128]{1,0:T(8,128)S(1)} %add.53), channel_id=1, source_target_pairs={{0,6},{6,0},{2,4},{4,2},{1,7},{7,1},{3,5},{5,3},{8,14},{14,8},{10,... | collective-permute-start | bytes 12296 | tf_op jit(solution)/shard_map/ppermute | solution.py:430
  20.9 1.4 %collective-permute-start.5 = (f32[2,32,512]{2,1,0:T(8,128)S(1)}, f32[2,32,512]{2,1,0:T(8,128)S(1)}, u32[]{:S(2)}, u32[]{:S(2)}) collective-permute-start(f32[2,32,512]{2,1,0:T(8,128)S(1)} %pad_maximum_fusion.3), channel_id=1, source_target_pairs={{0,1},{1,0},{2,3},{3,2},{4,5},{5,4},{6,7},{7,6},{8,9},{9,8},{10,11... | collective-permute-start | bytes 393224 | tf_op jit(solution)/shard_map/ppermute | solution.py:433
  22.4 5.9 %copy-start = (f32[32,512]{1,0:T(8,128)S(1)}, f32[32,512]{1,0:T(8,128)}, u32[]{:S(2)}) copy-start(f32[32,512]{1,0:T(8,128)} %x_ref.1) | copy-start | bytes 196612
  23.2 3.6 %collective-permute-start.6 = (f32[8,128]{1,0:T(8,128)S(1)}, f32[8,128]{1,0:T(8,128)S(1)}, u32[]{:S(2)}, u32[]{:S(2)}) collective-permute-start(f32[8,128]{1,0:T(8,128)S(1)} %add.54), channel_id=1, source_target_pairs={{0,8},{8,0},{16,24},{24,16},{1,9},{9,1},{17,25},{25,17},{2,10},{10... | collective-permute-start | bytes 12296 | tf_op jit(solution)/shard_map/ppermute | solution.py:437
  24.3 8.4 %collective-permute-start.7 = (f32[32,512]{1,0:T(8,128)S(1)}, f32[32,512]{1,0:T(8,128)S(1)}, u32[]{:S(2)}, u32[]{:S(2)}) collective-permute-start(f32[32,512]{1,0:T(8,128)S(1)} %down.2), channel_id=1, source_target_pairs={{0,5},{1,34},{2,67},{3,96},{4,144},{5,179},{6,214},{7,241},{8,13},... | collective-permute-start | bytes 196616 | tf_op jit(solution)/shard_map/ppermute | solution.py:397
  26.9 4.5 %collective-permute-start.8 = (f32[8,128]{1,0:T(8,128)S(1)}, f32[8,128]{1,0:T(8,128)S(1)}, u32[]{:S(2)}, u32[]{:S(2)}) collective-permute-start(f32[8,128]{1,0:T(8,128)S(1)} %add.55), channel_id=1, source_target_pairs={{0,16},{16,0},{8,24},{24,8},{1,17},{17,1},{9,25},{25,9},{2,18},{18... | collective-permute-start | bytes 12296 | tf_op jit(solution)/shard_map/ppermute | solution.py:438
  32.7 1.4 %collective-permute-start.9 = (f32[16,8,256]{2,1,0:T(8,128)S(1)}, f32[16,8,256]{2,1,0:T(8,128)S(1)}, u32[]{:S(2)}, u32[]{:S(2)}) collective-permute-start(f32[16,8,256]{2,1,0:T(8,128)S(1)} %slice_select_fusion.1), channel_id=1, source_target_pairs={{0,1},{1,0},{2,3},{3,2},{4,5},{5,4},{6,7},{7,6},{8,9},{9,8},{10,11... | collective-permute-start | bytes 393224 | tf_op jit(solution)/shard_map/ppermute | solution.py:409
  64.4 1.3 %collective-permute-start.10 = (f32[16,8,256]{2,1,0:T(8,128)S(1)}, f32[16,8,256]{2,1,0:T(8,128)S(1)}, u32[]{:S(2)}, u32[]{:S(2)}) collective-permute-start(f32[16,8,256]{2,1,0:T(8,128)S(1)} %all_to_all.21), channel_id=1, source_target_pairs={{0,1},{1,0},{2,3},{3,2},{4,5},{5,4},{6,7},{7,6},{8,9},{9,8},{10,11... | collective-permute-start | bytes 393224 | tf_op jit(solution)/shard_map/ppermute | solution.py:415
  65.9 5.3 %collective-permute-start.11 = (f32[32,512]{1,0:T(8,128)S(1)}, f32[32,512]{1,0:T(8,128)S(1)}, u32[]{:S(2)}, u32[]{:S(2)}) collective-permute-start(f32[32,512]{1,0:T(8,128)S(1)} %get-tuple-element.64), channel_id=1, source_target_pairs={{5,0},{34,1},{67,2},{96,3},{144,4},{179,5},{214,6},{241,7},{13,8},... | collective-permute-start | bytes 196616 | tf_op jit(solution)/shard_map/ppermute | solution.py:440
  66.8 8.3 %collective-permute-start.12 = (f32[32,512]{1,0:T(8,128)S(1)}, f32[32,512]{1,0:T(8,128)S(1)}, u32[]{:S(2)}, u32[]{:S(2)}) collective-permute-start(f32[32,512]{1,0:T(8,128)S(1)} %down.3), channel_id=1, source_target_pairs={{0,5},{1,34},{2,67},{3,96},{4,144},{5,179},{6,214},{7,241},{8,13},... | collective-permute-start | bytes 196616 | tf_op jit(solution)/shard_map/ppermute | solution.py:397
  75.3 1.4 %collective-permute-start.13 = (f32[16,8,256]{2,1,0:T(8,128)S(1)}, f32[16,8,256]{2,1,0:T(8,128)S(1)}, u32[]{:S(2)}, u32[]{:S(2)}) collective-permute-start(f32[16,8,256]{2,1,0:T(8,128)S(1)} %slice_select_fusion), channel_id=1, source_target_pairs={{0,1},{1,0},{2,3},{3,2},{4,5},{5,4},{6,7},{7,6},{8,9},{9,8},{10,11... | collective-permute-start | bytes 393224 | tf_op jit(solution)/shard_map/ppermute | solution.py:409
  93.5 12.6 %all-to-all-start.3 = ((f32[16,8,256]{2,1,0:T(8,128)}), f32[16,8,256]{2,1,0:T(8,128)S(1)}, u32[]{:S(2)}, u32[]{:S(2)}) async-start(f32[16,8,256]{2,1,0:T(8,128)} %sum_spread.3), calls=%async_computation.3 | async-start | bytes 262144 | tf_op jit(solution)/shard_map/all_to_all | solution.py:411
  98.2 5.9 %collective-permute-start.14 = (f32[32,96]{1,0:T(8,128)S(1)}, f32[32,96]{1,0:T(8,128)S(1)}, u32[]{:S(2)}, u32[]{:S(2)}) collective-permute-start(f32[32,96]{1,0:T(8,128)S(1)} %pad_maximum_fusion.5), channel_id=1, source_target_pairs={{0,144},{8,152},{16,128},{24,136},{128,16},{136,24},{144,0},{152,8... | collective-permute-start | bytes 36872 | tf_op jit(solution)/shard_map/ppermute | solution.py:331
  106.1 1.3 %collective-permute-start.15 = (f32[16,8,256]{2,1,0:T(8,128)S(1)}, f32[16,8,256]{2,1,0:T(8,128)S(1)}, u32[]{:S(2)}, u32[]{:S(2)}) collective-permute-start(f32[16,8,256]{2,1,0:T(8,128)S(1)} %all-to-all-done.3), channel_id=1, source_target_pairs={{0,1},{1,0},{2,3},{3,2},{4,5},{5,4},{6,7},{7,6},{8,9},{9,8},{10,11... | collective-permute-start | bytes 393224 | tf_op jit(solution)/shard_map/ppermute | solution.py:415
  108.4 3.9 %collective-permute-start.16 = (f32[32,192]{1,0:T(8,128)S(1)}, f32[32,192]{1,0:T(8,128)S(1)}, u32[]{:S(2)}, u32[]{:S(2)}) collective-permute-start(f32[32,192]{1,0:T(8,128)S(1)} %pad_maximum_fusion.4.left_ref), channel_id=1, source_target_pairs={{0,32},{32,0},{64,96},{96,64},{1,33},{33,1},{65,97},{97,65},{2,34}... | collective-permute-start | bytes 73736 | tf_op jit(solution)/shard_map/ppermute | solution.py:449
  112.3 6.5 %collective-permute-start.17 = (f32[32,192]{1,0:T(8,128)S(1)}, f32[32,192]{1,0:T(8,128)S(1)}, u32[]{:S(2)}, u32[]{:S(2)}) collective-permute-start(f32[32,192]{1,0:T(8,128)S(1)} %plus.2.left_ref), channel_id=1, source_target_pairs={{0,96},{96,0},{32,64},{64,32},{1,97},{97,1},{33,65},{65,33},{2,98}... | collective-permute-start | bytes 73736 | tf_op jit(solution)/shard_map/ppermute | solution.py:449
  112.6 10.7 %collective-permute-start.19 = (f32[32,512]{1,0:T(8,128)S(1)}, f32[32,512]{1,0:T(8,128)S(1)}, u32[]{:S(2)}, u32[]{:S(2)}) collective-permute-start(f32[32,512]{1,0:T(8,128)S(1)} %get-tuple-element.62), channel_id=1, source_target_pairs={{5,0},{34,1},{67,2},{96,3},{144,4},{179,5},{214,6},{241,7},{13,8},... | collective-permute-start | bytes 196616 | tf_op jit(solution)/shard_map/ppermute | solution.py:447
  118.9 6.0 %collective-permute-start.18 = (f32[32,192]{1,0:T(8,128)S(1)}, f32[32,192]{1,0:T(8,128)S(1)}, u32[]{:S(2)}, u32[]{:S(2)}) collective-permute-start(f32[32,192]{1,0:T(8,128)S(1)} %plus.3.both_ref), channel_id=1, source_target_pairs={{0,144},{8,152},{16,128},{24,136},{128,16},{136,24},{144,0},{152,8... | collective-permute-start | bytes 73736 | tf_op jit(solution)/shard_map/ppermute | solution.py:331

commit v12 on v11

--- a/solution.py
+++ b/solution.py
@@ -393,11 +393,12 @@
             name="across",
         )(lead, own, high, low)
 
-    def total(acrosses, downs, before, mean, far_mean, gram=None):
+    def total(acrosses, downs, before, mean, far_mean, tau=None, gram=None):
         arrived = lax.ppermute(downs, every, to_row_group())
         if far_mean is not None:
-            arrived, far_mean = lax.optimization_barrier((arrived, far_mean))
             mean = mean + far_mean
+            tau = jnp.broadcast_to(mean[None, :1, :1] - SHIFT, (1, vecs, width))
+            acrosses, mean, tau = lax.optimization_barrier((acrosses, mean, tau))
         acrosses, gram = lax.optimization_barrier((acrosses, gram))
         part = acrosses + jnp.where(in_slot, arrived[None], 0.0)
         part = part.reshape(slots * vecs // 8, 8, width)
@@ -416,8 +417,8 @@
         low = jnp.where(first, whole, facing)
         high = jnp.where(first, facing, whole)
         four = jnp.concatenate([low, high], axis=-1).reshape(slots, vecs, width)
-        four = four - (mean[:1, :1] - SHIFT)[None] * before
-        return four, gram, mean
+        four = four - tau * before
+        return four, gram, mean, tau
 
     def slot_of(four):
         return jnp.sum(jnp.where(in_slot, four, 0.0), axis=0)
@@ -436,13 +437,13 @@
     downs, mean = lax.optimization_barrier((down(x4), mean))
     mean = mean + lax.ppermute(mean, "z", PAIRS[0])
     far_mean = lax.ppermute(mean, "z", [(0, 2), (2, 0), (1, 3), (3, 1)])
-    y4, _, mean = total(across(x), downs, x4, mean, far_mean)
+    y4, _, mean, tau = total(across(x), downs, x4, mean, far_mean)
     y = lax.ppermute(slot_of(y4), every, from_row_group())
     downs = down(y4)
     y, x4_late, y4_late = lax.optimization_barrier((y, x4, y4))
     acrosses = across(y)
     gram = jnp.concatenate([grams_of(x4_late), grams_of(x4_late, y4_late)], axis=1)
-    z4, gram, mean = total(acrosses, downs, y4, mean, None, gram)
+    z4, gram, mean, tau = total(acrosses, downs, y4, mean, None, tau, gram)
     both = jnp.concatenate([grams_of(x4, y4, z4), gram], axis=1)
     zz = lax.ppermute(slot_of(z4), every, from_row_group())
     for pairs in PAIRS:

time: 129 us -> 129 us (level)
  starting transfers between devices: 29 us -> 26.7 us
  waiting for transfers between devices: 32.7 us -> 34.1 us
where the time goes in v12:
time: 129 us; the launch traced here: 128 us
  blocking collectives  47.4 us (37%)
  waiting for transfers between devices  34.1 us (26%)
  starting transfers between devices  26.7 us (21%)
  Pallas kernels  17.4 us (13%)
  between operations  1.49 us (1%)
    all_to_all x2, blocking collectives, total(): pieces = lax.all_to_all(mine, ('z', 'x'), 0, 0, tiled=True)  35.6 us
    all_to_all x1, blocking collectives, total(): whole = lax.all_to_all(sum_spread(pieces), ('z', 'x'), 0, 0, tiled=True)  11.8 us
    ppermute x2, waiting for transfers between devices, on_device(): both = plus(both, lax.ppermute(both, 'y', pairs))  7.06 us
    ppermute x2, waiting for transfers between devices, across_half(): return lax.ppermute(value, ('zh', 'z'), pairs)  6.48 us
    ppermute x1, starting transfers between devices, on_device(): lax.ppermute(mean, 'x', PAIRS[1])  5.94 us
    all_to_all x1, starting transfers between devices, total(): whole = lax.all_to_all(sum_spread(pieces), ('z', 'x'), 0, 0, tiled=True)  4.76 us
    pallas_call x1, Pallas kernels, begin(): pl.pallas_call(functools.partial(first_step, 1.0 / length), in_specs=[IN_...  4.46 us
    ppermute x2, starting transfers between devices, total(): arrived = lax.ppermute(downs, every, to_row_group())  4.28 us
  transfers between devices with their start and end apart: 21, of which 18 were waited for; matrix products, arithmetic and copies ran while one was open for 0% of the time, Pallas kernels for 9%

profile of v12, /device:TPU:2, one launch (start us, length us, event | category | flops | bytes accessed | tf_op | source)
XLA Modules:
  0.0 128.5 jit_solution(2027646521607253148)
XLA Ops:
  0.6 2.7 %collective-permute-start = (f32[32,512]{1,0:T(8,128)}, f32[32,512]{1,0:T(8,128)S(1)}, u32[]{:S(2)}, u32[]{:S(2)}) collective-permute-start(f32[32,512]{1,0:T(8,128)} %x_ref.1), channel_id=1, source_target_pairs={{0,5},{1,34},{2,67},{3,96},{4,144},{5,179},{6,214},{7,241},{8,13},... | collective-permute-start | bytes 196616 | tf_op jit(solution)/shard_map/ppermute | solution.py:426
  3.3 3.1 %split_blocks.1 = (bf16[2048,512]{1,0:T(8,128)(2,1)S(1)}, bf16[2048,512]{1,0:T(8,128)(2,1)S(1)}, f32[4,512]{1,0:T(4,128)S(1)}, f32[8,128]{1,0:T(8,128)S(1)}) custom-call(f32[1,512]{1,0:T(1,128)} %bitcast.25, f32[4,512,512]{2,1,0:T(8,128)} %bitcast.16), custom_call_target="tpu_custom_call" | custom-call | tf_op jit(solution)/shard_map/split_blocks/pallas_call | solution.py:358
  8.1 3.4 %collective-permute-done.2 = f32[8,128]{1,0:T(8,128)S(1)} collective-permute-done((f32[8,128]{1,0:T(8,128)S(1)}, f32[8,128]{1,0:T(8,128)S(1)}, u32[]{:S(2)}, u32[]{:S(2)}) %collective-permute-start.2) | collective-permute-done | bytes 4128 | tf_op jit(solution)/shard_map/ppermute | solution.py:428
  11.4 1.9 %collective-permute-start.3 = (f32[32,512]{1,0:T(8,128)S(1)}, f32[32,512]{1,0:T(8,128)S(1)}, u32[]{:S(2)}, u32[]{:S(2)}) collective-permute-start(f32[32,512]{1,0:T(8,128)S(1)} %collective-permute-done), channel_id=1, source_target_pairs={{0,8},{8,0},{16,24},{24,16},{1,9},{9,1},{17,25},{25,17},{2,10},{10... | collective-permute-start | bytes 196616 | tf_op jit(solution)/shard_map/ppermute | solution.py:430
  13.4 5.9 %collective-permute-start.4 = (f32[8,128]{1,0:T(8,128)S(1)}, f32[8,128]{1,0:T(8,128)S(1)}, u32[]{:S(2)}, u32[]{:S(2)}) collective-permute-start(f32[8,128]{1,0:T(8,128)S(1)} %add.54), channel_id=1, source_target_pairs={{0,6},{6,0},{2,4},{4,2},{1,7},{7,1},{3,5},{5,3},{8,14},{14,8},{10,... | collective-permute-start | bytes 12296 | tf_op jit(solution)/shard_map/ppermute | solution.py:431
  19.3 1.6 %collective-permute-done.4 = f32[8,128]{1,0:T(8,128)S(1)} collective-permute-done((f32[8,128]{1,0:T(8,128)S(1)}, f32[8,128]{1,0:T(8,128)S(1)}, u32[]{:S(2)}, u32[]{:S(2)}) %collective-permute-start.4) | collective-permute-done | bytes 4128 | tf_op jit(solution)/shard_map/ppermute | solution.py:431
  25.1 1.7 %collective-permute-done.6 = f32[8,128]{1,0:T(8,128)S(1)} collective-permute-done((f32[8,128]{1,0:T(8,128)S(1)}, f32[8,128]{1,0:T(8,128)S(1)}, u32[]{:S(2)}, u32[]{:S(2)}) %collective-permute-start.6) | collective-permute-done | bytes 4128 | tf_op jit(solution)/shard_map/ppermute | solution.py:438
  26.9 1.5 %collective-permute-start.7 = (f32[8,128]{1,0:T(8,128)S(1)}, f32[8,128]{1,0:T(8,128)S(1)}, u32[]{:S(2)}, u32[]{:S(2)}) collective-permute-start(f32[8,128]{1,0:T(8,128)S(1)} %add.56), channel_id=1, source_target_pairs={{0,16},{16,0},{8,24},{24,8},{1,17},{17,1},{9,25},{25,9},{2,18},{18... | collective-permute-start | bytes 12296 | tf_op jit(solution)/shard_map/ppermute | solution.py:439
  29.6 1.7 %collective-permute-done.7 = f32[8,128]{1,0:T(8,128)S(1)} collective-permute-done((f32[8,128]{1,0:T(8,128)S(1)}, f32[8,128]{1,0:T(8,128)S(1)}, u32[]{:S(2)}, u32[]{:S(2)}) %collective-permute-start.7) | collective-permute-done | bytes 4128 | tf_op jit(solution)/shard_map/ppermute | solution.py:439
  34.2 18.3 %all_to_all.20.parts_ref = f32[16,8,256]{2,1,0:T(8,128)S(1)} all-to-all(f32[16,8,256]{2,1,0:T(8,128)S(1)} %select_add_fusion.3), channel_id=1, replica_groups=mesh['zh'=2,'y'=4,'z'=4,'x'=4,'co'=2] {'z','x'}, dimensions={0} | all-to-all | bytes 262144 | tf_op jit(solution)/shard_map/all_to_all | solution.py:411
  52.6 11.8 %all_to_all.21 = f32[16,8,256]{2,1,0:T(8,128)S(1)} all-to-all(f32[16,8,256]{2,1,0:T(8,128)S(1)} %sum_spread.2), channel_id=1, replica_groups=mesh['zh'=2,'y'=4,'z'=4,'x'=4,'co'=2] {'z','x'}, dimensions={0} | all-to-all | bytes 262144 | tf_op jit(solution)/shard_map/all_to_all | solution.py:412
  64.4 1.3 %collective-permute-done.10 = f32[16,8,256]{2,1,0:T(8,128)S(1)} collective-permute-done((f32[16,8,256]{2,1,0:T(8,128)S(1)}, f32[16,8,256]{2,1,0:T(8,128)S(1)}, u32[]{:S(2)}, u32[]{:S(2)}) %collective-permute-start.10) | collective-permute-done | bytes 131104 | tf_op jit(solution)/shard_map/ppermute | solution.py:416
  66.8 3.4 %collective-permute-start.12 = (f32[32,512]{1,0:T(8,128)S(1)}, f32[32,512]{1,0:T(8,128)S(1)}, u32[]{:S(2)}, u32[]{:S(2)}) collective-permute-start(f32[32,512]{1,0:T(8,128)S(1)} %down.3), channel_id=1, source_target_pairs={{0,5},{1,34},{2,67},{3,96},{4,144},{5,179},{6,214},{7,241},{8,13},... | collective-permute-start | bytes 196616 | tf_op jit(solution)/shard_map/ppermute | solution.py:397
  73.5 1.7 %collective-permute-done.12 = f32[32,512]{1,0:T(8,128)S(1)} collective-permute-done((f32[32,512]{1,0:T(8,128)S(1)}, f32[32,512]{1,0:T(8,128)S(1)}, u32[]{:S(2)}, u32[]{:S(2)}) %collective-permute-start.12) | collective-permute-done | bytes 65568 | tf_op jit(solution)/shard_map/ppermute | solution.py:397
  76.7 17.3 %all_to_all.22.parts_ref = f32[16,8,256]{2,1,0:T(8,128)S(1)} all-to-all(f32[16,8,256]{2,1,0:T(8,128)S(1)} %select_add_fusion.2), channel_id=1, replica_groups=mesh['zh'=2,'y'=4,'z'=4,'x'=4,'co'=2] {'z','x'}, dimensions={0} | all-to-all | bytes 262144 | tf_op jit(solution)/shard_map/all_to_all | solution.py:411
  94.7 4.8 %all-to-all-start.3 = ((f32[16,8,256]{2,1,0:T(8,128)}), f32[16,8,256]{2,1,0:T(8,128)S(1)}, u32[]{:S(2)}, u32[]{:S(2)}) async-start(f32[16,8,256]{2,1,0:T(8,128)} %sum_spread.3), calls=%async_computation.3 | async-start | bytes 262144 | tf_op jit(solution)/shard_map/all_to_all | solution.py:412
  100.4 4.9 %collective-permute-done.14 = f32[32,96]{1,0:T(8,128)S(1)} collective-permute-done((f32[32,96]{1,0:T(8,128)S(1)}, f32[32,96]{1,0:T(8,128)S(1)}, u32[]{:S(2)}, u32[]{:S(2)}) %collective-permute-start.14) | collective-permute-done | bytes 12320 | tf_op jit(solution)/shard_map/ppermute | solution.py:331
  105.3 2.0 %all-to-all-done.3 = f32[16,8,256]{2,1,0:T(8,128)S(1)} async-done(((f32[16,8,256]{2,1,0:T(8,128)}), f32[16,8,256]{2,1,0:T(8,128)S(1)}, u32[]{:S(2)}, u32[]{:S(2)}) %all-to-all-start.3) | async-done | bytes 131104 | tf_op jit(solution)/shard_map/all_to_all | solution.py:412
  109.6 3.9 %collective-permute-done.16.right_ref = f32[32,192]{1,0:T(8,128)S(1)} collective-permute-done((f32[32,192]{1,0:T(8,128)S(1)}, f32[32,192]{1,0:T(8,128)S(1)}, u32[]{:S(2)}, u32[]{:S(2)}) %collective-permute-start.16) | collective-permute-done | bytes 24608 | tf_op jit(solution)/shard_map/ppermute | solution.py:450
  113.5 2.5 %collective-permute-start.19 = (f32[32,512]{1,0:T(8,128)S(1)}, f32[32,512]{1,0:T(8,128)S(1)}, u32[]{:S(2)}, u32[]{:S(2)}) collective-permute-start(f32[32,512]{1,0:T(8,128)S(1)} %get-tuple-element.64), channel_id=1, source_target_pairs={{5,0},{34,1},{67,2},{96,3},{144,4},{179,5},{214,6},{241,7},{13,8},... | collective-permute-start | bytes 196616 | tf_op jit(solution)/shard_map/ppermute | solution.py:448
  116.0 3.2 %collective-permute-done.17.right_ref = f32[32,192]{1,0:T(8,128)S(1)} collective-permute-done((f32[32,192]{1,0:T(8,128)S(1)}, f32[32,192]{1,0:T(8,128)S(1)}, u32[]{:S(2)}, u32[]{:S(2)}) %collective-permute-start.17) | collective-permute-done | bytes 24608 | tf_op jit(solution)/shard_map/ppermute | solution.py:450
  119.2 4.5 %first_step.1 = (f32[2,32,32]{2,1,0:T(8,128)S(1)}, f32[32,96]{1,0:T(8,128)S(1)}, f32[32,64]{1,0:T(8,128)S(1)}, f32[32,32]{1,0:T(8,128)S(1)}) custom-call(f32[32,192]{1,0:T(8,128)S(1)} %plus.3.both_ref), custom_call_target="tpu_custom_call" | custom-call | flops 6000000000 | bytes 100000 | tf_op jit(solution)/shard_map/first_step/pallas_call | solution.py:291
  123.6 1.6 %collective-permute-done.18.half_ref = f32[32,192]{1,0:T(8,128)S(1)} collective-permute-done((f32[32,192]{1,0:T(8,128)S(1)}, f32[32,192]{1,0:T(8,128)S(1)}, u32[]{:S(2)}, u32[]{:S(2)}) %collective-permute-start.18) | collective-permute-done | bytes 24608 | tf_op jit(solution)/shard_map/ppermute | solution.py:331
  125.2 3.3 %last_step.1 = (f32[2,2,32,32]{3,2,1,0:T(8,128)}, f32[32,512]{1,0:T(8,128)}) custom-call(f32[8,128]{1,0:T(8,128)S(1)} %add.57.mean_ref, f32[32,192]{1,0:T(8,128)S(1)} %plus.3.both_ref, f32[32,192]{1,0:T(8,128)S(1)} %collective-permute-done.18.half_ref, f32[2,32,32]{2,1,0:T(8,128)S(1)} %get-tuple-element.60.history0_ref, ...), custom_call_target="tpu_custom_call" | custom-call | tf_op jit(solution)/shard_map/last_step/pallas_call | solution.py:309
  (64 shorter events, 19.1 us)
Async XLA Ops:
  0.6 10.8 %collective-permute-start = (f32[32,512]{1,0:T(8,128)}, f32[32,512]{1,0:T(8,128)S(1)}, u32[]{:S(2)}, u32[]{:S(2)}) collective-permute-start(f32[32,512]{1,0:T(8,128)} %x_ref.1), channel_id=1, source_target_pairs={{0,5},{1,34},{2,67},{3,96},{4,144},{5,179},{6,214},{7,241},{8,13},... | collective-permute-start | bytes 196616 | tf_op jit(solution)/shard_map/ppermute | solution.py:426
  6.4 1.4 %collective-permute-start.1 = (f32[8,128]{1,0:T(8,128)S(1)}, f32[8,128]{1,0:T(8,128)S(1)}, u32[]{:S(2)}, u32[]{:S(2)}) collective-permute-start(f32[8,128]{1,0:T(8,128)S(1)} %get-tuple-element.37), channel_id=1, source_target_pairs={{0,1},{1,0},{2,3},{3,2},{4,5},{5,4},{6,7},{7,6},{8,9},{9,8},{10,11... | collective-permute-start | bytes 12296 | tf_op jit(solution)/shard_map/ppermute | solution.py:427
  7.8 3.6 %collective-permute-start.2 = (f32[8,128]{1,0:T(8,128)S(1)}, f32[8,128]{1,0:T(8,128)S(1)}, u32[]{:S(2)}, u32[]{:S(2)}) collective-permute-start(f32[8,128]{1,0:T(8,128)S(1)} %add.53), channel_id=1, source_target_pairs={{0,2},{2,0},{4,6},{6,4},{1,3},{3,1},{5,7},{7,5},{8,10},{10,8},{12,... | collective-permute-start | bytes 12296 | tf_op jit(solution)/shard_map/ppermute | solution.py:428
  11.4 9.4 %collective-permute-start.3 = (f32[32,512]{1,0:T(8,128)S(1)}, f32[32,512]{1,0:T(8,128)S(1)}, u32[]{:S(2)}, u32[]{:S(2)}) collective-permute-start(f32[32,512]{1,0:T(8,128)S(1)} %collective-permute-done), channel_id=1, source_target_pairs={{0,8},{8,0},{16,24},{24,16},{1,9},{9,1},{17,25},{25,17},{2,10},{10... | collective-permute-start | bytes 196616 | tf_op jit(solution)/shard_map/ppermute | solution.py:430
  13.4 7.5 %collective-permute-start.4 = (f32[8,128]{1,0:T(8,128)S(1)}, f32[8,128]{1,0:T(8,128)S(1)}, u32[]{:S(2)}, u32[]{:S(2)}) collective-permute-start(f32[8,128]{1,0:T(8,128)S(1)} %add.54), channel_id=1, source_target_pairs={{0,6},{6,0},{2,4},{4,2},{1,7},{7,1},{3,5},{5,3},{8,14},{14,8},{10,... | collective-permute-start | bytes 12296 | tf_op jit(solution)/shard_map/ppermute | solution.py:431
  20.9 1.4 %collective-permute-start.5 = (f32[2,32,512]{2,1,0:T(8,128)S(1)}, f32[2,32,512]{2,1,0:T(8,128)S(1)}, u32[]{:S(2)}, u32[]{:S(2)}) collective-permute-start(f32[2,32,512]{2,1,0:T(8,128)S(1)} %pad_maximum_fusion.3), channel_id=1, source_target_pairs={{0,1},{1,0},{2,3},{3,2},{4,5},{5,4},{6,7},{7,6},{8,9},{9,8},{10,11... | collective-permute-start | bytes 393224 | tf_op jit(solution)/shard_map/ppermute | solution.py:434
  22.4 5.9 %copy-start = (f32[32,512]{1,0:T(8,128)S(1)}, f32[32,512]{1,0:T(8,128)}, u32[]{:S(2)}) copy-start(f32[32,512]{1,0:T(8,128)} %x_ref.1) | copy-start | bytes 196612
  23.2 3.6 %collective-permute-start.6 = (f32[8,128]{1,0:T(8,128)S(1)}, f32[8,128]{1,0:T(8,128)S(1)}, u32[]{:S(2)}, u32[]{:S(2)}) collective-permute-start(f32[8,128]{1,0:T(8,128)S(1)} %add.55), channel_id=1, source_target_pairs={{0,8},{8,0},{16,24},{24,16},{1,9},{9,1},{17,25},{25,17},{2,10},{10... | collective-permute-start | bytes 12296 | tf_op jit(solution)/shard_map/ppermute | solution.py:438
  24.3 8.4 %collective-permute-start.8 = (f32[32,512]{1,0:T(8,128)S(1)}, f32[32,512]{1,0:T(8,128)S(1)}, u32[]{:S(2)}, u32[]{:S(2)}) collective-permute-start(f32[32,512]{1,0:T(8,128)S(1)} %down.2), channel_id=1, source_target_pairs={{0,5},{1,34},{2,67},{3,96},{4,144},{5,179},{6,214},{7,241},{8,13},... | collective-permute-start | bytes 196616 | tf_op jit(solution)/shard_map/ppermute | solution.py:397
  26.9 4.5 %collective-permute-start.7 = (f32[8,128]{1,0:T(8,128)S(1)}, f32[8,128]{1,0:T(8,128)S(1)}, u32[]{:S(2)}, u32[]{:S(2)}) collective-permute-start(f32[8,128]{1,0:T(8,128)S(1)} %add.56), channel_id=1, source_target_pairs={{0,16},{16,0},{8,24},{24,8},{1,17},{17,1},{9,25},{25,9},{2,18},{18... | collective-permute-start | bytes 12296 | tf_op jit(solution)/shard_map/ppermute | solution.py:439
  32.7 1.4 %collective-permute-start.9 = (f32[16,8,256]{2,1,0:T(8,128)S(1)}, f32[16,8,256]{2,1,0:T(8,128)S(1)}, u32[]{:S(2)}, u32[]{:S(2)}) collective-permute-start(f32[16,8,256]{2,1,0:T(8,128)S(1)} %slice_select_fusion.1), channel_id=1, source_target_pairs={{0,1},{1,0},{2,3},{3,2},{4,5},{5,4},{6,7},{7,6},{8,9},{9,8},{10,11... | collective-permute-start | bytes 393224 | tf_op jit(solution)/shard_map/ppermute | solution.py:410
  64.4 1.3 %collective-permute-start.10 = (f32[16,8,256]{2,1,0:T(8,128)S(1)}, f32[16,8,256]{2,1,0:T(8,128)S(1)}, u32[]{:S(2)}, u32[]{:S(2)}) collective-permute-start(f32[16,8,256]{2,1,0:T(8,128)S(1)} %all_to_all.21), channel_id=1, source_target_pairs={{0,1},{1,0},{2,3},{3,2},{4,5},{5,4},{6,7},{7,6},{8,9},{9,8},{10,11... | collective-permute-start | bytes 393224 | tf_op jit(solution)/shard_map/ppermute | solution.py:416
  65.9 5.3 %collective-permute-start.11 = (f32[32,512]{1,0:T(8,128)S(1)}, f32[32,512]{1,0:T(8,128)S(1)}, u32[]{:S(2)}, u32[]{:S(2)}) collective-permute-start(f32[32,512]{1,0:T(8,128)S(1)} %get-tuple-element.66), channel_id=1, source_target_pairs={{5,0},{34,1},{67,2},{96,3},{144,4},{179,5},{214,6},{241,7},{13,8},... | collective-permute-start | bytes 196616 | tf_op jit(solution)/shard_map/ppermute | solution.py:441
  66.8 8.3 %collective-permute-start.12 = (f32[32,512]{1,0:T(8,128)S(1)}, f32[32,512]{1,0:T(8,128)S(1)}, u32[]{:S(2)}, u32[]{:S(2)}) collective-permute-start(f32[32,512]{1,0:T(8,128)S(1)} %down.3), channel_id=1, source_target_pairs={{0,5},{1,34},{2,67},{3,96},{4,144},{5,179},{6,214},{7,241},{8,13},... | collective-permute-start | bytes 196616 | tf_op jit(solution)/shard_map/ppermute | solution.py:397
  75.3 1.4 %collective-permute-start.13 = (f32[16,8,256]{2,1,0:T(8,128)S(1)}, f32[16,8,256]{2,1,0:T(8,128)S(1)}, u32[]{:S(2)}, u32[]{:S(2)}) collective-permute-start(f32[16,8,256]{2,1,0:T(8,128)S(1)} %slice_select_fusion), channel_id=1, source_target_pairs={{0,1},{1,0},{2,3},{3,2},{4,5},{5,4},{6,7},{7,6},{8,9},{9,8},{10,11... | collective-permute-start | bytes 393224 | tf_op jit(solution)/shard_map/ppermute | solution.py:410
  94.7 12.6 %all-to-all-start.3 = ((f32[16,8,256]{2,1,0:T(8,128)}), f32[16,8,256]{2,1,0:T(8,128)S(1)}, u32[]{:S(2)}, u32[]{:S(2)}) async-start(f32[16,8,256]{2,1,0:T(8,128)} %sum_spread.3), calls=%async_computation.3 | async-start | bytes 262144 | tf_op jit(solution)/shard_map/all_to_all | solution.py:412
  99.4 5.9 %collective-permute-start.14 = (f32[32,96]{1,0:T(8,128)S(1)}, f32[32,96]{1,0:T(8,128)S(1)}, u32[]{:S(2)}, u32[]{:S(2)}) collective-permute-start(f32[32,96]{1,0:T(8,128)S(1)} %pad_maximum_fusion.5), channel_id=1, source_target_pairs={{0,144},{8,152},{16,128},{24,136},{128,16},{136,24},{144,0},{152,8... | collective-permute-start | bytes 36872 | tf_op jit(solution)/shard_map/ppermute | solution.py:331
  107.3 1.3 %collective-permute-start.15 = (f32[16,8,256]{2,1,0:T(8,128)S(1)}, f32[16,8,256]{2,1,0:T(8,128)S(1)}, u32[]{:S(2)}, u32[]{:S(2)}) collective-permute-start(f32[16,8,256]{2,1,0:T(8,128)S(1)} %all-to-all-done.3), channel_id=1, source_target_pairs={{0,1},{1,0},{2,3},{3,2},{4,5},{5,4},{6,7},{7,6},{8,9},{9,8},{10,11... | collective-permute-start | bytes 393224 | tf_op jit(solution)/shard_map/ppermute | solution.py:416
  109.6 3.9 %collective-permute-start.16 = (f32[32,192]{1,0:T(8,128)S(1)}, f32[32,192]{1,0:T(8,128)S(1)}, u32[]{:S(2)}, u32[]{:S(2)}) collective-permute-start(f32[32,192]{1,0:T(8,128)S(1)} %pad_maximum_fusion.4.left_ref), channel_id=1, source_target_pairs={{0,32},{32,0},{64,96},{96,64},{1,33},{33,1},{65,97},{97,65},{2,34}... | collective-permute-start | bytes 73736 | tf_op jit(solution)/shard_map/ppermute | solution.py:450
  113.5 5.6 %collective-permute-start.17 = (f32[32,192]{1,0:T(8,128)S(1)}, f32[32,192]{1,0:T(8,128)S(1)}, u32[]{:S(2)}, u32[]{:S(2)}) collective-permute-start(f32[32,192]{1,0:T(8,128)S(1)} %plus.2.left_ref), channel_id=1, source_target_pairs={{0,96},{96,0},{32,64},{64,32},{1,97},{97,1},{33,65},{65,33},{2,98}... | collective-permute-start | bytes 73736 | tf_op jit(solution)/shard_map/ppermute | solution.py:450
  113.5 10.1 %collective-permute-start.19 = (f32[32,512]{1,0:T(8,128)S(1)}, f32[32,512]{1,0:T(8,128)S(1)}, u32[]{:S(2)}, u32[]{:S(2)}) collective-permute-start(f32[32,512]{1,0:T(8,128)S(1)} %get-tuple-element.64), channel_id=1, source_target_pairs={{5,0},{34,1},{67,2},{96,3},{144,4},{179,5},{214,6},{241,7},{13,8},... | collective-permute-start | bytes 196616 | tf_op jit(solution)/shard_map/ppermute | solution.py:448
  119.2 6.0 %collective-permute-start.18 = (f32[32,192]{1,0:T(8,128)S(1)}, f32[32,192]{1,0:T(8,128)S(1)}, u32[]{:S(2)}, u32[]{:S(2)}) collective-permute-start(f32[32,192]{1,0:T(8,128)S(1)} %plus.3.both_ref), channel_id=1, source_target_pairs={{0,144},{8,152},{16,128},{24,136},{128,16},{136,24},{144,0},{152,8... | collective-permute-start | bytes 73736 | tf_op jit(solution)/shard_map/ppermute | solution.py:331
